TPU v7x, 128 devices: a whole 4x4x4 slice. The times are simulated.
128 devices in a mesh: seq: 8 (over y_hi, x), exp: 16 (over z, y_lo, core).
Axes of the slice: x: 4, y: 4 (y_hi: 2, y_lo: 2; y = y_hi * 2 + y_lo), z: 4, core: 2. Of those that a mesh axis runs over, the one named last changes fastest.
Arguments:
- tokens: bfloat16 [16, 8192, 1280], P('exp', 'seq'), may hold values from -48 to 48, as said below
- router: bfloat16 [1280, 32], replicated, as said below
- w_in: bfloat16 [32, 1280, 5120], P('exp', None, 'seq'), may hold values from -0.15625 to 0.15625
- w_out: bfloat16 [32, 5120, 1280], P('exp', 'seq'), may hold values from -0.078125 to 0.078125
- grad_out: bfloat16 [16, 8192, 1280], P('exp', 'seq'), may hold values from -6 to 6
Outputs:
- mixed: bfloat16 [16, 8192, 1280], P('exp', 'seq')
- grad_tokens: bfloat16 [16, 8192, 1280], P('exp', 'seq')
- grad_router: float32 [1280, 32], P('seq')
- grad_w_in: bfloat16 [32, 1280, 5120], P('exp', None, 'seq')
- grad_w_out: bfloat16 [32, 5120, 1280], P('exp', 'seq')
Inputs may be any that keep to these rules, and one draw needn't show every extreme that they name: tokens are finite and of order one but for a few rows in some draws. `router`: entries are of the order of 2.5 times the inverse square root of 1280.
All inputs are finite; a program needn't handle non-finite values.
Results may differ from a plain program's by a relative error of at most 0.035.
Values may be sent and summed in bfloat16 or wider, within the bound.
No kernel may reach another device: no remote copies, remote signals or barrier semaphores. Data moves between devices by JAX's collectives and lax.ppermute only.
A program may use at most 128 MiB of HBM per device.

v0:
```python
import math

import jax
import jax.numpy as jnp
from jax import lax
from jax.sharding import PartitionSpec as P


def gelu_slope(activation):
    cumulative = 0.5 * (1.0 + lax.erf(activation * (1.0 / math.sqrt(2.0))))
    density = jnp.exp(-0.5 * activation * activation) * (1.0 / math.sqrt(2.0 * math.pi))
    return cumulative + activation * density


def per_device(tokens, router, w_in, w_out, grad_out):
    seq_count = lax.axis_size("seq")
    exp_count = lax.axis_size("exp")
    local_tokens = tokens[0]
    local_grad = grad_out[0]
    model_width = router.shape[0]
    slot_count = router.shape[1]
    held_count = w_in.shape[0]
    logits = jnp.dot(local_tokens, router, preferred_element_type=jnp.float32)
    column_top = lax.pmax(jnp.max(logits, axis=0), "seq")
    weights_raw = jnp.exp(logits - column_top[None, :])
    weights_half = weights_raw.astype(jnp.bfloat16)
    local_den = jnp.sum(weights_raw, axis=0)
    local_num = jnp.einsum(
        "tw,td->wd", weights_half, local_tokens, preferred_element_type=jnp.float32
    )
    probs = jax.nn.softmax(logits, axis=1)
    probs_half = probs.astype(jnp.bfloat16)
    denominator, numerator = lax.psum((local_den, local_num), "seq")
    slot_full = numerator / denominator[:, None]
    slot_half = slot_full.astype(jnp.bfloat16)
    routed = lax.all_to_all(slot_half, "exp", split_axis=0, concat_axis=0, tiled=True).reshape(
        exp_count, held_count, model_width
    )
    activation = jnp.einsum("cke,kef->ckf", routed, w_in, preferred_element_type=jnp.float32)
    hidden = jax.nn.gelu(activation, approximate=False).astype(jnp.bfloat16)
    partial_out = jnp.einsum("ckf,kfd->ckd", hidden, w_out, preferred_element_type=jnp.float32)
    totals = lax.psum(partial_out.astype(jnp.bfloat16), "seq")
    slot_out = lax.all_to_all(
        totals.reshape(slot_count, model_width), "exp", split_axis=0, concat_axis=0, tiled=True
    )
    mixed = jnp.dot(probs_half, slot_out, preferred_element_type=jnp.float32).astype(jnp.bfloat16)
    grad_probs = jnp.einsum("td,wd->tw", local_grad, slot_out, preferred_element_type=jnp.float32)
    comb_grad = probs * (grad_probs - jnp.sum(probs * grad_probs, axis=1, keepdims=True))
    local_slot_grad = jnp.einsum(
        "tw,td->wd", probs_half, local_grad, preferred_element_type=jnp.float32
    )
    slot_grad = lax.psum(local_slot_grad.astype(jnp.bfloat16), "seq")
    expert_grad = lax.all_to_all(slot_grad, "exp", split_axis=0, concat_axis=0, tiled=True).reshape(
        exp_count, held_count, model_width
    )
    hidden_grad = jnp.einsum("ckd,kfd->ckf", expert_grad, w_out, preferred_element_type=jnp.float32)
    grad_w_out = jnp.einsum(
        "ckf,ckd->kfd", hidden, expert_grad, preferred_element_type=jnp.float32
    ).astype(jnp.bfloat16)
    pre_grad = (hidden_grad * gelu_slope(activation)).astype(jnp.bfloat16)
    grad_w_in = jnp.einsum(
        "cke,ckf->kef", routed, pre_grad, preferred_element_type=jnp.float32
    ).astype(jnp.bfloat16)
    partial_in = jnp.einsum("ckf,kef->cke", pre_grad, w_in, preferred_element_type=jnp.float32)
    input_total = lax.psum(partial_in.astype(jnp.bfloat16), "seq").astype(jnp.float32)
    input_grad = lax.all_to_all(
        input_total.reshape(slot_count, model_width).astype(jnp.bfloat16),
        "exp",
        split_axis=0,
        concat_axis=0,
        tiled=True,
    ).astype(jnp.float32)
    in_half = input_grad.astype(jnp.bfloat16)
    in_scaled = (input_grad / denominator[:, None]).astype(jnp.bfloat16)
    inner_prod = jnp.einsum("td,wd->tw", local_tokens, in_half, preferred_element_type=jnp.float32)
    local_shift = jnp.sum(weights_half.astype(jnp.float32) * inner_prod, axis=0)
    shift_term = lax.psum(local_shift, "seq") / denominator
    disp_grad = weights_raw / denominator[None, :] * (inner_prod - shift_term[None, :])
    logit_grad = (comb_grad + disp_grad).astype(jnp.bfloat16)
    token_grad = jnp.einsum("tw,dw->td", logit_grad, router, preferred_element_type=jnp.float32)
    token_grad = token_grad + jnp.dot(weights_half, in_scaled, preferred_element_type=jnp.float32)
    grad_tokens = token_grad.astype(jnp.bfloat16)[None]
    row_share = model_width // seq_count
    router_local = jnp.einsum(
        "td,tw->dw", local_tokens, logit_grad, preferred_element_type=jnp.float32
    )
    router_full = lax.psum(router_local, ("seq", "exp"))
    grad_router = lax.dynamic_slice_in_dim(
        router_full, lax.axis_index("seq") * row_share, row_share, 0
    )
    return (mixed[None], grad_tokens, grad_router, grad_w_in, grad_w_out)


def solution(mesh):
    in_specs = (
        P("exp", "seq", None),
        P(),
        P("exp", None, "seq"),
        P("exp", "seq", None),
        P("exp", "seq", None),
    )
    out_specs = (
        P("exp", "seq", None),
        P("exp", "seq", None),
        P("seq", None),
        P("exp", None, "seq"),
        P("exp", "seq", None),
    )
    return jax.shard_map(
        per_device, mesh=mesh, in_specs=in_specs, out_specs=out_specs, check_vma=False
    )
```

profile of v0, /device:TPU:1, one launch (start us, length us, event | category | flops | bytes accessed | tf_op | source)
XLA Modules:
  0.0 503.1 jit_solution(12831804418841454261)
XLA Ops:
  7.2 0.0 all-reduce.6.cloned.1.call-start
  7.2 2.9 fusion.59
  10.1 21.4 %pmax.7 = f32[32]{0:T(128)S(1)} all-reduce(f32[32]{0:T(128)S(1)} %get-tuple-element.8), channel_id=1, replica_groups=mesh['seq'=8,'exp'=16] {'seq'}, use_global_device_ids=true, to_apply=%region_3.0 | all-reduce | flops 32 | bytes 256 | tf_op jit(solution)/shard_map/pmax | solution.py:24
  31.5 0.2 fusion.31
  31.7 0.6 copy-done.4
  32.3 3.0 fusion.10
  35.3 0.0 all-reduce.6.cloned.1.call-update
  35.3 0.0 all-reduce.8.cloned.1.call-start
  35.4 2.3 fusion.17
  37.7 0.7 all_to_all.28
  38.4 15.6 %psum.50 = f32[32]{0:T(128)S(1)} all-reduce(f32[32]{0:T(128)S(1)} %get-tuple-element.6), channel_id=1, replica_groups=mesh['seq'=8,'exp'=16] {'seq'}, use_global_device_ids=true, to_apply=%region_6.0 | all-reduce | flops 32 | bytes 256 | tf_op jit(solution)/shard_map/psum | solution.py:33
  54.0 59.3 %all-reduce.6.cloned.1.call-done = f32[32,1280]{1,0:T(8,128)} async-done(((f32[32,1280]{1,0:T(8,128)}), f32[32,1280]{1,0:T(8,128)}) %all-reduce.6.cloned.1.call-update) | async-done | bytes 163856 | tf_op jit(solution)/shard_map/psum | solution.py:33
  113.3 1.0 divide_convert_fusion.1
  114.3 0.7 all_to_all.24
  115.0 10.4 %all-to-all-start = ((bf16[16,2,1280]{2,1,0:T(2,128)(2,1)}), bf16[16,2,1280]{2,1,0:T(2,128)(2,1)S(1)}, u32[]{:S(2)}, u32[]{:S(2)}) async-start(bf16[16,2,1280]{2,1,0:T(2,128)(2,1)} %all_to_all.24), calls=%async_computation | async-start | bytes 163840 | tf_op jit(solution)/shard_map/all_to_all | solution.py:36
  125.3 69.1 %all-reduce.8.cloned.1.call-done = bf16[16,2,1280]{2,1,0:T(2,128)(2,1)} async-done(((bf16[16,2,1280]{2,1,0:T(2,128)(2,1)}), bf16[16,2,1280]{2,1,0:T(2,128)(2,1)}) %all-reduce.8.cloned.1.call-update) | async-done | bytes 81936 | tf_op jit(solution)/shard_map/psum | solution.py:52
  194.5 9.0 %all-to-all-start.2 = ((bf16[16,2,1280]{2,1,0:T(2,128)(2,1)}), bf16[16,2,1280]{2,1,0:T(2,128)(2,1)}, u32[]{:S(2)}, u32[]{:S(2)}) async-start(bf16[16,2,1280]{2,1,0:T(2,128)(2,1)} %all-reduce.8.cloned.1.call-done), calls=%async_computation.2 | async-start | bytes 163840 | tf_op jit(solution)/shard_map/all_to_all | solution.py:53
  203.5 0.0 all-reduce.12.cloned.1.call-start
  203.5 2.5 convolution_bitcast_fusion.1
  206.0 0.6 copy-done.6
  206.6 1.3 fusion.20
  207.9 1.5 all-to-all-done.2
  209.4 2.0 fusion.29
  211.4 1.6 fusion.21
  213.1 0.0 all-reduce.12.cloned.1.call-update
  213.1 3.7 convolution_convert_fusion
  216.8 71.5 %all-reduce.12.cloned.1.call-done = (bf16[16,2,1280]{2,0,1:T(8,128)(2,1)}, bf16[16,2,1280]{2,0,1:T(8,128)(2,1)}) async-done(((bf16[16,2,1280]{2,0,1:T(8,128)(2,1)}, bf16[16,2,1280]{2,0,1:T(8,128)(2,1)}), (bf16[16,2,1280]{2,0,1:T(8,128)(2,1)}, bf16[16,2,1280]{2,0,1:T(8,128)(2,1)})) %all-reduce.12.cloned.1.call-update) | async-done | bytes 163856 | tf_op jit(solution)/shard_map/psum | solution.py:42
  288.3 1.6 copy.20
  289.9 10.3 %all-to-all-start.3 = ((bf16[16,2,1280]{2,1,0:T(2,128)(2,1)}), bf16[16,2,1280]{2,1,0:T(2,128)(2,1)}, u32[]{:S(2)}, u32[]{:S(2)}) async-start(bf16[16,2,1280]{2,1,0:T(2,128)(2,1)} %copy.20), calls=%async_computation.3 | async-start | bytes 163840 | tf_op jit(solution)/shard_map/all_to_all | solution.py:66
  300.2 2.8 convolution_convert_fusion.1
  303.0 0.7 copy.18
  303.7 2.5 all-to-all-done.3
  306.2 4.4 all-to-all-start.1
  310.5 0.0 all-reduce.10.cloned.1.call-start
  310.6 1.6 all_to_all.31
  312.1 3.2 multiply_reduce_fusion
  315.4 1.2 all-to-all-done.1
  316.5 1.6 all_to_all.27
  318.1 3.3 multiply_reduce_fusion.1
  321.4 20.0 %psum.54 = f32[32]{0:T(128)} all-reduce(f32[32]{0:T(128)} %get-tuple-element.13), channel_id=1, replica_groups=mesh['seq'=8,'exp'=16] {'seq'}, use_global_device_ids=true, to_apply=%region_12.0 | all-reduce | flops 32 | bytes 256 | tf_op jit(solution)/shard_map/psum | solution.py:77
  341.4 0.8 div.39
  342.2 4.3 fusion.60
  346.5 1.9 fusion.14
  348.4 5.0 fusion.1
  353.4 0.0 all-reduce.10.cloned.1.call-update
  353.4 2.4 fusion
  355.8 139.3 %all-reduce.10.cloned.1.call-done = f32[1280,32]{0,1:T(8,128)} async-done(((f32[1280,32]{0,1:T(8,128)}), f32[1280,32]{0,1:T(8,128)}) %all-reduce.10.cloned.1.call-update) | async-done | bytes 163856 | tf_op jit(solution)/shard_map/psum | solution.py:87
  495.1 1.5 constant_dynamic-slice_fusion
  (18 shorter events, 0.1 us)
Async XLA Ops:
  7.2 199.5 %copy-start = (bf16[2,640,1280]{2,1,0:T(8,128)(2,1)S(1)}, bf16[2,640,1280]{2,1,0:T(8,128)(2,1)}, u32[]{:S(2)}) copy-start(bf16[2,640,1280]{2,1,0:T(8,128)(2,1)} %param.8) | copy-start | bytes 9830404
  7.2 106.1 %all-reduce.6.cloned.1.call-start = ((), (), s32[]{:S(2)}) async-start(), calls=%async_computation.4 | async-start | bytes 327680 | tf_op jit(solution)/shard_map/psum | solution.py:33
  31.5 3.9 copy-start.8
  31.7 0.6 copy-start.4
  35.3 159.1 %all-reduce.8.cloned.1.call-start = ((), (), s32[]{:S(2)}) async-start(), calls=%async_computation.5 | async-start | bytes 163840 | tf_op jit(solution)/shard_map/psum | solution.py:52
  115.0 79.5 %all-to-all-start = ((bf16[16,2,1280]{2,1,0:T(2,128)(2,1)}), bf16[16,2,1280]{2,1,0:T(2,128)(2,1)S(1)}, u32[]{:S(2)}, u32[]{:S(2)}) async-start(bf16[16,2,1280]{2,1,0:T(2,128)(2,1)} %all_to_all.24), calls=%async_computation | async-start | bytes 163840 | tf_op jit(solution)/shard_map/all_to_all | solution.py:36
  194.5 14.9 %all-to-all-start.2 = ((bf16[16,2,1280]{2,1,0:T(2,128)(2,1)}), bf16[16,2,1280]{2,1,0:T(2,128)(2,1)}, u32[]{:S(2)}, u32[]{:S(2)}) async-start(bf16[16,2,1280]{2,1,0:T(2,128)(2,1)} %all-reduce.8.cloned.1.call-done), calls=%async_computation.2 | async-start | bytes 163840 | tf_op jit(solution)/shard_map/all_to_all | solution.py:53
  203.5 84.9 %all-reduce.12.cloned.1.call-start = ((), (), s32[]{:S(2)}) async-start(), calls=%async_computation.7 | async-start | bytes 327680 | tf_op jit(solution)/shard_map/psum | solution.py:42
  206.0 0.6 copy-start.6
  209.4 2.0 copy-start.2
  289.9 16.3 %all-to-all-start.3 = ((bf16[16,2,1280]{2,1,0:T(2,128)(2,1)}), bf16[16,2,1280]{2,1,0:T(2,128)(2,1)}, u32[]{:S(2)}, u32[]{:S(2)}) async-start(bf16[16,2,1280]{2,1,0:T(2,128)(2,1)} %copy.20), calls=%async_computation.3 | async-start | bytes 163840 | tf_op jit(solution)/shard_map/all_to_all | solution.py:66
  300.2 2.8 copy-start.7
  306.2 10.4 %all-to-all-start.1 = ((bf16[16,2,1280]{2,1,0:T(2,128)(2,1)}), bf16[16,2,1280]{2,1,0:T(2,128)(2,1)}, u32[]{:S(2)}, u32[]{:S(2)}) async-start(bf16[16,2,1280]{2,1,0:T(2,128)(2,1)} %copy.18), calls=%async_computation.1 | async-start | bytes 163840 | tf_op jit(solution)/shard_map/all_to_all | solution.py:43
  310.5 184.6 %all-reduce.10.cloned.1.call-start = ((), (), s32[]{:S(2)}) async-start(), calls=%async_computation.6 | async-start | bytes 327680 | tf_op jit(solution)/shard_map/psum | solution.py:87
  341.4 5.1 %copy-start.1 = (bf16[1,1024,1280]{2,1,0:T(8,128)(2,1)S(1)}, bf16[1,1024,1280]{2,1,0:T(8,128)(2,1)}, u32[]{:S(2)}) copy-start(bf16[1,1024,1280]{2,1,0:T(8,128)(2,1)} %param.5) | copy-start | bytes 7864324
  341.4 5.1 %copy-start.3 = (f32[1024,32]{0,1:T(8,128)S(1)}, f32[1024,32]{0,1:T(8,128)}, u32[]{:S(2)}) copy-start(f32[1024,32]{0,1:T(8,128)} %get-tuple-element.16) | copy-start | bytes 393220
  348.4 5.0 copy-start.5
Sparse Core Ops, SparseCore 0:
  35.5 77.8 all-reduce.5
  116.5 77.9 all-reduce.7
  213.2 75.0 all-reduce.11
  353.5 141.5 all-reduce.9
where the time goes:
time: 504 us; the launch traced here: 503 us
  waiting for transfers between devices  344 us (68%)
  blocking collectives  57 us (11%)
  matrix products  42.1 us (8%)
  starting transfers between devices  34.2 us (7%)
  between operations  13.8 us (3%)
  local copies, waits for them, and re-layouts  9.52 us (2%)
    psum x1, waiting for transfers between devices, per_device(): router_full = lax.psum(router_local, ('seq', 'exp'))  139 us
    psum x1, waiting for transfers between devices, per_device(): totals = lax.psum(partial_out.astype(jnp.bfloat16), 'seq')  71.5 us
    psum x1, waiting for transfers between devices, per_device(): slot_grad = lax.psum(local_slot_grad.astype(jnp.bfloat16), 'seq')  69.1 us
    psum x1, waiting for transfers between devices, per_device(): denominator, numerator = lax.psum((local_den, local_num), 'seq')  59.3 us
    pmax x1, blocking collectives, per_device(): column_top = lax.pmax(jnp.max(logits, axis=0), 'seq')  21.4 us
    psum x1, blocking collectives, per_device(): shift_term = lax.psum(local_shift, 'seq') / denominator  20 us
    psum x1, blocking collectives, per_device(): denominator, numerator = lax.psum((local_den, local_num), 'seq')  15.6 us
    all_to_all x1, starting transfers between devices, per_device(): lax.all_to_all(slot_half, 'exp', split_axis=0, concat_axis=0, tiled=True)  10.4 us
  transfers between devices with their start and end apart: 8, of which 7 were waited for; matrix products, arithmetic and copies ran while one was open for 4% of the time, Pallas kernels for 0%

commit v1 on v0

v1 whole, which is shorter than its diff:
```python
import math

import jax
import jax.numpy as jnp
from jax import lax
from jax.sharding import Mesh, PartitionSpec as P

bf16 = jnp.bfloat16
f32 = jnp.float32
ALL = ("yh", "x", "z", "yl", "core")
SEQ = ("yh", "x")
EXP = ("z", "yl", "core")
EXTRA = 128


def gelu_slope(activation):
    cumulative = 0.5 * (1.0 + lax.erf(activation * (1.0 / math.sqrt(2.0))))
    density = jnp.exp(-0.5 * activation * activation) * (1.0 / math.sqrt(2.0 * math.pi))
    return cumulative + activation * density


def pieces(value):
    high = lax.reduce_precision(value, 8, 7)
    rest = value - high
    middle = lax.reduce_precision(rest, 8, 7)
    low = rest - middle
    return jnp.stack([high, middle, low], axis=-1).astype(bf16)


def joined(parts):
    wide = parts.astype(f32)
    return wide[..., 0] + wide[..., 1] + wide[..., 2]


def padded(parts):
    return jnp.pad(parts, [(0, 0)] * (parts.ndim - 1) + [(0, EXTRA - parts.shape[-1])])


def per_device(tokens, router, w_in, w_out, grad_out):
    x_index = lax.axis_index("x")
    own_slot = x_index // 2
    own_array = x_index % 2
    tok = tokens[0]
    grad = grad_out[0]
    width = router.shape[0]
    slots = router.shape[1]
    held = w_in.shape[0]
    owners = slots // held
    router_t = router.T.reshape(owners, held, width).swapaxes(0, 1).reshape(slots, width)
    logits = jnp.einsum("wd,td->wt", router_t, tok, preferred_element_type=f32)
    top = jnp.max(logits, axis=1, keepdims=True)
    weights = jnp.exp(logits - top)
    total = jnp.sum(weights, axis=1, keepdims=True)
    local_slot = jnp.dot(weights.astype(bf16), tok, preferred_element_type=f32) / total
    local_lse = (top + jnp.log(total))[:, 0]
    probs = jax.nn.softmax(logits, axis=0)
    probs_half = probs.astype(bf16)
    local_grad = jnp.dot(probs_half, grad, preferred_element_type=f32)
    rows = jnp.stack(
        [local_slot.reshape(held, owners, width), local_grad.reshape(held, owners, width)], axis=1
    ).astype(bf16)
    rows = rows.reshape(2 * held, owners, width)
    extra = padded(pieces(local_lse.reshape(held, owners).T).reshape(owners, 3 * held))
    send = jnp.concatenate(
        [rows, jnp.broadcast_to(extra[None], (2 * held, owners, EXTRA))], axis=2
    )
    got = lax.all_to_all(send, "x", 0, 0, tiled=True)
    lse_x = joined(got[:, :, width : width + 3 * held].reshape(4, owners, held, 3))
    lse_own = lax.dynamic_index_in_dim(lse_x, own_slot, 2, keepdims=False)
    lse_sum = jax.nn.logsumexp(lse_own, axis=0)
    scale = jnp.where(own_array == 0, jnp.exp(lse_own - lse_sum[None]), 1.0)
    row = jnp.sum(got[:, :, :width].astype(f32) * scale[:, :, None], axis=0).astype(bf16)
    row = jnp.concatenate([row, padded(pieces(lse_sum))], axis=1)
    wide = width + EXTRA
    send = jnp.broadcast_to(row[None], (8, owners, wide)).reshape(8 * owners, wide)
    got = lax.all_to_all(send, ALL, 0, 0, tiled=True).reshape(2, held, 2, owners, wide)
    lse_y = joined(got[:, :, 0, :, width : width + 3])
    lse = jax.nn.logsumexp(lse_y, axis=0)
    scale = jnp.exp(lse_y - lse[None])
    slot_half = jnp.sum(got[:, :, 0, :, :width].astype(f32) * scale[..., None], axis=0).astype(bf16)
    slot_grad = jnp.sum(got[:, :, 1, :, :width].astype(f32), axis=0).astype(bf16)
    activation = jnp.einsum("kce,kef->kcf", slot_half, w_in, preferred_element_type=f32)
    hidden = jax.nn.gelu(activation, approximate=False).astype(bf16)
    partial_out = jnp.einsum("kcf,kfd->kcd", hidden, w_out, preferred_element_type=f32)
    hidden_grad = jnp.einsum("kcd,kfd->kcf", slot_grad, w_out, preferred_element_type=f32)
    pre_grad = (hidden_grad * gelu_slope(activation)).astype(bf16)
    partial_in = jnp.einsum("kcf,kef->kce", pre_grad, w_in, preferred_element_type=f32)
    send = jnp.stack([partial_out, partial_in], axis=1).astype(bf16).reshape(2 * held, owners, width)
    got = lax.all_to_all(send, "x", 0, 0, tiled=True)
    grad_w_out = jnp.einsum(
        "kcf,kcd->kfd", hidden, slot_grad, preferred_element_type=f32
    ).astype(bf16)
    grad_w_in = jnp.einsum(
        "kce,kcf->kef", slot_half, pre_grad, preferred_element_type=f32
    ).astype(bf16)
    row = jnp.sum(got.astype(f32), axis=0).astype(bf16)
    own_half = lax.dynamic_index_in_dim(slot_half, own_slot, 0, keepdims=False).astype(f32)
    own_lse = lax.dynamic_index_in_dim(lse, own_slot, 0, keepdims=False)
    shift = jnp.sum(own_half * row.astype(f32), axis=1)
    extra = padded(jnp.concatenate([pieces(own_lse), pieces(shift)], axis=1))
    row = jnp.concatenate([row, extra], axis=1)
    send = jnp.broadcast_to(row[None], (8, owners, wide)).reshape(8 * owners, wide)
    got = lax.all_to_all(send, ALL, 0, 0, tiled=True).reshape(2, held, 2, owners, wide)
    summed = jnp.sum(got[..., :width].astype(f32), axis=0).astype(bf16)
    slot_out = summed[:, 0].reshape(slots, width)
    in_half = summed[:, 1].reshape(slots, width)
    lse = joined(got[0, :, 0, :, width : width + 3]).reshape(slots, 1)
    shift = jnp.sum(joined(got[:, :, 1, :, width + 3 : width + 6]), axis=0).reshape(slots, 1)
    grad_probs = jnp.einsum("wd,td->wt", slot_out, grad, preferred_element_type=f32)
    comb_grad = probs * (grad_probs - jnp.sum(probs * grad_probs, axis=0, keepdims=True))
    share = jnp.exp(logits - lse)
    inner = jnp.einsum("wd,td->wt", in_half, tok, preferred_element_type=f32)
    logit_grad = (comb_grad + share * (inner - shift)).astype(bf16)
    router_local = jnp.dot(logit_grad, tok, preferred_element_type=f32)
    router_local = router_local.reshape(held, owners, 8, 16, width // 128).transpose(2, 3, 4, 1, 0)
    got = lax.all_to_all(
        router_local.reshape(128, width // 128 * slots), ALL, 0, 0, tiled=True
    )
    part = jnp.sum(got, axis=0)
    mixed = jnp.einsum("wt,wd->td", probs_half, slot_out, preferred_element_type=f32).astype(bf16)
    both = jnp.concatenate([logit_grad, share.astype(bf16)], axis=0)
    table = jnp.concatenate([router_t, in_half], axis=0)
    grad_tokens = jnp.einsum("wt,wd->td", both, table, preferred_element_type=f32).astype(bf16)
    got = lax.all_to_all(
        jnp.broadcast_to(part[None], (16, part.shape[0])), EXP, 0, 0, tiled=True
    )
    grad_router = got.reshape(width // 8, slots)
    return (mixed[None], grad_tokens[None], grad_router, grad_w_in, grad_w_out)


def solution(mesh):
    fine = Mesh(mesh.devices.reshape(2, 4, 4, 2, 2), ALL)
    in_specs = (
        P(EXP, SEQ, None),
        P(),
        P(EXP, None, SEQ),
        P(EXP, SEQ, None),
        P(EXP, SEQ, None),
    )
    out_specs = (
        P(EXP, SEQ, None),
        P(EXP, SEQ, None),
        P(SEQ, None),
        P(EXP, None, SEQ),
        P(EXP, SEQ, None),
    )
    return jax.shard_map(
        per_device, mesh=fine, in_specs=in_specs, out_specs=out_specs, check_vma=False
    )
```

time: 504 us -> 170 us (0.34)
  waiting for transfers between devices: 344 us -> 11.9 us
  local copies, waits for them, and re-layouts: 9.52 us -> 48.8 us
  blocking collectives: 57 us -> 30.7 us
  other arithmetic: 2.01 us -> 18.9 us
  between operations: 13.8 us -> 1.09 us
  matrix products: 42.1 us -> 32 us
  starting transfers between devices: 34.2 us -> 25.3 us
    psum x4 -> x0, waiting for transfers between devices: 339 us -> none  [the longest x1 139 us: per_device(): router_full = lax.psum(router_local, ('seq', 'exp'))]
    psum x2 -> x0, blocking collectives: 35.6 us -> none  [the longest x1 20 us: per_device(): shift_term = lax.psum(local_shift, 'seq') / denominator]
    all_to_all x0 -> x2, blocking collectives: none -> 30.7 us  [the longest x1 22.6 us: per_device(): lax.all_to_all(send, ALL, 0, 0, tiled=True)]
    pmax x1 -> x0, blocking collectives: 21.4 us -> none  [per_device(): column_top = lax.pmax(jnp.max(logits, axis=0), 'seq')]
    unnamed x18 -> x57, local copies, waits for them, and re-layouts: 1.3 us -> 21 us
    dot_general x0 -> x2, local copies, waits for them, and re-layouts: none -> 10.3 us  [per_device(): router_local = jnp.dot(logit_grad, tok, preferred_element_type=f32)]
    dot_general x15 -> x14, matrix products: 42.1 us -> 32 us  [the longest x1 5.93 us: per_device(): router_local = jnp.dot(logit_grad, tok, preferred_element_type=f32)]
    all_to_all x4, starting transfers between devices: 34.1 us -> 25.3 us  [the longest x1 10.3 us: per_device(): lax.all_to_all(router_local.reshape(128, width // 128 * slots), ALL, 0, 0...]
  transfers between devices with their start and end apart: 8 -> 4, of which waited for: 7 -> 3; matrix products, arithmetic and copies ran while one was open for 4% -> 14% of each run, Pallas kernels for 0% -> 0%
where the time goes in v1:
time: 170 us; the launch traced here: 169 us
  local copies, waits for them, and re-layouts  48.8 us (29%)
  matrix products  32 us (19%)
  blocking collectives  30.7 us (18%)
  starting transfers between devices  25.3 us (15%)
  other arithmetic  18.9 us (11%)
  waiting for transfers between devices  11.9 us (7%)
    all_to_all x1, blocking collectives, per_device(): lax.all_to_all(send, ALL, 0, 0, tiled=True)  22.6 us
    unnamed x57, local copies, waits for them, and re-layouts  21 us
    dot_general x2, local copies, waits for them, and re-layouts, per_device(): router_local = jnp.dot(logit_grad, tok, preferred_element_type=f32)  10.3 us
    all_to_all x1, starting transfers between devices, per_device(): lax.all_to_all(router_local.reshape(128, width // 128 * slots), ALL, 0, 0...  10.3 us
    all_to_all x1, blocking collectives, per_device(): got = lax.all_to_all(send, 'x', 0, 0, tiled=True)  8.05 us
    all_to_all x1, starting transfers between devices, per_device(): lax.all_to_all(send, ALL, 0, 0, tiled=True)  6.23 us
    dot_general x1, matrix products, per_device(): router_local = jnp.dot(logit_grad, tok, preferred_element_type=f32)  5.93 us
    all_to_all x1, waiting for transfers between devices, per_device(): got = lax.all_to_all(send, 'x', 0, 0, tiled=True)  5.2 us
  transfers between devices with their start and end apart: 4, of which 3 were waited for; matrix products, arithmetic and copies ran while one was open for 14% of the time, Pallas kernels for 0%

profile of v1, /device:TPU:1, one launch (start us, length us, event | category | flops | bytes accessed | tf_op | source)
XLA Modules:
  0.0 168.7 jit_solution(1756086838349429394)
XLA Ops:
  0.6 1.1 reshape.263
  2.4 2.9 %fusion.101 = (f32[32]{0:T(128)S(1)}, f32[1024]{0:T(1024)S(1)}, f32[32,1024]{1,0:T(8,128)S(1)}) fusion(bf16[32,1280]{1,0:T(8,128)(2,1)S(1)} %bitcast.187, bf16[1,1024,1280]{2,1,0:T(8,128)(2,1)} %param.5), kind=kOutput, calls=%fused_computation.155 | convolution fusion | flops 83950560 | bytes 2838656 | tf_op jit(solution)/shard_map/wd,td->wt/dot_general | solution.py:50
  8.2 2.3 %fusion.26 = bf16[2,1,16,1280]{3,2,0,1:T(8,128)(2,1)S(1)} fusion(bf16[2,16,1024]{2,1,0:T(8,128)(2,1)S(1)} %bitcast.191, bf16[1,1024,1280]{2,1,0:T(8,128)(2,1)} %param.9), kind=kOutput, calls=%fused_computation.26 | convolution fusion | flops 83927040 | bytes 2768896 | tf_op jit(solution)/shard_map/dot_general | solution.py:58
  11.2 4.8 %all-to-all-start = ((bf16[4,16,1408]{2,1,0:T(8,128)(2,1)}), bf16[4,16,1408]{2,1,0:T(8,128)(2,1)}, u32[]{:S(2)}, u32[]{:S(2)}) async-start(bf16[4,16,1408]{2,1,0:T(8,128)(2,1)} %pad_maximum_fusion), calls=%async_computation | async-start | bytes 360448 | tf_op jit(solution)/shard_map/all_to_all | solution.py:67
  16.1 5.2 %all-to-all-done = bf16[4,16,1408]{2,1,0:T(8,128)(2,1)} async-done(((bf16[4,16,1408]{2,1,0:T(8,128)(2,1)}), bf16[4,16,1408]{2,1,0:T(8,128)(2,1)}, u32[]{:S(2)}, u32[]{:S(2)}) %all-to-all-start) | async-done | bytes 180256 | tf_op jit(solution)/shard_map/all_to_all | solution.py:67
  22.2 1.0 multiply_reduce_fusion
  23.2 0.9 copy.124
  24.1 1.7 %copy.109 = bf16[16,1280]{1,0:T(8,128)(2,1)} copy(bf16[16,1280]{0,1:T(8,128)(2,1)} %copy.124) | data formatting | bytes 81920 | tf_op jit(solution)/shard_map/convert_element_type | solution.py:72
  28.1 2.5 %reduce.18 = bf16[128,1408]{1,0:T(8,128)(2,1)} reduce(bf16[128,1,1408]{2,0,1:T(8,128)(2,1)} %bitcast.175, bf16[]{:T(256)} %broadcast.124), dimensions={1}, to_apply=%copy.111.reduce_sub_computation | reduce | bytes 720898 | tf_op jit(solution)/shard_map/all_to_all | solution.py:76
  30.6 2.1 %reshape.281 = bf16[128,2,704]{2,1,0:T(2,128)(2,1)} reshape(bf16[128,1408]{1,0:T(8,128)(2,1)} %reduce.18) | data formatting | bytes 720896
  32.7 22.6 %all_to_all.43 = bf16[128,2,704]{2,1,0:T(2,128)(2,1)} all-to-all(bf16[128,2,704]{2,1,0:T(2,128)(2,1)} %reshape.281), channel_id=1, replica_groups=mesh['yh'=2,'x'=4,'z'=4,'yl'=2,'core'=2] {'yh','x','z','yl','core'}, dimensions={0} | all-to-all | bytes 720896 | tf_op jit(solution)/shard_map/all_to_all | solution.py:76
  55.3 3.6 %reshape.282 = bf16[128,1,1408]{2,1,0:T(2,128)(2,1)} reshape(bf16[128,2,704]{2,1,0:T(2,128)(2,1)} %all_to_all.43) | data formatting | bytes 720896
  58.9 1.3 copy.122
  62.0 1.0 fusion.44
  62.9 1.0 fusion.25
  64.6 8.1 %all_to_all.44 = bf16[4,16,1280]{2,1,0:T(8,128)(2,1)} all-to-all(bf16[4,16,1280]{2,1,0:T(8,128)(2,1)S(1)} %bitcast.190), channel_id=1, replica_groups=mesh['yh'=2,'x'=4,'z'=4,'yl'=2,'core'=2] {'x'}, dimensions={0} | all-to-all | bytes 327680 | tf_op jit(solution)/shard_map/all_to_all | solution.py:89
  72.7 1.6 reduce_sum.135
  74.3 0.9 fusion.66
  75.2 1.3 fusion.90
  76.5 1.3 concatenate.21
  77.8 1.4 copy.129
  79.1 0.8 fusion.76
  80.7 2.5 %reduce.19 = bf16[128,1408]{1,0:T(8,128)(2,1)} reduce(bf16[128,1,1408]{2,0,1:T(8,128)(2,1)} %bitcast.176, bf16[]{:T(256)} %broadcast.124), dimensions={1}, to_apply=%copy.114.reduce_sub_computation | reduce | bytes 720898 | tf_op jit(solution)/shard_map/all_to_all | solution.py:103
  83.2 2.1 %reshape.283 = bf16[128,2,704]{2,1,0:T(2,128)(2,1)} reshape(bf16[128,1408]{1,0:T(8,128)(2,1)} %reduce.19) | data formatting | bytes 720896
  85.3 6.2 %all-to-all-start.3 = ((bf16[128,2,704]{2,1,0:T(2,128)(2,1)}), bf16[128,2,704]{2,1,0:T(2,128)(2,1)}, u32[]{:S(2)}, u32[]{:S(2)}) async-start(bf16[128,2,704]{2,1,0:T(2,128)(2,1)} %reshape.283), calls=%async_computation.3 | async-start | bytes 786432 | tf_op jit(solution)/shard_map/all_to_all | solution.py:103
  91.6 4.4 %copy.116 = bf16[1280,1024]{1,0:T(8,128)(2,1)} copy(bf16[1280,1024]{0,1:T(8,128)(2,1)} %bitcast.174) | data formatting | bytes 5242880 | tf_op jit(solution)/shard_map/dot_general | solution.py:114
  95.9 5.9 %dot_general.64 = bf16[8,16,10,1024]{3,2,1,0:T(8,128)(2,1)} reshape(bf16[1280,1024]{1,0:T(8,128)(2,1)} %copy.116) | data formatting | bytes 5242880 | tf_op jit(solution)/shard_map/dot_general | solution.py:114
  101.9 3.8 %convolution_convert_fusion = bf16[2,640,1280]{2,1,0:T(8,128)(2,1)} fusion(bf16[2,16,1280]{2,1,0:T(8,128)(2,1)} %copy-done.8, f32[2,16,640]{2,1,0:T(8,128)} %copy-done.9, u8[16,640]{1,0:T(8,128)(4,1)} %copy-done.17, u8[16,640]{1,0:T(8,128)(4,1)} %copy-done.16), kind=kOutput, calls=%fused_computation | convolution fusion | flops 55500800 | bytes 3461120 | tf_op jit(solution)/shard_map/kcf,kcd->kfd/dot_general | solution.py:90
  105.7 3.6 %reshape.284 = bf16[128,1,1408]{2,1,0:T(2,128)(2,1)} reshape(bf16[128,2,704]{2,1,0:T(2,128)(2,1)} %all-to-all-done.3) | data formatting | bytes 720896
  109.3 1.2 copy.123
  112.4 1.3 copy.126
  115.0 1.3 add.130
  116.3 1.6 fusion.77
  117.9 1.3 sub.183
  119.2 3.3 %multiply_reduce_fusion.1 = (f32[1024]{0:T(1024)S(1)}, bf16[32,1024]{1,0:T(8,128)(2,1)}, f32[32,1024]{1,0:T(8,128)S(1)}) fusion(f32[1024]{0:T(1024)} %get-tuple-element.41, f32[32,1024]{1,0:T(8,128)S(1)} %get-tuple-element.71, f32[1024]{0:T(1024)} %copy-done.13, f32[32]{0:T(128)} %add.130, bf16[32,1280]{1,0:T(8,128)(2,1)} %bitcast.185, ...), kind=kOutput, calls=%fused_computation.50 | convolution fusion | flops 84081664 | bytes 3043456 | tf_op jit(solution)/shard_map/wd,td->wt/dot_general | solution.py:109
  122.5 0.9 fusion.41
  124.0 5.9 %fusion.29 = f32[8,16,10,16,2]{1,3,2,0,4:T(8,128)S(1)} fusion(bf16[2,16,1024,1,1]{2,1,4,3,0:T(8,128)(2,1)S(1)} %bitcast.194, bf16[8,16,10,1024]{3,2,1,0:T(8,128)(2,1)} %dot_general.64), kind=kOutput, calls=%fused_computation.27 | convolution fusion | flops 83886080 | bytes 2850816 | tf_op jit(solution)/shard_map/dot_general | solution.py:114
  130.0 1.8 %copy.118 = f32[8,16,10,16,2]{1,0,4,3,2:T(8,128)} copy(f32[8,16,10,16,2]{1,3,2,0,4:T(8,128)S(1)} %fusion.29) | data formatting | bytes 327680 | tf_op jit(solution)/shard_map/transpose | solution.py:115
  131.8 2.3 %all_to_all.34 = f32[128,1,320]{0,2,1:T(8,128)} reshape(f32[8,16,10,16,2]{1,0,4,3,2:T(8,128)} %copy.118) | data formatting | bytes 327680 | tf_op jit(solution)/shard_map/all_to_all | solution.py:116
  134.1 1.7 %copy.119 = f32[128,1,320]{2,1,0:T(1,128)} copy(f32[128,1,320]{0,2,1:T(8,128)} %all_to_all.34) | data formatting | bytes 327680 | tf_op jit(solution)/shard_map/all_to_all | solution.py:116
  135.9 10.3 %all-to-all-start.4 = ((f32[128,1,320]{2,1,0:T(1,128)}), f32[128,1,320]{2,1,0:T(1,128)}, u32[]{:S(2)}, u32[]{:S(2)}) async-start(f32[128,1,320]{2,1,0:T(1,128)} %copy.119), calls=%async_computation.4 | async-start | bytes 393216 | tf_op jit(solution)/shard_map/all_to_all | solution.py:116
  146.2 2.8 %convolution_convert_fusion.1 = bf16[2,1280,640]{2,1,0:T(8,128)(2,1)} fusion(bf16[2,16,1280]{2,1,0:T(8,128)(2,1)S(1)} %fusion.45, bf16[2,16,640]{2,1,0:T(8,128)(2,1)S(1)} %copy-done.11), kind=kOutput, calls=%fused_computation.1 | convolution fusion | flops 54067200 | bytes 3399680 | tf_op jit(solution)/shard_map/kce,kcf->kef/dot_general | solution.py:93
  148.9 3.3 %fusion = bf16[1,1024,1280]{2,1,0:T(8,128)(2,1)} fusion(bf16[32,1024]{1,0:T(8,128)(2,1)S(1)} %fusion.82, bf16[32,1280]{1,0:T(8,128)(2,1)} %bitcast.186), kind=kOutput, calls=%fused_computation.4 | convolution fusion | flops 85196800 | bytes 2768896 | tf_op jit(solution)/shard_map/wt,wd->td/dot_general | solution.py:120
  152.2 4.1 %all-to-all-done.4 = f32[128,1,320]{2,1,0:T(1,128)} async-done(((f32[128,1,320]{2,1,0:T(1,128)}), f32[128,1,320]{2,1,0:T(1,128)}, u32[]{:S(2)}, u32[]{:S(2)}) %all-to-all-start.4) | async-done | bytes 163872 | tf_op jit(solution)/shard_map/all_to_all | solution.py:116
  156.4 1.1 reduce_sum.141
  158.1 3.9 %all-to-all-start.5 = ((f32[16,1,320]{2,1,0:T(1,128)}), f32[16,1,320]{2,1,0:T(1,128)S(1)}, u32[]{:S(2)}, u32[]{:S(2)}) async-start(f32[16,1,320]{2,1,0:T(1,128)} %broadcast_in_dim.25), calls=%async_computation.5 | async-start | bytes 49152 | tf_op jit(solution)/shard_map/all_to_all | solution.py:124
  162.0 3.2 %fusion.1 = bf16[1,1024,1280]{2,1,0:T(8,128)(2,1)} fusion(bf16[32,1280]{1,0:T(8,128)(2,1)S(1)} %bitcast.184, bf16[32,1280]{1,0:T(8,128)(2,1)S(1)} %bitcast.188, bf16[32,1024]{1,0:T(8,128)(2,1)} %get-tuple-element.56, bf16[32,1024]{1,0:T(8,128)(2,1)} %copy-done.12), kind=kOutput, calls=%fused_computation.5 | convolution fusion | flops 169672704 | bytes 2916352 | tf_op jit(solution)/shard_map/wt,wd->td/dot_general | solution.py:123
  165.2 2.6 %all-to-all-done.5 = f32[16,1,320]{2,1,0:T(1,128)S(1)} async-done(((f32[16,1,320]{2,1,0:T(1,128)}), f32[16,1,320]{2,1,0:T(1,128)S(1)}, u32[]{:S(2)}, u32[]{:S(2)}) %all-to-all-start.5) | async-done | bytes 20512 | tf_op jit(solution)/shard_map/all_to_all | solution.py:124
  (99 shorter events, 15.8 us)
Async XLA Ops:
  0.6 60.7 %copy-start = (bf16[2,1280,640]{2,1,0:T(8,128)(2,1)S(1)}, bf16[2,1280,640]{2,1,0:T(8,128)(2,1)}, u32[]{:S(2)}) copy-start(bf16[2,1280,640]{2,1,0:T(8,128)(2,1)} %param.7) | copy-start | bytes 9830404
  1.7 4.3 %copy-start.1 = (bf16[1,1024,1280]{2,1,0:T(8,128)(2,1)S(1)}, bf16[1,1024,1280]{2,1,0:T(8,128)(2,1)}, u32[]{:S(2)}) copy-start(bf16[1,1024,1280]{2,1,0:T(8,128)(2,1)} %param.5) | copy-start | bytes 7864324
  1.8 0.6 copy-start.6
  5.3 0.7 copy-start.13
  7.4 3.1 %copy-start.18 = (bf16[16,6]{1,0:T(8,128)(2,1)S(1)}, bf16[16,6]{1,0:T(8,128)(2,1)}, u32[]{:S(2)}) copy-start(bf16[16,6]{1,0:T(8,128)(2,1)} %copy.127) | copy-start | bytes 580
  11.2 10.0 %all-to-all-start = ((bf16[4,16,1408]{2,1,0:T(8,128)(2,1)}), bf16[4,16,1408]{2,1,0:T(8,128)(2,1)}, u32[]{:S(2)}, u32[]{:S(2)}) async-start(bf16[4,16,1408]{2,1,0:T(8,128)(2,1)} %pad_maximum_fusion), calls=%async_computation | async-start | bytes 360448 | tf_op jit(solution)/shard_map/all_to_all | solution.py:67
  58.9 3.0 %copy-start.3 = (bf16[2,640,1280]{2,1,0:T(8,128)(2,1)S(1)}, bf16[2,640,1280]{2,1,0:T(8,128)(2,1)}, u32[]{:S(2)}) copy-start(bf16[2,640,1280]{2,1,0:T(8,128)(2,1)} %param.8) | copy-start | bytes 9830404
  60.3 2.6 %copy-start.8 = (bf16[2,16,1280]{2,1,0:T(8,128)(2,1)}, bf16[2,16,1280]{2,1,0:T(8,128)(2,1)S(1)}, u32[]{:S(2)}) copy-start(bf16[2,16,1280]{2,1,0:T(8,128)(2,1)S(1)} %slice_reduce_fusion.1) | copy-start | bytes 245764
  60.5 0.6 copy-start.19
  61.9 2.0 %copy-start.9 = (f32[2,16,640]{2,1,0:T(8,128)}, f32[2,16,640]{2,1,0:T(8,128)S(1)}, u32[]{:S(2)}) copy-start(f32[2,16,640]{2,1,0:T(8,128)S(1)} %get-tuple-element.72) | copy-start | bytes 245764
  61.9 2.0 %copy-start.16 = (u8[16,640]{1,0:T(8,128)(4,1)}, u8[16,640]{1,0:T(8,128)(4,1)S(1)}, u32[]{:S(2)}) copy-start(u8[16,640]{1,0:T(8,128)(4,1)S(1)} %get-tuple-element.44) | copy-start | bytes 30724
  61.9 2.0 %copy-start.17 = (u8[16,640]{1,0:T(8,128)(4,1)}, u8[16,640]{1,0:T(8,128)(4,1)S(1)}, u32[]{:S(2)}) copy-start(u8[16,640]{1,0:T(8,128)(4,1)S(1)} %get-tuple-element.45) | copy-start | bytes 30724
  62.9 1.6 copy-start.10
  85.3 20.3 %all-to-all-start.3 = ((bf16[128,2,704]{2,1,0:T(2,128)(2,1)}), bf16[128,2,704]{2,1,0:T(2,128)(2,1)}, u32[]{:S(2)}, u32[]{:S(2)}) async-start(bf16[128,2,704]{2,1,0:T(2,128)(2,1)} %reshape.283), calls=%async_computation.3 | async-start | bytes 786432 | tf_op jit(solution)/shard_map/all_to_all | solution.py:103
  119.2 3.3 %copy-start.2 = (bf16[1,1024,1280]{2,1,0:T(8,128)(2,1)S(1)}, bf16[1,1024,1280]{2,1,0:T(8,128)(2,1)}, u32[]{:S(2)}) copy-start(bf16[1,1024,1280]{2,1,0:T(8,128)(2,1)} %param.5) | copy-start | bytes 7864324
  119.2 3.3 %copy-start.4 = (bf16[2,1,16,1280]{3,2,1,0:T(8,128)(2,1)S(1)}, bf16[2,1,16,1280]{3,2,1,0:T(8,128)(2,1)}, u32[]{:S(2)}) copy-start(bf16[2,1,16,1280]{3,2,1,0:T(8,128)(2,1)} %get-tuple-element.53) | copy-start | bytes 245764
  119.2 3.3 %copy-start.14 = (f32[1024]{0:T(1024)S(1)}, f32[1024]{0:T(1024)}, u32[]{:S(2)}) copy-start(f32[1024]{0:T(1024)} %copy-done.13) | copy-start | bytes 12292
  119.2 3.3 %copy-start.15 = (f32[1024]{0:T(1024)S(1)}, f32[1024]{0:T(1024)}, u32[]{:S(2)}) copy-start(f32[1024]{0:T(1024)} %get-tuple-element.41) | copy-start | bytes 12292
  119.2 3.3 %copy-start.20 = (f32[32]{0:T(128)S(1)}, f32[32]{0:T(128)}, u32[]{:S(2)}) copy-start(f32[32]{0:T(128)} %add.130) | copy-start | bytes 388
  119.2 3.3 %copy-start.21 = (f32[32]{0:T(128)S(1)}, f32[32]{0:T(128)}, u32[]{:S(2)}) copy-start(f32[32]{0:T(128)} %sub.183) | copy-start | bytes 388
  123.4 0.6 copy-start.12
  130.0 16.2 %copy-start.11 = (bf16[2,16,640]{2,1,0:T(8,128)(2,1)S(1)}, bf16[2,16,640]{2,1,0:T(8,128)(2,1)}, u32[]{:S(2)}) copy-start(bf16[2,16,640]{2,1,0:T(8,128)(2,1)} %copy-done.10) | copy-start | bytes 122884
  135.9 20.5 %all-to-all-start.4 = ((f32[128,1,320]{2,1,0:T(1,128)}), f32[128,1,320]{2,1,0:T(1,128)}, u32[]{:S(2)}, u32[]{:S(2)}) async-start(f32[128,1,320]{2,1,0:T(1,128)} %copy.119), calls=%async_computation.4 | async-start | bytes 393216 | tf_op jit(solution)/shard_map/all_to_all | solution.py:116
  146.2 15.8 %copy-start.5 = (bf16[2,1,16,1280]{3,2,1,0:T(8,128)(2,1)S(1)}, bf16[2,1,16,1280]{3,2,1,0:T(8,128)(2,1)}, u32[]{:S(2)}) copy-start(bf16[2,1,16,1280]{3,2,1,0:T(8,128)(2,1)} %get-tuple-element.53) | copy-start | bytes 245764
  148.9 13.0 %copy-start.7 = (bf16[2,16,1280]{2,1,0:T(8,128)(2,1)S(1)}, bf16[2,16,1280]{2,1,0:T(8,128)(2,1)}, u32[]{:S(2)}) copy-start(bf16[2,16,1280]{2,1,0:T(8,128)(2,1)} %copy-done.6) | copy-start | bytes 245764
  158.1 9.7 %all-to-all-start.5 = ((f32[16,1,320]{2,1,0:T(1,128)}), f32[16,1,320]{2,1,0:T(1,128)S(1)}, u32[]{:S(2)}, u32[]{:S(2)}) async-start(f32[16,1,320]{2,1,0:T(1,128)} %broadcast_in_dim.25), calls=%async_computation.5 | async-start | bytes 49152 | tf_op jit(solution)/shard_map/all_to_all | solution.py:124

commit v2 on v1

v2 whole, which is shorter than its diff:
```python
import math

import jax
import jax.numpy as jnp
from jax import lax
from jax.experimental import pallas as pl
from jax.experimental.pallas import tpu as pltpu
from jax.sharding import Mesh, PartitionSpec as P

bf16 = jnp.bfloat16
f32 = jnp.float32
ALL = ("yh", "x", "z", "yl", "core")
SEQ = ("yh", "x")
EXP = ("z", "yl", "core")
CHIPS = ("yh", "x", "z", "yl")
LANES = 128
CHUNKS = 4
MIB = 1024 * 1024

VMEM = pl.BlockSpec(memory_space=pltpu.VMEM)
SMEM = pl.BlockSpec(memory_space=pltpu.SMEM)
HBM = pl.BlockSpec(memory_space=pl.ANY)


def nn(a, b):
    return jnp.dot(a, b, preferred_element_type=f32)


def nt(a, b):
    return lax.dot_general(a, b, (((1,), (1,)), ((), ())), preferred_element_type=f32)


def tn(a, b):
    return lax.dot_general(a, b, (((0,), (0,)), ((), ())), preferred_element_type=f32)


def shape(dims, dtype):
    return jax.ShapeDtypeStruct(dims, dtype)


def cost(flops, moved):
    return pl.CostEstimate(flops=flops, bytes_accessed=moved, transcendentals=0)


def pieces(value):
    high = value.astype(bf16).astype(f32)
    rest = value - high
    middle = rest.astype(bf16).astype(f32)
    return high, middle, rest - middle


def in_lanes(columns):
    rows = columns[0].shape[0]
    lane = lax.broadcasted_iota(jnp.int32, (rows, LANES), 1)
    result = jnp.zeros((rows, LANES), f32)
    for place, column in enumerate(columns):
        result = jnp.where(lane == place, column, result)
    return result


def from_lanes(block, first):
    lane = lax.broadcasted_iota(jnp.int32, block.shape, 1)
    kept = jnp.where((lane >= first) & (lane < first + 3), block, 0.0)
    return jnp.sum(kept, axis=1, keepdims=True)


def log_sum_exp(values):
    top = values[0]
    for value in values[1:]:
        top = jnp.maximum(top, value)
    total = jnp.exp(values[0] - top)
    for value in values[1:]:
        total = total + jnp.exp(value - top)
    return top + jnp.log(total)


def normal(value):
    return 0.5 * (1.0 + lax.erf(value * (1.0 / math.sqrt(2.0))))


def router_rows(router_ref, owners, held):
    slots = owners * held
    row = lax.broadcasted_iota(jnp.int32, (slots, slots), 0)
    column = lax.broadcasted_iota(jnp.int32, (slots, slots), 1)
    order = (column == (row % owners) * held + row // owners).astype(bf16)
    return nt(order, router_ref[...]).astype(bf16)


def slot_softmax(logits):
    top = jnp.max(logits, axis=0, keepdims=True)
    raw = jnp.exp(logits - top)
    return raw / jnp.sum(raw, axis=0, keepdims=True)


def first_kernel(
    x_ref, tok_ref, router_ref, grad_ref, out0, out1, out2, out3, logits_ref,
    tok, grad, held_rows, sems,
):
    length, width = tok_ref.shape
    slots = router_ref.shape[1]
    owners = out0.shape[0]
    held = slots // owners
    chunk = length // CHUNKS
    copies = []
    for source, target, first in ((tok_ref, tok, 0), (grad_ref, grad, CHUNKS)):
        for part in range(CHUNKS):
            rows = pl.ds(part * chunk, chunk)
            copies.append(
                pltpu.make_async_copy(
                    source.at[rows, :], target.at[rows, :], sems.at[first + part]
                )
            )
    for copy in copies:
        copy.start()
    table = router_rows(router_ref, owners, held)
    for part in range(CHUNKS):
        copies[part].wait()
        rows = pl.ds(part * chunk, chunk)
        logits_ref[:, rows] = nt(table, tok[rows, :])
    logits = logits_ref[...]
    top = jnp.max(logits, axis=1, keepdims=True)
    raw = jnp.exp(logits - top)
    total = jnp.sum(raw, axis=1, keepdims=True)
    local_slot = nn(raw.astype(bf16), tok[...]) / total
    lse = top + jnp.log(total)
    probs = slot_softmax(logits).astype(bf16)
    for copy in copies[CHUNKS:]:
        copy.wait()
    local_grad = nn(probs, grad[...])
    columns = []
    for place in range(held):
        columns += pieces(lse[place * owners : (place + 1) * owners])
    extra = in_lanes(columns).astype(bf16)
    for place in range(held):
        for array, value in enumerate((local_slot, local_grad)):
            quarter = place * 2 + array
            rows = value[place * owners : (place + 1) * owners]
            held_rows[quarter, :, :width] = rows.astype(bf16)
            held_rows[quarter, :, width:] = extra
    x = x_ref[0]
    for turn, out in enumerate((out0, out1, out2, out3)):
        out[...] = held_rows[(x + turn) % 4]


def write_rows(out_ref, row, extra):
    owners, width = row.shape
    half = width // 2
    halves = [
        jnp.concatenate([row[:, :half], extra], axis=1),
        jnp.concatenate([row[:, half:], extra], axis=1),
    ]
    both = jnp.stack(halves, axis=1).astype(bf16)
    for member in range(out_ref.shape[0] // owners):
        out_ref[member * owners : (member + 1) * owners] = both


def read_rows(got_ref, member, owners):
    first = member * owners
    half = got_ref.shape[2] - LANES
    left = got_ref[first : first + owners, 0, :].astype(f32)
    right = got_ref[first : first + owners, 1, :].astype(f32)
    return jnp.concatenate([left[:, :half], right[:, :half]], axis=1), left[:, half:]


def first_sum_kernel(x_ref, in0, in1, in2, in3, out_ref):
    width = in0.shape[1] - LANES
    x = x_ref[0]
    blocks = [ref[...].astype(f32) for ref in (in0, in1, in2, in3)]
    lses = []
    for block in blocks:
        extra = block[:, width:]
        lses.append(jnp.where(x // 2 == 0, from_lanes(extra, 0), from_lanes(extra, 3)))
    lse = log_sum_exp(lses)
    row = None
    for block, part in zip(blocks, lses):
        scale = jnp.where(x % 2 == 0, jnp.exp(part - lse), 1.0)
        term = block[:, :width] * scale
        row = term if row is None else row + term
    write_rows(out_ref, row, in_lanes(pieces(lse)))


def expert_kernel(
    x_ref, got_ref, w_in_ref, w_out_ref,
    out0, out1, out2, out3, slot_ref, slot_grad_ref, hidden_ref, pre_ref, lse_ref, held_rows,
):
    held = w_in_ref.shape[0]
    owners = out0.shape[0]
    for place in range(held):
        rows, lses = [], []
        for y in range(2):
            data, extra = read_rows(got_ref, y * 4 + place * 2, owners)
            rows.append(data)
            lses.append(from_lanes(extra, 0))
        lse = log_sum_exp(lses)
        slot = (
            rows[0] * jnp.exp(lses[0] - lse) + rows[1] * jnp.exp(lses[1] - lse)
        ).astype(bf16)
        grads = [read_rows(got_ref, y * 4 + place * 2 + 1, owners)[0] for y in range(2)]
        slot_grad = (grads[0] + grads[1]).astype(bf16)
        slot_ref[place] = slot
        slot_grad_ref[place] = slot_grad
        lse_ref[place] = in_lanes(pieces(lse))
        activation = nn(slot, w_in_ref[place])
        hidden_grad = nt(slot_grad, w_out_ref[place])
        cumulative = normal(activation)
        density = jnp.exp(-0.5 * activation * activation) * (1.0 / math.sqrt(2.0 * math.pi))
        hidden = (activation * cumulative).astype(bf16)
        pre = (hidden_grad * (cumulative + activation * density)).astype(bf16)
        hidden_ref[place] = hidden
        pre_ref[place] = pre
        held_rows[place * 2] = nn(hidden, w_out_ref[place]).astype(bf16)
        held_rows[place * 2 + 1] = nt(pre, w_in_ref[place]).astype(bf16)
    x = x_ref[0]
    for turn, out in enumerate((out0, out1, out2, out3)):
        out[...] = held_rows[(x + turn) % 4]


def weight_kernel(slot_ref, slot_grad_ref, hidden_ref, pre_ref, w_in_ref, w_out_ref):
    w_out_ref[0] = tn(hidden_ref[0], slot_grad_ref[0]).astype(bf16)
    w_in_ref[0] = tn(slot_ref[0], pre_ref[0]).astype(bf16)


def second_sum_kernel(x_ref, in0, in1, in2, in3, slot_ref, lse_ref, out_ref):
    place = x_ref[0] // 2
    row = in0[...].astype(f32) + in1[...].astype(f32) + in2[...].astype(f32) + in3[...].astype(f32)
    row = row.astype(bf16).astype(f32)
    shift = jnp.sum(slot_ref[place].astype(f32) * row, axis=1, keepdims=True)
    columns = in_lanes((shift * 0.0,) * 3 + pieces(shift))
    write_rows(out_ref, row, lse_ref[place] + columns)


def token_kernel(
    core_ref, got_ref, logits_ref, tok_ref, grad_ref,
    slot_out_ref, in_half_ref, mix_ref, keep_ref, give_ref, sums,
):
    slots = logits_ref.shape[0]
    width = tok_ref.shape[1]
    owners = 16
    held = slots // owners
    lses, shifts = [], []
    for place in range(held):
        span = slice(place * owners, (place + 1) * owners)
        first, extra = read_rows(got_ref, place * 2, owners)
        second, _ = read_rows(got_ref, 4 + place * 2, owners)
        slot_out_ref[span] = (first + second).astype(bf16)
        lses.append(from_lanes(extra, 0))
        first, extra_a = read_rows(got_ref, place * 2 + 1, owners)
        second, extra_b = read_rows(got_ref, 4 + place * 2 + 1, owners)
        in_half_ref[span] = (first + second).astype(bf16)
        shifts.append(from_lanes(extra_a, 3) + from_lanes(extra_b, 3))
    lse = jnp.concatenate(lses, axis=0)
    shift = jnp.concatenate(shifts, axis=0)
    logits = logits_ref[...]
    probs = slot_softmax(logits)
    share = jnp.exp(logits - lse)
    grad_probs = nt(slot_out_ref[...], grad_ref[...])
    comb = probs * (grad_probs - jnp.sum(probs * grad_probs, axis=0, keepdims=True))
    inner = nt(in_half_ref[...], tok_ref[...])
    logit_grad = (comb + share * (inner - shift)).astype(bf16)
    mix_ref[0:slots] = probs.astype(bf16)
    mix_ref[slots : 2 * slots] = logit_grad
    mix_ref[2 * slots : 3 * slots] = share.astype(bf16)
    total = nn(logit_grad, tok_ref[...])
    half = slots // 2
    sums[0] = total[:half]
    sums[1] = total[half:]
    core = core_ref[0]
    keep_ref[...] = sums[core]
    give_ref[...] = sums[1 - core]


def router_split_kernel(keep_ref, got_ref, out_ref):
    width = keep_ref.shape[1]
    share = width // 8
    total = keep_ref[...] + got_ref[...]
    rest = jnp.zeros((keep_ref.shape[0], out_ref.shape[2] - share), bf16)
    for member in range(8):
        part = total[:, member * share : (member + 1) * share].astype(bf16)
        for copy in range(8):
            out_ref[member * 8 + copy, :, :share] = part
            out_ref[member * 8 + copy, :, share:] = rest


def router_sum_kernel(got_ref, out_ref):
    total = got_ref[0].astype(f32)
    for member in range(1, got_ref.shape[0]):
        total = total + got_ref[member].astype(f32)
    out_ref[...] = total


def mix_kernel(mix_ref, slot_out_ref, in_half_ref, router_ref, mixed_ref, grad_ref):
    slots, width = slot_out_ref.shape
    mixed_ref[...] = tn(mix_ref[0:slots], slot_out_ref[...]).astype(bf16)
    table = jnp.concatenate(
        [router_rows(router_ref, 16, slots // 16), in_half_ref[...]], axis=0
    )
    grad_ref[...] = tn(mix_ref[slots : 3 * slots], table).astype(bf16)


def around_x(arrays):
    got = [arrays[0]]
    for turn in range(1, 4):
        pairs = [(place, (place + turn) % 4) for place in range(4)]
        got.append(lax.ppermute(arrays[turn], "x", pairs))
    return got


def params(mib):
    return pltpu.CompilerParams(vmem_limit_bytes=mib * MIB)


def per_device(tokens, router, w_in, w_out, grad_out):
    x = lax.axis_index("x").astype(jnp.int32).reshape(1)
    core = lax.axis_index("core").astype(jnp.int32).reshape(1)
    tok = tokens[0]
    grad = grad_out[0]
    length, width = tok.shape
    slots = router.shape[1]
    held, _, units = w_in.shape
    owners = slots // held
    wide = width + LANES
    sent = shape((8 * owners, 2, width // 2 + LANES), bf16)
    token_flops = 2 * length * width * slots
    expert_flops = 2 * held * owners * width * units

    *send, logits = pl.pallas_call(
        first_kernel,
        out_shape=[shape((owners, wide), bf16)] * 4 + [shape((slots, length), f32)],
        in_specs=[SMEM, HBM, VMEM, HBM],
        out_specs=[VMEM] * 5,
        scratch_shapes=[
            pltpu.VMEM((length, width), bf16),
            pltpu.VMEM((length, width), bf16),
            pltpu.VMEM((4, owners, wide), bf16),
            pltpu.SemaphoreType.DMA((2 * CHUNKS,)),
        ],
        compiler_params=params(24),
        cost_estimate=cost(3 * token_flops, 4 * length * width),
        name="first",
    )(x, tok, router, grad)
    got = around_x(send)
    send = pl.pallas_call(
        first_sum_kernel,
        out_shape=sent,
        in_specs=[SMEM] + [VMEM] * 4,
        out_specs=VMEM,
        compiler_params=params(8),
        name="first_sum",
    )(x, *got)
    got = lax.all_to_all(send, ALL, 0, 0, tiled=True)
    *send, slot, slot_grad, hidden, pre, lse = pl.pallas_call(
        expert_kernel,
        out_shape=[shape((owners, width), bf16)] * 4
        + [shape((held, owners, width), bf16)] * 2
        + [shape((held, owners, units), bf16)] * 2
        + [shape((held, owners, LANES), f32)],
        in_specs=[SMEM] + [VMEM] * 3,
        out_specs=[VMEM] * 9,
        scratch_shapes=[pltpu.VMEM((4, owners, width), bf16)],
        compiler_params=params(24),
        cost_estimate=cost(4 * expert_flops, 4 * held * width * units),
        name="experts",
    )(x, got, w_in, w_out)
    got = around_x(send)
    send = pl.pallas_call(
        second_sum_kernel,
        out_shape=sent,
        in_specs=[SMEM] + [VMEM] * 6,
        out_specs=VMEM,
        compiler_params=params(8),
        name="second_sum",
    )(x, *got, slot, lse)
    got = lax.all_to_all(send, ALL, 0, 0, tiled=True)
    rows = lambda last: pl.BlockSpec((1, owners, last), lambda k: (k, 0, 0))
    grad_w_in, grad_w_out = pl.pallas_call(
        weight_kernel,
        grid=(held,),
        out_shape=[shape((held, width, units), bf16), shape((held, units, width), bf16)],
        in_specs=[rows(width), rows(width), rows(units), rows(units)],
        out_specs=[
            pl.BlockSpec((1, width, units), lambda k: (k, 0, 0)),
            pl.BlockSpec((1, units, width), lambda k: (k, 0, 0)),
        ],
        compiler_params=params(24),
        cost_estimate=cost(2 * expert_flops * 8, 4 * held * width * units),
        name="weights",
    )(slot, slot_grad, hidden, pre)
    slot_out, in_half, mix, keep, give = pl.pallas_call(
        token_kernel,
        out_shape=[shape((slots, width), bf16)] * 2
        + [shape((3 * slots, length), bf16)]
        + [shape((slots // 2, width), f32)] * 2,
        in_specs=[SMEM] + [VMEM] * 4,
        out_specs=[VMEM] * 5,
        scratch_shapes=[pltpu.VMEM((2, slots // 2, width), f32)],
        compiler_params=params(24),
        cost_estimate=cost(3 * token_flops, 4 * length * width),
        name="tokens",
    )(core, got, logits, tok, grad)
    swap = [(0, 1), (1, 0)]
    got = lax.ppermute(give, "core", swap)
    send = pl.pallas_call(
        router_split_kernel,
        out_shape=shape((64, slots // 2, 256), bf16),
        in_specs=[VMEM] * 2,
        out_specs=VMEM,
        compiler_params=params(8),
        name="router_split",
    )(keep, got)
    got = lax.all_to_all(send, CHIPS, 0, 0, tiled=True)
    half = pl.pallas_call(
        router_sum_kernel,
        out_shape=shape((slots // 2, 256), f32),
        in_specs=[VMEM],
        out_specs=VMEM,
        compiler_params=params(8),
        name="router_sum",
    )(got)
    other = lax.ppermute(half, "core", swap)
    chunk = length // 4
    mixed, grad_tokens = pl.pallas_call(
        mix_kernel,
        grid=(4,),
        out_shape=[shape((length, width), bf16)] * 2,
        in_specs=[
            pl.BlockSpec((3 * slots, chunk), lambda i: (0, i)),
            pl.BlockSpec((slots, width), lambda i: (0, 0)),
            pl.BlockSpec((slots, width), lambda i: (0, 0)),
            pl.BlockSpec((width, slots), lambda i: (0, 0)),
        ],
        out_specs=[pl.BlockSpec((chunk, width), lambda i: (i, 0))] * 2,
        compiler_params=params(24),
        cost_estimate=cost(3 * token_flops * 4, 4 * length * width),
        name="mix",
    )(mix, slot_out, in_half, router)
    share = width // 8
    first = jnp.where(core[0] == 0, half, other)
    second = jnp.where(core[0] == 0, other, half)
    grad_router = jnp.stack([first, second], axis=0)[:, :, :share]
    grad_router = grad_router.transpose(2, 1, 0).reshape(share, slots)
    return (mixed[None], grad_tokens[None], grad_router, grad_w_in, grad_w_out)


def solution(mesh):
    fine = Mesh(mesh.devices.reshape(2, 4, 4, 2, 2), ALL)
    in_specs = (
        P(EXP, SEQ, None),
        P(),
        P(EXP, None, SEQ),
        P(EXP, SEQ, None),
        P(EXP, SEQ, None),
    )
    out_specs = (
        P(EXP, SEQ, None),
        P(EXP, SEQ, None),
        P(SEQ, None),
        P(EXP, None, SEQ),
        P(EXP, SEQ, None),
    )
    return jax.shard_map(
        per_device, mesh=fine, in_specs=in_specs, out_specs=out_specs, check_vma=False
    )
```

time: 170 us -> 104 us (0.61)
  local copies, waits for them, and re-layouts: 48.8 us -> 13.2 us
  matrix products: 32 us -> 0 us
  Pallas kernels: 0 us -> 19.5 us
  other arithmetic: 18.9 us -> 0.01 us
  waiting for transfers between devices: 11.9 us -> 22.4 us
  blocking collectives: 30.7 us -> 23.8 us
    dot_general x14 -> x0, matrix products: 32 us -> none  [the longest x1 5.93 us: per_device(): router_local = jnp.dot(logit_grad, tok, preferred_element_type=f32)]
    pallas_call x0 -> x9, Pallas kernels: none -> 19.5 us  [the longest x1 5.06 us: per_device(): pl.pallas_call(first_kernel, out_shape=[shape((owners, wide), bf16)] * 4...]
    all_to_all x4 -> x2, starting transfers between devices: 25.3 us -> 11.8 us  [the longest x1 6.85 us: per_device(): got = lax.all_to_all(send, ALL, 0, 0, tiled=True)]
    ppermute x0 -> x8, starting transfers between devices: none -> 12.3 us  [the longest x6 9.1 us: around_x(): got.append(lax.ppermute(arrays[turn], 'x', pairs))]
    dot_general x2 -> x0, local copies, waits for them, and re-layouts: 10.3 us -> none  [per_device(): router_local = jnp.dot(logit_grad, tok, preferred_element_type=f32)]
    unnamed x57 -> x37, local copies, waits for them, and re-layouts: 21 us -> 12.6 us
    reduce_sum x11 -> x0, other arithmetic: 7.12 us -> none  [the longest x1 1.6 us: per_device(): jnp.sum(joined(got[:, :, 1, :, width + 3:width + 6]), axis=0)]
    all_to_all x2 -> x1, blocking collectives: 30.7 us -> 23.8 us  [per_device(): got = lax.all_to_all(send, ALL, 0, 0, tiled=True)]
  transfers between devices with their start and end apart: 4 -> 10, of which waited for: 3 -> 7; matrix products, arithmetic and copies ran while one was open for 14% -> 0% of each run, Pallas kernels for 0% -> 7%
where the time goes in v2:
time: 104 us
  starting transfers between devices  24.1 us (23%)
  blocking collectives  23.8 us (23%)
  waiting for transfers between devices  22.4 us (22%)
  Pallas kernels  19.5 us (19%)
  local copies, waits for them, and re-layouts  13.2 us (13%)
    all_to_all x1, blocking collectives, per_device(): got = lax.all_to_all(send, ALL, 0, 0, tiled=True)  23.8 us
    unnamed x37, local copies, waits for them, and re-layouts  12.6 us
    all_to_all x1, waiting for transfers between devices, per_device(): got = lax.all_to_all(send, ALL, 0, 0, tiled=True)  12.2 us
    ppermute x6, starting transfers between devices, around_x(): got.append(lax.ppermute(arrays[turn], 'x', pairs))  9.1 us
    all_to_all x1, starting transfers between devices, per_device(): got = lax.all_to_all(send, ALL, 0, 0, tiled=True)  6.85 us
    all_to_all x1, waiting for transfers between devices, per_device(): got = lax.all_to_all(send, CHIPS, 0, 0, tiled=True)  5.2 us
    pallas_call x1, Pallas kernels, per_device(): pl.pallas_call(first_kernel, out_shape=[shape((owners, wide), bf16)] * 4...  5.06 us
    all_to_all x1, starting transfers between devices, per_device(): got = lax.all_to_all(send, CHIPS, 0, 0, tiled=True)  5 us
  transfers between devices with their start and end apart: 10, of which 7 were waited for; matrix products, arithmetic and copies ran while one was open for 0% of the time, Pallas kernels for 7%

profile of v2, /device:TPU:1, one launch (start us, length us, event | category | flops | bytes accessed | tf_op | source)
XLA Modules:
  0.0 103.7 jit_solution(2608558111606221525)
XLA Ops:
  0.6 1.1 %copy.12.router_ref = bf16[1280,32]{1,0:T(8,128)(2,1)S(1)} copy(bf16[1280,32]{0,1:T(8,128)(2,1)} %param.6) | data formatting | bytes 163840 | tf_op args[1]
  1.7 0.0 copy-start
  1.8 1.7 %copy-done = bf16[1,1024,1280]{2,1,0:T(8,128)(2,1)S(1)} copy-done((bf16[1,1024,1280]{2,1,0:T(8,128)(2,1)S(1)}, bf16[1,1024,1280]{2,1,0:T(8,128)(2,1)}, u32[]{:S(2)}) %copy-start) | copy-done | bytes 2621464
  3.5 1.7 %copy-done.2 = bf16[1,1024,1280]{2,1,0:T(8,128)(2,1)S(1)} copy-done((bf16[1,1024,1280]{2,1,0:T(8,128)(2,1)S(1)}, bf16[1,1024,1280]{2,1,0:T(8,128)(2,1)}, u32[]{:S(2)}) %copy-start.2) | copy-done | bytes 2621464
  5.2 5.1 %first.1 = (bf16[16,1408]{1,0:T(8,128)(2,1)S(1)}, bf16[16,1408]{1,0:T(8,128)(2,1)S(1)}, bf16[16,1408]{1,0:T(8,128)(2,1)S(1)}, bf16[16,1408]{1,0:T(8,128)(2,1)S(1)}, f32[32,1024]{1,0:T(8,128)S(1)}) custom-call(s32[1]{0:T(128)} %bitcast.1.x_ref, bf16[1024,1280]{1,0:T(8,128)(2,1)S(1)} %bitcast.14, bf16[1280,32]{1,0:T(8,128)(2,1)S(1)} %copy.12.router_ref, ...), custom_call_target="tpu_custom_call" | custom-call | flops 251658240 | bytes 5242880 | tf_op jit(solution)/shard_map/first/pallas_call | solution.py:326
  10.3 2.1 %collective-permute-start = (bf16[16,1408]{1,0:T(8,128)(2,1)S(1)}, bf16[16,1408]{1,0:T(8,128)(2,1)S(1)}, u32[]{:S(2)}, u32[]{:S(2)}) collective-permute-start(bf16[16,1408]{1,0:T(8,128)(2,1)S(1)} %get-tuple-element.29), channel_id=1, source_target_pairs={{0,16},{16,32},{32,48},{48,0},{1,17},{17,33},{33,49},{49,1},{2,18}... | collective-permute-start | bytes 135176 | tf_op jit(solution)/shard_map/ppermute | solution.py:304
  12.4 2.5 %collective-permute-start.1 = (bf16[16,1408]{1,0:T(8,128)(2,1)S(1)}, bf16[16,1408]{1,0:T(8,128)(2,1)S(1)}, u32[]{:S(2)}, u32[]{:S(2)}) collective-permute-start(bf16[16,1408]{1,0:T(8,128)(2,1)S(1)} %get-tuple-element.30), channel_id=1, source_target_pairs={{0,32},{16,48},{32,0},{48,16},{1,33},{17,49},{33,1},{49,17},{2,34}... | collective-permute-start | bytes 135176 | tf_op jit(solution)/shard_map/ppermute | solution.py:304
  14.9 1.1 %collective-permute-start.2 = (bf16[16,1408]{1,0:T(8,128)(2,1)S(1)}, bf16[16,1408]{1,0:T(8,128)(2,1)S(1)}, u32[]{:S(2)}, u32[]{:S(2)}) collective-permute-start(bf16[16,1408]{1,0:T(8,128)(2,1)S(1)} %get-tuple-element.31), channel_id=1, source_target_pairs={{0,48},{16,0},{32,16},{48,32},{1,49},{17,1},{33,17},{49,33},{2,50}... | collective-permute-start | bytes 135176 | tf_op jit(solution)/shard_map/ppermute | solution.py:304
  16.0 0.0 collective-permute-done.in1
  16.0 0.8 collective-permute-done.1.in2
  16.8 1.2 %collective-permute-done.2.in3 = bf16[16,1408]{1,0:T(8,128)(2,1)S(1)} collective-permute-done((bf16[16,1408]{1,0:T(8,128)(2,1)S(1)}, bf16[16,1408]{1,0:T(8,128)(2,1)S(1)}, u32[]{:S(2)}, u32[]{:S(2)}) %collective-permute-start.2) | collective-permute-done | bytes 45088 | tf_op jit(solution)/shard_map/ppermute | solution.py:304
  18.1 0.3 first_sum.1
  18.3 23.8 %all_to_all.15.got_ref = bf16[128,2,768]{2,1,0:T(2,128)(2,1)S(1)} all-to-all(bf16[128,2,768]{2,1,0:T(2,128)(2,1)S(1)} %first_sum.1), channel_id=1, replica_groups=mesh['yh'=2,'x'=4,'z'=4,'yl'=2,'core'=2] {'yh','x','z','yl','core'}, dimensions={0} | all-to-all | bytes 786432 | tf_op jit(solution)/shard_map/all_to_all | solution.py:350
  42.1 2.8 %experts.1 = (bf16[16,1280]{1,0:T(8,128)(2,1)S(1)}, bf16[16,1280]{1,0:T(8,128)(2,1)S(1)}, bf16[16,1280]{1,0:T(8,128)(2,1)S(1)}, bf16[16,1280]{1,0:T(8,128)(2,1)S...) custom-call(s32[1]{0:T(128)} %bitcast.1.x_ref, ...), custom_call_target="tpu_custom_call" | custom-call | flops 209715200 | bytes 6553600 | tf_op jit(solution)/shard_map/experts/pallas_call | solution.py:351
  44.9 0.0 copy-start.8
  44.9 0.6 copy-done.8
  45.5 0.6 copy-done.14
  46.2 0.6 copy-done.16
  46.8 0.0 collective-permute-start.3
  46.8 1.7 %collective-permute-start.4 = (bf16[16,1280]{1,0:T(8,128)(2,1)S(1)}, bf16[16,1280]{1,0:T(8,128)(2,1)S(1)}, u32[]{:S(2)}, u32[]{:S(2)}) collective-permute-start(bf16[16,1280]{1,0:T(8,128)(2,1)S(1)} %get-tuple-element.34), channel_id=1, source_target_pairs={{0,32},{16,48},{32,0},{48,16},{1,33},{17,49},{33,1},{49,17},{2,34}... | collective-permute-start | bytes 122888 | tf_op jit(solution)/shard_map/ppermute | solution.py:304
  48.5 1.7 %collective-permute-start.5 = (bf16[16,1280]{1,0:T(8,128)(2,1)S(1)}, bf16[16,1280]{1,0:T(8,128)(2,1)S(1)}, u32[]{:S(2)}, u32[]{:S(2)}) collective-permute-start(bf16[16,1280]{1,0:T(8,128)(2,1)S(1)} %get-tuple-element.35), channel_id=1, source_target_pairs={{0,48},{16,0},{32,16},{48,32},{1,49},{17,1},{33,17},{49,33},{2,50}... | collective-permute-start | bytes 122888 | tf_op jit(solution)/shard_map/ppermute | solution.py:304
  50.2 1.1 %collective-permute-done.3.in1 = bf16[16,1280]{1,0:T(8,128)(2,1)S(1)} collective-permute-done((bf16[16,1280]{1,0:T(8,128)(2,1)S(1)}, bf16[16,1280]{1,0:T(8,128)(2,1)S(1)}, u32[]{:S(2)}, u32[]{:S(2)}) %collective-permute-start.3) | collective-permute-done | bytes 40992 | tf_op jit(solution)/shard_map/ppermute | solution.py:304
  51.3 0.0 collective-permute-done.4.in2
  51.3 0.9 collective-permute-done.5.in3
  52.1 1.0 second_sum.1
  53.1 6.8 %all-to-all-start.1 = ((bf16[128,2,768]{2,1,0:T(2,128)(2,1)}), bf16[128,2,768]{2,1,0:T(2,128)(2,1)S(1)}, u32[]{:S(2)}, u32[]{:S(2)}) async-start(bf16[128,2,768]{2,1,0:T(2,128)(2,1)} %second_sum.1), calls=%async_computation.1 | async-start | bytes 786432 | tf_op jit(solution)/shard_map/all_to_all | solution.py:373
  60.0 12.2 %all-to-all-done.1.got_ref = bf16[128,2,768]{2,1,0:T(2,128)(2,1)S(1)} async-done(((bf16[128,2,768]{2,1,0:T(2,128)(2,1)}), bf16[128,2,768]{2,1,0:T(2,128)(2,1)S(1)}, u32[]{:S(2)}, u32[]{:S(2)}) %all-to-all-start.1) | async-done | bytes 393248 | tf_op jit(solution)/shard_map/all_to_all | solution.py:373
  72.2 1.7 %copy-done.3 = bf16[1,1024,1280]{2,1,0:T(8,128)(2,1)S(1)} copy-done((bf16[1,1024,1280]{2,1,0:T(8,128)(2,1)S(1)}, bf16[1,1024,1280]{2,1,0:T(8,128)(2,1)}, u32[]{:S(2)}) %copy-start.3) | copy-done | bytes 2621464
  73.9 2.1 %tokens.1 = (bf16[32,1280]{1,0:T(8,128)(2,1)S(1)}, bf16[32,1280]{1,0:T(8,128)(2,1)S(1)}, bf16[96,1024]{1,0:T(8,128)(2,1)S(1)}, f32[16,1280]{1,0:T(8,128)S(1)}, f32[16,1280]{1,0:T(8,128)S(1)}) custom-call(s32[1]{0:T(128)} %bitcast.core_ref, bf16[128,2,768]{2,1,0:T(2,128)(2,1)S(1)} %all-to-all-done.1.got_ref, f32[32,1024]{1,0:T(8,128)S(1)} %get-tuple-element.38.logits_ref, ...), custom_call_target="tpu_custom_call" | custom-call | flops 251658240 | bytes 5242880 | tf_op jit(solution)/shard_map/tokens/pallas_call | solution.py:388
  76.0 0.0 copy-start.6
  76.1 0.7 copy-done.6
  76.7 0.6 copy-done.10
  77.4 0.6 copy-done.12
  78.0 0.7 collective-permute-start.6
  78.7 0.9 collective-permute-done.6.got_ref
  79.6 0.9 router_split.1
  80.5 5.0 %all-to-all-start.2 = ((bf16[64,16,256]{2,1,0:T(8,128)(2,1)}), bf16[64,16,256]{2,1,0:T(8,128)(2,1)S(1)}, u32[]{:S(2)}, u32[]{:S(2)}) async-start(bf16[64,16,256]{2,1,0:T(8,128)(2,1)} %router_split.1), calls=%async_computation.2 | async-start | bytes 1048576 | tf_op jit(solution)/shard_map/all_to_all | solution.py:410
  85.5 0.0 copy-start.9
  85.6 0.9 copy-done.9
  86.4 0.8 copy-done.15
  87.2 0.8 copy-done.17
  88.0 3.5 %weights.1 = (bf16[2,1280,640]{2,1,0:T(8,128)(2,1)}, bf16[2,640,1280]{2,1,0:T(8,128)(2,1)}) custom-call(bf16[2,16,1280]{2,1,0:T(8,128)(2,1)S(1)} %get-tuple-element.36.slot_ref, bf16[2,16,1280]{2,1,0:T(8,128)(2,1)S(1)} %copy-done.9, bf16[2,16,640]{2,1,0:T(8,128)(2,1)S(1)} %copy-done.15, bf16[2,16,640]{2,1,0:T(8,128)(2,1)S(1)} %copy-done.17), custom_call_target="tpu_custom_call" | custom-call | flops 838860800 | bytes 6553600 | tf_op jit(solution)/shard_map/weights/pallas_call | solution.py:375
  91.5 5.2 %all-to-all-done.2.got_ref = bf16[64,16,256]{2,1,0:T(8,128)(2,1)S(1)} async-done(((bf16[64,16,256]{2,1,0:T(8,128)(2,1)}), bf16[64,16,256]{2,1,0:T(8,128)(2,1)S(1)}, u32[]{:S(2)}, u32[]{:S(2)}) %all-to-all-start.2) | async-done | bytes 524320 | tf_op jit(solution)/shard_map/all_to_all | solution.py:410
  96.7 0.1 router_sum.1
  96.8 2.5 %collective-permute-start.7 = (f32[16,256]{1,0:T(8,128)S(1)}, f32[16,256]{1,0:T(8,128)S(1)}, u32[]{:S(2)}, u32[]{:S(2)}) collective-permute-start(f32[16,256]{1,0:T(8,128)S(1)} %router_sum.1), channel_id=1, source_target_pairs={{0,1},{1,0},{2,3},{3,2},{4,5},{5,4},{6,7},{7,6},{8,9},{9,8},{10,11... | collective-permute-start | bytes 49160 | tf_op jit(solution)/shard_map/ppermute | solution.py:419
  99.3 3.8 %mix.1 = (bf16[1024,1280]{1,0:T(8,128)(2,1)}, bf16[1024,1280]{1,0:T(8,128)(2,1)}) custom-call(bf16[96,1024]{1,0:T(8,128)(2,1)S(1)} %copy-done.7, bf16[32,1280]{1,0:T(8,128)(2,1)S(1)} %copy-done.11, bf16[32,1280]{1,0:T(8,128)(2,1)S(1)} %copy-done.13, bf16[1280,32]{1,0:T(8,128)(2,1)S(1)} %copy.12.router_ref), custom_call_target="tpu_custom_call" | custom-call | flops 1006632960 | bytes 5242880 | tf_op jit(solution)/shard_map/mix/pallas_call | solution.py:421
  103.0 0.0 collective-permute-done.7
  103.1 0.6 reshape.21
  (23 shorter events, 0.1 us)
Async XLA Ops:
  1.7 1.7 %copy-start = (bf16[1,1024,1280]{2,1,0:T(8,128)(2,1)S(1)}, bf16[1,1024,1280]{2,1,0:T(8,128)(2,1)}, u32[]{:S(2)}) copy-start(bf16[1,1024,1280]{2,1,0:T(8,128)(2,1)} %param.5) | copy-start | bytes 7864324
  3.5 1.7 %copy-start.2 = (bf16[1,1024,1280]{2,1,0:T(8,128)(2,1)S(1)}, bf16[1,1024,1280]{2,1,0:T(8,128)(2,1)}, u32[]{:S(2)}) copy-start(bf16[1,1024,1280]{2,1,0:T(8,128)(2,1)} %param.9) | copy-start | bytes 7864324
  5.2 36.8 %copy-start.4 = (bf16[2,1280,640]{2,1,0:T(8,128)(2,1)S(1)}, bf16[2,1280,640]{2,1,0:T(8,128)(2,1)}, u32[]{:S(2)}) copy-start(bf16[2,1280,640]{2,1,0:T(8,128)(2,1)} %w_in_ref.1) | copy-start | bytes 9830404
  5.2 36.9 %copy-start.5 = (bf16[2,640,1280]{2,1,0:T(8,128)(2,1)S(1)}, bf16[2,640,1280]{2,1,0:T(8,128)(2,1)}, u32[]{:S(2)}) copy-start(bf16[2,640,1280]{2,1,0:T(8,128)(2,1)} %w_out_ref.1) | copy-start | bytes 9830404
  10.3 5.7 %collective-permute-start = (bf16[16,1408]{1,0:T(8,128)(2,1)S(1)}, bf16[16,1408]{1,0:T(8,128)(2,1)S(1)}, u32[]{:S(2)}, u32[]{:S(2)}) collective-permute-start(bf16[16,1408]{1,0:T(8,128)(2,1)S(1)} %get-tuple-element.29), channel_id=1, source_target_pairs={{0,16},{16,32},{32,48},{48,0},{1,17},{17,33},{33,49},{49,1},{2,18}... | collective-permute-start | bytes 135176 | tf_op jit(solution)/shard_map/ppermute | solution.py:304
  12.4 4.4 %collective-permute-start.1 = (bf16[16,1408]{1,0:T(8,128)(2,1)S(1)}, bf16[16,1408]{1,0:T(8,128)(2,1)S(1)}, u32[]{:S(2)}, u32[]{:S(2)}) collective-permute-start(bf16[16,1408]{1,0:T(8,128)(2,1)S(1)} %get-tuple-element.30), channel_id=1, source_target_pairs={{0,32},{16,48},{32,0},{48,16},{1,33},{17,49},{33,1},{49,17},{2,34}... | collective-permute-start | bytes 135176 | tf_op jit(solution)/shard_map/ppermute | solution.py:304
  14.9 3.2 %collective-permute-start.2 = (bf16[16,1408]{1,0:T(8,128)(2,1)S(1)}, bf16[16,1408]{1,0:T(8,128)(2,1)S(1)}, u32[]{:S(2)}, u32[]{:S(2)}) collective-permute-start(bf16[16,1408]{1,0:T(8,128)(2,1)S(1)} %get-tuple-element.31), channel_id=1, source_target_pairs={{0,48},{16,0},{32,16},{48,32},{1,49},{17,1},{33,17},{49,33},{2,50}... | collective-permute-start | bytes 135176 | tf_op jit(solution)/shard_map/ppermute | solution.py:304
  42.1 30.1 %copy-start.1 = (bf16[1,1024,1280]{2,1,0:T(8,128)(2,1)S(1)}, bf16[1,1024,1280]{2,1,0:T(8,128)(2,1)}, u32[]{:S(2)}) copy-start(bf16[1,1024,1280]{2,1,0:T(8,128)(2,1)} %param.5) | copy-start | bytes 7864324
  44.9 0.6 copy-start.8
  45.5 0.6 copy-start.14
  46.1 0.6 copy-start.16
  46.8 4.5 %collective-permute-start.3 = (bf16[16,1280]{1,0:T(8,128)(2,1)S(1)}, bf16[16,1280]{1,0:T(8,128)(2,1)S(1)}, u32[]{:S(2)}, u32[]{:S(2)}) collective-permute-start(bf16[16,1280]{1,0:T(8,128)(2,1)S(1)} %get-tuple-element.33), channel_id=1, source_target_pairs={{0,16},{16,32},{32,48},{48,0},{1,17},{17,33},{33,49},{49,1},{2,18}... | collective-permute-start | bytes 122888 | tf_op jit(solution)/shard_map/ppermute | solution.py:304
  46.8 4.5 %collective-permute-start.4 = (bf16[16,1280]{1,0:T(8,128)(2,1)S(1)}, bf16[16,1280]{1,0:T(8,128)(2,1)S(1)}, u32[]{:S(2)}, u32[]{:S(2)}) collective-permute-start(bf16[16,1280]{1,0:T(8,128)(2,1)S(1)} %get-tuple-element.34), channel_id=1, source_target_pairs={{0,32},{16,48},{32,0},{48,16},{1,33},{17,49},{33,1},{49,17},{2,34}... | collective-permute-start | bytes 122888 | tf_op jit(solution)/shard_map/ppermute | solution.py:304
  48.5 3.6 %collective-permute-start.5 = (bf16[16,1280]{1,0:T(8,128)(2,1)S(1)}, bf16[16,1280]{1,0:T(8,128)(2,1)S(1)}, u32[]{:S(2)}, u32[]{:S(2)}) collective-permute-start(bf16[16,1280]{1,0:T(8,128)(2,1)S(1)} %get-tuple-element.35), channel_id=1, source_target_pairs={{0,48},{16,0},{32,16},{48,32},{1,49},{17,1},{33,17},{49,33},{2,50}... | collective-permute-start | bytes 122888 | tf_op jit(solution)/shard_map/ppermute | solution.py:304
  53.1 19.1 %all-to-all-start.1 = ((bf16[128,2,768]{2,1,0:T(2,128)(2,1)}), bf16[128,2,768]{2,1,0:T(2,128)(2,1)S(1)}, u32[]{:S(2)}, u32[]{:S(2)}) async-start(bf16[128,2,768]{2,1,0:T(2,128)(2,1)} %second_sum.1), calls=%async_computation.1 | async-start | bytes 786432 | tf_op jit(solution)/shard_map/all_to_all | solution.py:373
  72.2 1.7 %copy-start.3 = (bf16[1,1024,1280]{2,1,0:T(8,128)(2,1)S(1)}, bf16[1,1024,1280]{2,1,0:T(8,128)(2,1)}, u32[]{:S(2)}) copy-start(bf16[1,1024,1280]{2,1,0:T(8,128)(2,1)} %param.9) | copy-start | bytes 7864324
  76.0 0.7 copy-start.6
  76.7 0.6 copy-start.10
  77.4 0.6 copy-start.12
  78.0 21.3 %copy-start.7 = (bf16[96,1024]{1,0:T(8,128)(2,1)S(1)}, bf16[96,1024]{1,0:T(8,128)(2,1)}, u32[]{:S(2)}) copy-start(bf16[96,1024]{1,0:T(8,128)(2,1)} %copy-done.6) | copy-start | bytes 589828
  78.0 21.3 %copy-start.11 = (bf16[32,1280]{1,0:T(8,128)(2,1)S(1)}, bf16[32,1280]{1,0:T(8,128)(2,1)}, u32[]{:S(2)}) copy-start(bf16[32,1280]{1,0:T(8,128)(2,1)} %copy-done.10) | copy-start | bytes 245764
  78.0 21.3 %copy-start.13 = (bf16[32,1280]{1,0:T(8,128)(2,1)S(1)}, bf16[32,1280]{1,0:T(8,128)(2,1)}, u32[]{:S(2)}) copy-start(bf16[32,1280]{1,0:T(8,128)(2,1)} %copy-done.12) | copy-start | bytes 245764
  78.0 1.6 %collective-permute-start.6 = (f32[16,1280]{1,0:T(8,128)S(1)}, f32[16,1280]{1,0:T(8,128)S(1)}, u32[]{:S(2)}, u32[]{:S(2)}) collective-permute-start(f32[16,1280]{1,0:T(8,128)S(1)} %get-tuple-element.45), channel_id=1, source_target_pairs={{0,1},{1,0},{2,3},{3,2},{4,5},{5,4},{6,7},{7,6},{8,9},{9,8},{10,11... | collective-permute-start | bytes 245768 | tf_op jit(solution)/shard_map/ppermute | solution.py:401
  80.5 16.1 %all-to-all-start.2 = ((bf16[64,16,256]{2,1,0:T(8,128)(2,1)}), bf16[64,16,256]{2,1,0:T(8,128)(2,1)S(1)}, u32[]{:S(2)}, u32[]{:S(2)}) async-start(bf16[64,16,256]{2,1,0:T(8,128)(2,1)} %router_split.1), calls=%async_computation.2 | async-start | bytes 1048576 | tf_op jit(solution)/shard_map/all_to_all | solution.py:410
  85.5 0.9 copy-start.9
  86.4 0.8 copy-start.15
  87.2 0.8 copy-start.17
  96.8 6.3 %collective-permute-start.7 = (f32[16,256]{1,0:T(8,128)S(1)}, f32[16,256]{1,0:T(8,128)S(1)}, u32[]{:S(2)}, u32[]{:S(2)}) collective-permute-start(f32[16,256]{1,0:T(8,128)S(1)} %router_sum.1), channel_id=1, source_target_pairs={{0,1},{1,0},{2,3},{3,2},{4,5},{5,4},{6,7},{7,6},{8,9},{9,8},{10,11... | collective-permute-start | bytes 49160 | tf_op jit(solution)/shard_map/ppermute | solution.py:419

commit v3 on v2

v3 whole, which is shorter than its diff:
```python
import math

import jax
import jax.numpy as jnp
from jax import lax
from jax.experimental import pallas as pl
from jax.experimental.pallas import tpu as pltpu
from jax.sharding import Mesh, PartitionSpec as P

bf16 = jnp.bfloat16
f32 = jnp.float32
ALL = ("yh", "x", "z", "yl", "core")
SEQ = ("yh", "x")
EXP = ("z", "yl", "core")
CHIPS = ("yh", "x", "z", "yl")
LANES = 128
CHUNKS = 4
MIB = 1024 * 1024

VMEM = pl.BlockSpec(memory_space=pltpu.VMEM)
SMEM = pl.BlockSpec(memory_space=pltpu.SMEM)
HBM = pl.BlockSpec(memory_space=pltpu.HBM)


def nn(a, b):
    return jnp.dot(a, b, preferred_element_type=f32)


def nt(a, b):
    return lax.dot_general(a, b, (((1,), (1,)), ((), ())), preferred_element_type=f32)


def tn(a, b):
    return lax.dot_general(a, b, (((0,), (0,)), ((), ())), preferred_element_type=f32)


def shape(dims, dtype):
    return jax.ShapeDtypeStruct(dims, dtype)


def cost(flops, moved):
    return pl.CostEstimate(flops=flops, bytes_accessed=moved, transcendentals=0)


def pieces(value):
    high = value.astype(bf16).astype(f32)
    rest = value - high
    middle = rest.astype(bf16).astype(f32)
    return high, middle, rest - middle


def in_lanes(columns):
    rows = columns[0].shape[0]
    lane = lax.broadcasted_iota(jnp.int32, (rows, LANES), 1)
    result = jnp.zeros((rows, LANES), f32)
    for place, column in enumerate(columns):
        result = jnp.where(lane == place, column, result)
    return result


def from_lanes(block, first):
    lane = lax.broadcasted_iota(jnp.int32, block.shape, 1)
    kept = jnp.where((lane >= first) & (lane < first + 3), block, 0.0)
    return jnp.sum(kept, axis=1, keepdims=True)


def log_sum_exp(values):
    top = values[0]
    for value in values[1:]:
        top = jnp.maximum(top, value)
    total = jnp.exp(values[0] - top)
    for value in values[1:]:
        total = total + jnp.exp(value - top)
    return top + jnp.log(total)


def normal(value):
    return 0.5 * (1.0 + lax.erf(value * (1.0 / math.sqrt(2.0))))


def slot_order(owners, held):
    slots = owners * held
    row = lax.broadcasted_iota(jnp.int32, (slots, slots), 0)
    column = lax.broadcasted_iota(jnp.int32, (slots, slots), 1)
    return (column == (row % owners) * held + row // owners).astype(bf16)


def router_rows(router_ref, owners, held):
    return nn(slot_order(owners, held), router_ref[...]).astype(bf16)


def fetches(sources, targets, sems):
    copies = []
    for source, target in zip(sources, targets):
        chunk = source.shape[0] // CHUNKS
        for part in range(CHUNKS):
            rows = pl.ds(part * chunk, chunk)
            copies.append(
                pltpu.make_async_copy(
                    source.at[rows, :], target.at[rows, :], sems.at[len(copies)]
                )
            )
    for copy in copies:
        copy.start()
    return copies


def slot_softmax(logits):
    top = jnp.max(logits, axis=0, keepdims=True)
    raw = jnp.exp(logits - top)
    return raw / jnp.sum(raw, axis=0, keepdims=True)


def first_kernel(
    place_ref, tok_ref, router_ref, grad_ref, out0, out1, out2, out3, logits_ref, tok, grad,
    held_rows, sems,
):
    length, width = tok_ref.shape
    slots = router_ref.shape[0]
    owners = out0.shape[0]
    held = slots // owners
    chunk = length // CHUNKS
    copies = fetches((tok_ref, grad_ref), (tok, grad), sems)
    table = router_rows(router_ref, owners, held)
    for part in range(CHUNKS):
        copies[part].wait()
        rows = pl.ds(part * chunk, chunk)
        logits_ref[:, rows] = nt(table, tok[rows, :])
    logits = logits_ref[...]
    top = jnp.max(logits, axis=1, keepdims=True)
    raw = jnp.exp(logits - top)
    total = jnp.sum(raw, axis=1, keepdims=True)
    local_slot = nn(raw.astype(bf16), tok[...]) / total
    lse = top + jnp.log(total)
    probs = slot_softmax(logits).astype(bf16)
    for copy in copies[CHUNKS:]:
        copy.wait()
    local_grad = nn(probs, grad[...])
    columns = []
    for place in range(held):
        columns += pieces(lse[place * owners : (place + 1) * owners])
    extra = in_lanes(columns).astype(bf16)
    for place in range(held):
        for array, value in enumerate((local_slot, local_grad)):
            quarter = place * 2 + array
            rows = value[place * owners : (place + 1) * owners]
            held_rows[quarter, :, :width] = rows.astype(bf16)
            held_rows[quarter, :, width:] = extra
    x = place_ref[0] % 4
    for turn, out in enumerate((out0, out1, out2, out3)):
        out[...] = held_rows[(x + turn) % 4]


def write_rows(out_ref, row, extra):
    owners, width = row.shape
    half = width // 2
    halves = [
        jnp.concatenate([row[:, :half], extra], axis=1),
        jnp.concatenate([row[:, half:], extra], axis=1),
    ]
    both = jnp.stack(halves, axis=1).astype(bf16)
    for member in range(out_ref.shape[0] // owners):
        out_ref[member * owners : (member + 1) * owners] = both


def read_rows(got_ref, member, owners):
    first = member * owners
    half = got_ref.shape[2] - LANES
    left = got_ref[first : first + owners, 0, :].astype(f32)
    right = got_ref[first : first + owners, 1, :].astype(f32)
    return jnp.concatenate([left[:, :half], right[:, :half]], axis=1), left[:, half:]


def first_sum_kernel(place_ref, in0, in1, in2, in3, out_ref):
    width = in0.shape[1] - LANES
    x = place_ref[0] % 4
    blocks = [ref[...].astype(f32) for ref in (in0, in1, in2, in3)]
    lses = []
    for block in blocks:
        extra = block[:, width:]
        lses.append(jnp.where(x // 2 == 0, from_lanes(extra, 0), from_lanes(extra, 3)))
    lse = log_sum_exp(lses)
    row = None
    for block, part in zip(blocks, lses):
        scale = jnp.where(x % 2 == 0, jnp.exp(part - lse), 1.0)
        term = block[:, :width] * scale
        row = term if row is None else row + term
    write_rows(out_ref, row, in_lanes(pieces(lse)))


def expert_kernel(
    place_ref, got_ref, w_in_ref, w_out_ref,
    out0, out1, out2, out3, own_slot_ref, own_lse_ref, rows_kept, units_kept,
    held_rows, held_lse,
):
    held = w_in_ref.shape[0]
    owners = out0.shape[0]
    for place in range(held):
        rows, lses = [], []
        for y in range(2):
            data, extra = read_rows(got_ref, y * 4 + place * 2, owners)
            rows.append(data)
            lses.append(from_lanes(extra, 0))
        lse = log_sum_exp(lses)
        slot = (
            rows[0] * jnp.exp(lses[0] - lse) + rows[1] * jnp.exp(lses[1] - lse)
        ).astype(bf16)
        grads = [read_rows(got_ref, y * 4 + place * 2 + 1, owners)[0] for y in range(2)]
        slot_grad = (grads[0] + grads[1]).astype(bf16)
        rows_kept[place * 2] = slot
        rows_kept[place * 2 + 1] = slot_grad
        held_lse[place] = in_lanes(pieces(lse))
        activation = nn(slot, w_in_ref[place])
        hidden_grad = nt(slot_grad, w_out_ref[place])
        cumulative = normal(activation)
        density = jnp.exp(-0.5 * activation * activation) * (1.0 / math.sqrt(2.0 * math.pi))
        hidden = (activation * cumulative).astype(bf16)
        pre = (hidden_grad * (cumulative + activation * density)).astype(bf16)
        units_kept[place * 2] = hidden
        units_kept[place * 2 + 1] = pre
        held_rows[place * 2] = nn(hidden, w_out_ref[place]).astype(bf16)
        held_rows[place * 2 + 1] = nt(pre, w_in_ref[place]).astype(bf16)
    x = place_ref[0] % 4
    for turn, out in enumerate((out0, out1, out2, out3)):
        out[...] = held_rows[(x + turn) % 4]
    own_slot_ref[...] = rows_kept[x // 2 * 2]
    own_lse_ref[...] = held_lse[x // 2]


def weight_kernel(rows_ref, units_ref, w_in_ref, w_out_ref):
    w_out_ref[0] = tn(units_ref[0], rows_ref[1]).astype(bf16)
    w_in_ref[0] = tn(rows_ref[0], units_ref[1]).astype(bf16)


def second_sum_kernel(in0, in1, in2, in3, slot_ref, lse_ref, out_ref):
    row = in0[...].astype(f32) + in1[...].astype(f32) + in2[...].astype(f32) + in3[...].astype(f32)
    row = row.astype(bf16).astype(f32)
    shift = jnp.sum(slot_ref[...].astype(f32) * row, axis=1, keepdims=True)
    columns = in_lanes((shift * 0.0,) * 3 + pieces(shift))
    write_rows(out_ref, row, lse_ref[...] + columns)


def token_kernel(
    place_ref, got_ref, logits_ref, tok_ref, grad_ref,
    mix, rows, keep_ref, give_ref, sums,
):
    slots, length = logits_ref.shape
    owners = 16
    held = slots // owners
    lses, shifts = [], []
    for place in range(held):
        first, extra = read_rows(got_ref, place * 2, owners)
        second, _ = read_rows(got_ref, 4 + place * 2, owners)
        rows[0, place * owners : (place + 1) * owners] = (first + second).astype(bf16)
        lses.append(from_lanes(extra, 0))
        first, extra_a = read_rows(got_ref, place * 2 + 1, owners)
        second, extra_b = read_rows(got_ref, 4 + place * 2 + 1, owners)
        rows[1, place * owners : (place + 1) * owners] = (first + second).astype(bf16)
        shifts.append(from_lanes(extra_a, 3) + from_lanes(extra_b, 3))
    lse = jnp.concatenate(lses, axis=0)
    shift = jnp.concatenate(shifts, axis=0)
    logits = logits_ref[...]
    probs = slot_softmax(logits)
    share = jnp.exp(logits - lse)
    mix[0] = probs.astype(bf16)
    mix[2] = share.astype(bf16)
    grad_probs = nt(rows[0], grad_ref[...])
    comb = probs * (grad_probs - jnp.sum(probs * grad_probs, axis=0, keepdims=True))
    inner = nt(rows[1], tok_ref[...])
    logit_grad = (comb + share * (inner - shift)).astype(bf16)
    mix[1] = logit_grad
    natural = tn(slot_order(owners, held), logit_grad).astype(bf16)
    total = nn(natural, tok_ref[...])
    half = slots // 2
    sums[0] = total[:half]
    sums[1] = total[half:]
    core = place_ref[0] // 4
    keep_ref[...] = sums[core]
    give_ref[...] = sums[1 - core]


def router_split_kernel(keep_ref, got_ref, out_ref):
    share = keep_ref.shape[1] // 8
    rows = out_ref.shape[1]
    total = keep_ref[...] + got_ref[...]
    for member in range(8):
        part = total[:, member * share : (member + 1) * share]
        packed = jnp.concatenate(
            [part[group * rows : (group + 1) * rows] for group in range(part.shape[0] // rows)],
            axis=1,
        ).astype(bf16)
        for copy in range(8):
            out_ref[member * 8 + copy] = packed


def router_sum_kernel(got_ref, out_ref):
    share = out_ref.shape[1]
    rows = got_ref.shape[1]
    total = got_ref[0].astype(f32)
    for member in range(1, got_ref.shape[0]):
        total = total + got_ref[member].astype(f32)
    for group in range(out_ref.shape[0] // rows):
        out_ref[group * rows : (group + 1) * rows] = total[:, group * share : (group + 1) * share]


def router_join_kernel(place_ref, half_ref, other_ref, out_ref):
    half = half_ref.shape[0]
    first = place_ref[0] // 4 == 0
    own, other = half_ref[...], other_ref[...]
    out_ref[:half] = jnp.where(first, own, other)
    out_ref[half:] = jnp.where(first, other, own)


def mix_kernel(mix_ref, rows_ref, router_ref, mixed_ref, grad_ref):
    slots = rows_ref.shape[1]
    mixed_ref[...] = tn(mix_ref[0], rows_ref[0]).astype(bf16)
    table = jnp.concatenate([router_rows(router_ref, 16, slots // 16), rows_ref[1]], axis=0)
    both = jnp.concatenate([mix_ref[1], mix_ref[2]], axis=0)
    grad_ref[...] = tn(both, table).astype(bf16)


def around_x(arrays):
    got = [arrays[0]]
    for turn in range(1, 4):
        pairs = [(place, (place + turn) % 4) for place in range(4)]
        got.append(lax.ppermute(arrays[turn], "x", pairs))
    return got


def params(mib):
    return pltpu.CompilerParams(vmem_limit_bytes=mib * MIB)


def per_device(tokens, router, w_in, w_out, grad_out):
    place = (lax.axis_index("x") + 4 * lax.axis_index("core")).astype(jnp.int32).reshape(1)
    tok = tokens[0]
    grad = grad_out[0]
    length, width = tok.shape
    router_t = router.T
    slots = router.shape[1]
    held, _, units = w_in.shape
    owners = slots // held
    wide = width + LANES
    sent = shape((8 * owners, 2, width // 2 + LANES), bf16)
    token_flops = 2 * length * width * slots
    expert_flops = 2 * held * owners * width * units

    *send, logits, tok_held, grad_held = pl.pallas_call(
        first_kernel,
        out_shape=[shape((owners, wide), bf16)] * 4
        + [shape((slots, length), f32)]
        + [shape((length, width), bf16)] * 2,
        in_specs=[SMEM, HBM, VMEM, HBM],
        out_specs=[VMEM] * 7,
        scratch_shapes=[
            pltpu.VMEM((4, owners, wide), bf16),
            pltpu.SemaphoreType.DMA((2 * CHUNKS,)),
        ],
        compiler_params=params(48),
        cost_estimate=cost(3 * token_flops, 4 * length * width),
        name="first",
    )(place, tok, router_t, grad)
    got = around_x(send)
    send = pl.pallas_call(
        first_sum_kernel,
        out_shape=sent,
        in_specs=[SMEM] + [VMEM] * 4,
        out_specs=VMEM,
        compiler_params=params(8),
        name="first_sum",
    )(place, *got)
    got = lax.all_to_all(send, ALL, 0, 0, tiled=True)
    *send, own_slot, own_lse, rows, units_held = pl.pallas_call(
        expert_kernel,
        out_shape=[shape((owners, width), bf16)] * 5
        + [shape((owners, LANES), f32)]
        + [shape((2 * held, owners, width), bf16), shape((2 * held, owners, units), bf16)],
        in_specs=[SMEM] + [VMEM] * 3,
        out_specs=[VMEM] * 8,
        scratch_shapes=[
            pltpu.VMEM((4, owners, width), bf16),
            pltpu.VMEM((held, owners, LANES), f32),
        ],
        compiler_params=params(8),
        cost_estimate=cost(4 * expert_flops, 4 * held * width * units),
        name="experts",
    )(place, got, w_in, w_out)
    got = around_x(send)
    send = pl.pallas_call(
        second_sum_kernel,
        out_shape=sent,
        in_specs=[VMEM] * 6,
        out_specs=VMEM,
        compiler_params=params(8),
        name="second_sum",
    )(*got, own_slot, own_lse)
    got = lax.all_to_all(send, ALL, 0, 0, tiled=True)
    mix, backs, keep, give = pl.pallas_call(
        token_kernel,
        out_shape=[shape((3, slots, length), bf16), shape((2, slots, width), bf16)]
        + [shape((slots // 2, width), f32)] * 2,
        in_specs=[SMEM] + [VMEM] * 4,
        out_specs=[VMEM] * 4,
        scratch_shapes=[pltpu.VMEM((2, slots // 2, width), f32)],
        compiler_params=params(8),
        cost_estimate=cost(3 * token_flops, 4 * length * width),
        name="tokens",
    )(place, got, logits, tok_held, grad_held)
    swap = [(0, 1), (1, 0)]
    got = lax.ppermute(give, "core", swap)
    share = width // 8
    send = pl.pallas_call(
        router_split_kernel,
        out_shape=shape((64, 4, 4 * share), bf16),
        in_specs=[VMEM] * 2,
        out_specs=VMEM,
        compiler_params=params(8),
        name="router_split",
    )(keep, got)
    send, rows, units_held, mix, backs = lax.optimization_barrier(
        (send, rows, units_held, mix, backs)
    )
    got = lax.all_to_all(send, CHIPS, 0, 0, tiled=True)
    grad_w_in, grad_w_out = pl.pallas_call(
        weight_kernel,
        grid=(held,),
        out_shape=[shape((held, width, units), bf16), shape((held, units, width), bf16)],
        in_specs=[
            pl.BlockSpec((2, owners, width), lambda k: (k, 0, 0)),
            pl.BlockSpec((2, owners, units), lambda k: (k, 0, 0)),
        ],
        out_specs=[
            pl.BlockSpec((1, width, units), lambda k: (k, 0, 0)),
            pl.BlockSpec((1, units, width), lambda k: (k, 0, 0)),
        ],
        compiler_params=params(8),
        cost_estimate=cost(150 * expert_flops, 4 * held * width * units),
        name="weights",
    )(rows, units_held)
    chunk = length // 4
    mixed, grad_tokens = pl.pallas_call(
        mix_kernel,
        grid=(4,),
        out_shape=[shape((length, width), bf16)] * 2,
        in_specs=[
            pl.BlockSpec((3, slots, chunk), lambda i: (0, 0, i)),
            pl.BlockSpec((2, slots, width), lambda i: (0, 0, 0)),
            pl.BlockSpec((slots, width), lambda i: (0, 0)),
        ],
        out_specs=[pl.BlockSpec((chunk, width), lambda i: (i, 0))] * 2,
        compiler_params=params(8),
        cost_estimate=cost(60 * token_flops, 4 * length * width),
        name="mix",
    )(mix, backs, router_t)
    got, mixed, grad_tokens, grad_w_in, grad_w_out = lax.optimization_barrier(
        (got, mixed, grad_tokens, grad_w_in, grad_w_out)
    )
    half = pl.pallas_call(
        router_sum_kernel,
        out_shape=shape((slots // 2, share), f32),
        in_specs=[VMEM],
        out_specs=VMEM,
        compiler_params=params(8),
        name="router_sum",
    )(got)
    other = lax.ppermute(half, "core", swap)
    grad_router = pl.pallas_call(
        router_join_kernel,
        out_shape=shape((slots, share), f32),
        in_specs=[SMEM] + [VMEM] * 2,
        out_specs=VMEM,
        compiler_params=params(8),
        name="router_join",
    )(place, half, other)
    return (mixed[None], grad_tokens[None], grad_router.T, grad_w_in, grad_w_out)


def solution(mesh):
    fine = Mesh(mesh.devices.reshape(2, 4, 4, 2, 2), ALL)
    in_specs = (
        P(EXP, SEQ, None),
        P(),
        P(EXP, None, SEQ),
        P(EXP, SEQ, None),
        P(EXP, SEQ, None),
    )
    out_specs = (
        P(EXP, SEQ, None),
        P(EXP, SEQ, None),
        P(SEQ, None),
        P(EXP, None, SEQ),
        P(EXP, SEQ, None),
    )
    return jax.shard_map(
        per_device, mesh=fine, in_specs=in_specs, out_specs=out_specs, check_vma=False
    )
```

time: 104 us -> 88.5 us (0.85)
  blocking collectives: 23.8 us -> 42.7 us
  waiting for transfers between devices: 22.4 us -> 7.81 us
  local copies, waits for them, and re-layouts: 13.2 us -> 0.9 us
  starting transfers between devices: 24.1 us -> 17.3 us
    all_to_all x1 -> x2, blocking collectives: 23.8 us -> 42.7 us  [per_device(): got = lax.all_to_all(send, ALL, 0, 0, tiled=True)]
    all_to_all x1 -> x0, waiting for transfers between devices: 12.2 us -> none  [per_device(): got = lax.all_to_all(send, ALL, 0, 0, tiled=True)]
    unnamed x37 -> x8, local copies, waits for them, and re-layouts: 12.6 us -> 0.9 us
    all_to_all x1 -> x0, starting transfers between devices: 6.85 us -> none  [per_device(): got = lax.all_to_all(send, ALL, 0, 0, tiled=True)]
    all_to_all x1, waiting for transfers between devices: 5.2 us -> 2.03 us  [per_device(): got = lax.all_to_all(send, CHIPS, 0, 0, tiled=True)]
    pallas_call x4 -> x5, Pallas kernels: 4.1 us -> 4.09 us  [the longest x1 2.26 us: per_device(): pl.pallas_call(token_kernel, out_shape=[shape((3, slots, length), bf16),...]
  transfers between devices with their start and end apart: 10 -> 9, of which waited for: 7 -> 8; matrix products, arithmetic and copies ran while one was open for 0% -> 0% of each run, Pallas kernels for 7% -> 8%
where the time goes in v3:
time: 88.5 us; the launch traced here: 88.3 us
  blocking collectives  42.7 us (48%)
  Pallas kernels  18.8 us (21%)
  starting transfers between devices  17.3 us (20%)
  waiting for transfers between devices  7.81 us (9%)
  local copies, waits for them, and re-layouts  0.9 us (1%)
    all_to_all x2, blocking collectives, per_device(): got = lax.all_to_all(send, ALL, 0, 0, tiled=True)  42.7 us
    ppermute x6, starting transfers between devices, around_x(): got.append(lax.ppermute(arrays[turn], 'x', pairs))  9.16 us
    all_to_all x1, starting transfers between devices, per_device(): got = lax.all_to_all(send, CHIPS, 0, 0, tiled=True)  5.01 us
    pallas_call x1, Pallas kernels, per_device(): pl.pallas_call(first_kernel, out_shape=[shape((owners, wide), bf16)] * 4...  4.42 us
    ppermute x6, waiting for transfers between devices, around_x(): got.append(lax.ppermute(arrays[turn], 'x', pairs))  4.02 us
    pallas_call x1, Pallas kernels, per_device(): pl.pallas_call(mix_kernel, grid=(4,), out_shape=[shape((length, width), b...  3.72 us
    pallas_call x1, Pallas kernels, per_device(): pl.pallas_call(weight_kernel, grid=(held,), out_shape=[shape((held, width...  3.51 us
    pallas_call x1, Pallas kernels, per_device(): pl.pallas_call(expert_kernel, out_shape=[shape((owners, width), bf16)] *...  2.83 us
  transfers between devices with their start and end apart: 9, of which 8 were waited for; matrix products, arithmetic and copies ran while one was open for 0% of the time, Pallas kernels for 8%

profile of v3, /device:TPU:1, one launch (start us, length us, event | category | flops | bytes accessed | tf_op | source)
XLA Modules:
  0.0 88.3 jit_solution(18011489798888986053)
XLA Ops:
  0.6 0.0 copy-start.2
  0.7 0.9 copy-done.2
  1.5 0.0 copy-start
  1.5 0.0 copy-start.1
  1.5 4.4 %first.1 = (bf16[16,1408]{1,0:T(8,128)(2,1)S(1)}, bf16[16,1408]{1,0:T(8,128)(2,1)S(1)}, bf16[16,1408]{1,0:T(8,128)(2,1)S(1)}, bf16[16,1408]{1,0:T(8,128)(2,1)S(1...) custom-call(s32[1]{0:T(128)} %bitcast.place_ref, ...), custom_call_target="tpu_custom_call" | custom-call | flops 251658240 | bytes 5242880 | tf_op jit(solution)/shard_map/first/pallas_call | solution.py:348
  6.0 2.1 %collective-permute-start = (bf16[16,1408]{1,0:T(8,128)(2,1)S(1)}, bf16[16,1408]{1,0:T(8,128)(2,1)S(1)}, u32[]{:S(2)}, u32[]{:S(2)}) collective-permute-start(bf16[16,1408]{1,0:T(8,128)(2,1)S(1)} %get-tuple-element.39), channel_id=1, source_target_pairs={{0,16},{16,32},{32,48},{48,0},{1,17},{17,33},{33,49},{49,1},{2,18}... | collective-permute-start | bytes 135176 | tf_op jit(solution)/shard_map/ppermute | solution.py:326
  8.1 2.4 %collective-permute-start.1 = (bf16[16,1408]{1,0:T(8,128)(2,1)S(1)}, bf16[16,1408]{1,0:T(8,128)(2,1)S(1)}, u32[]{:S(2)}, u32[]{:S(2)}) collective-permute-start(bf16[16,1408]{1,0:T(8,128)(2,1)S(1)} %get-tuple-element.40), channel_id=1, source_target_pairs={{0,32},{16,48},{32,0},{48,16},{1,33},{17,49},{33,1},{49,17},{2,34}... | collective-permute-start | bytes 135176 | tf_op jit(solution)/shard_map/ppermute | solution.py:326
  10.5 1.2 %collective-permute-start.2 = (bf16[16,1408]{1,0:T(8,128)(2,1)S(1)}, bf16[16,1408]{1,0:T(8,128)(2,1)S(1)}, u32[]{:S(2)}, u32[]{:S(2)}) collective-permute-start(bf16[16,1408]{1,0:T(8,128)(2,1)S(1)} %get-tuple-element.41), channel_id=1, source_target_pairs={{0,48},{16,0},{32,16},{48,32},{1,49},{17,1},{33,17},{49,33},{2,50}... | collective-permute-start | bytes 135176 | tf_op jit(solution)/shard_map/ppermute | solution.py:326
  11.7 0.0 collective-permute-done.in1
  11.7 0.8 collective-permute-done.1.in2
  12.5 1.2 %collective-permute-done.2.in3 = bf16[16,1408]{1,0:T(8,128)(2,1)S(1)} collective-permute-done((bf16[16,1408]{1,0:T(8,128)(2,1)S(1)}, bf16[16,1408]{1,0:T(8,128)(2,1)S(1)}, u32[]{:S(2)}, u32[]{:S(2)}) %collective-permute-start.2) | collective-permute-done | bytes 45088 | tf_op jit(solution)/shard_map/ppermute | solution.py:326
  13.7 0.3 first_sum.1
  14.0 23.8 %all_to_all.15.got_ref = bf16[128,2,768]{2,1,0:T(2,128)(2,1)S(1)} all-to-all(bf16[128,2,768]{2,1,0:T(2,128)(2,1)S(1)} %first_sum.1), channel_id=1, replica_groups=mesh['yh'=2,'x'=4,'z'=4,'yl'=2,'core'=2] {'yh','x','z','yl','core'}, dimensions={0} | all-to-all | bytes 786432 | tf_op jit(solution)/shard_map/all_to_all | solution.py:372
  37.7 0.0 copy-done
  37.7 0.0 copy-done.1
  37.7 2.8 %experts.1 = (bf16[16,1280]{1,0:T(8,128)(2,1)S(1)}, bf16[16,1280]{1,0:T(8,128)(2,1)S(1)}, bf16[16,1280]{1,0:T(8,128)(2,1)S(1)}, bf16[16,1280]{1,0:T(8,128)(2,1)S...) custom-call(s32[1]{0:T(128)} %bitcast.place_ref, ...), custom_call_target="tpu_custom_call" | custom-call | flops 209715200 | bytes 6553600 | tf_op jit(solution)/shard_map/experts/pallas_call | solution.py:373
  40.6 0.1 collective-permute-start.3
  40.7 1.7 %collective-permute-start.4 = (bf16[16,1280]{1,0:T(8,128)(2,1)S(1)}, bf16[16,1280]{1,0:T(8,128)(2,1)S(1)}, u32[]{:S(2)}, u32[]{:S(2)}) collective-permute-start(bf16[16,1280]{1,0:T(8,128)(2,1)S(1)} %get-tuple-element.44), channel_id=1, source_target_pairs={{0,32},{16,48},{32,0},{48,16},{1,33},{17,49},{33,1},{49,17},{2,34}... | collective-permute-start | bytes 122888 | tf_op jit(solution)/shard_map/ppermute | solution.py:326
  42.4 1.7 %collective-permute-start.5 = (bf16[16,1280]{1,0:T(8,128)(2,1)S(1)}, bf16[16,1280]{1,0:T(8,128)(2,1)S(1)}, u32[]{:S(2)}, u32[]{:S(2)}) collective-permute-start(bf16[16,1280]{1,0:T(8,128)(2,1)S(1)} %get-tuple-element.45), channel_id=1, source_target_pairs={{0,48},{16,0},{32,16},{48,32},{1,49},{17,1},{33,17},{49,33},{2,50}... | collective-permute-start | bytes 122888 | tf_op jit(solution)/shard_map/ppermute | solution.py:326
  44.0 0.7 collective-permute-done.3.in1
  44.7 0.4 collective-permute-done.4.in2
  45.2 0.9 collective-permute-done.5.in3
  46.0 0.2 second_sum.1
  46.2 19.0 %all_to_all.16.got_ref = bf16[128,2,768]{2,1,0:T(2,128)(2,1)S(1)} all-to-all(bf16[128,2,768]{2,1,0:T(2,128)(2,1)S(1)} %second_sum.1), channel_id=1, replica_groups=mesh['yh'=2,'x'=4,'z'=4,'yl'=2,'core'=2] {'yh','x','z','yl','core'}, dimensions={0} | all-to-all | bytes 786432 | tf_op jit(solution)/shard_map/all_to_all | solution.py:397
  65.2 2.3 %tokens.1 = (bf16[3,32,1024]{2,1,0:T(8,128)(2,1)S(1)}, bf16[2,32,1280]{2,1,0:T(8,128)(2,1)S(1)}, f32[16,1280]{1,0:T(8,128)S(1)}, f32[16,1280]{1,0:T(8,128)S(1)}) custom-call(s32[1]{0:T(128)} %bitcast.place_ref, bf16[128,2,768]{2,1,0:T(2,128)(2,1)S(1)} %all_to_all.16.got_ref, f32[32,1024]{1,0:T(8,128)S(1)} %get-tuple-element.48.logits_ref, ...), custom_call_target="tpu_custom_call" | custom-call | flops 251658240 | bytes 5242880 | tf_op jit(solution)/shard_map/tokens/pallas_call | solution.py:398
  67.5 0.7 collective-permute-start.6
  68.2 0.9 %collective-permute-done.6.got_ref = f32[16,1280]{1,0:T(8,128)S(1)} collective-permute-done((f32[16,1280]{1,0:T(8,128)S(1)}, f32[16,1280]{1,0:T(8,128)S(1)}, u32[]{:S(2)}, u32[]{:S(2)}) %collective-permute-start.6) | collective-permute-done | bytes 81952 | tf_op jit(solution)/shard_map/ppermute | solution.py:410
  69.2 0.8 router_split.1
  70.0 5.0 %all-to-all-start.2 = ((bf16[64,4,640]{2,1,0:T(4,128)(2,1)}), bf16[64,4,640]{2,1,0:T(4,128)(2,1)S(1)}, u32[]{:S(2)}, u32[]{:S(2)}) async-start(bf16[64,4,640]{2,1,0:T(4,128)(2,1)} %router_split.1), calls=%async_computation.2 | async-start | bytes 655360 | tf_op jit(solution)/shard_map/all_to_all | solution.py:423
  75.0 0.0 copy-start.3
  75.0 3.5 %weights.1 = (bf16[2,1280,640]{2,1,0:T(8,128)(2,1)}, bf16[2,640,1280]{2,1,0:T(8,128)(2,1)}) custom-call(bf16[4,16,1280]{2,1,0:T(8,128)(2,1)S(1)} %get-tuple-element.62.rows_ref, bf16[4,16,640]{2,1,0:T(8,128)(2,1)S(1)} %get-tuple-element.63.units_ref), custom_call_target="tpu_custom_call" | custom-call | flops 7864320000 | bytes 6553600 | tf_op jit(solution)/shard_map/weights/pallas_call | solution.py:424
  78.6 0.0 copy-done.3
  78.6 3.7 %mix.1 = (bf16[1024,1280]{1,0:T(8,128)(2,1)}, bf16[1024,1280]{1,0:T(8,128)(2,1)}) custom-call(bf16[3,32,1024]{2,1,0:T(8,128)(2,1)S(1)} %get-tuple-element.58.mix_ref, bf16[2,32,1280]{2,1,0:T(8,128)(2,1)S(1)} %get-tuple-element.59.rows_ref, bf16[32,1280]{1,0:T(8,128)(2,1)S(1)} %bitcast.8), custom_call_target="tpu_custom_call" | custom-call | flops 5033164800 | bytes 5242880 | tf_op jit(solution)/shard_map/mix/pallas_call | solution.py:441
  82.3 2.0 %all-to-all-done.2.got_ref = bf16[64,4,640]{2,1,0:T(4,128)(2,1)S(1)} async-done(((bf16[64,4,640]{2,1,0:T(4,128)(2,1)}), bf16[64,4,640]{2,1,0:T(4,128)(2,1)S(1)}, u32[]{:S(2)}, u32[]{:S(2)}) %all-to-all-start.2) | async-done | bytes 327712 | tf_op jit(solution)/shard_map/all_to_all | solution.py:423
  84.3 0.2 router_sum.1.half_ref
  84.5 2.4 %collective-permute-start.7 = (f32[16,160]{1,0:T(8,128)S(1)}, f32[16,160]{1,0:T(8,128)S(1)}, u32[]{:S(2)}, u32[]{:S(2)}) collective-permute-start(f32[16,160]{1,0:T(8,128)S(1)} %router_sum.1.half_ref), channel_id=1, source_target_pairs={{0,1},{1,0},{2,3},{3,2},{4,5},{5,4},{6,7},{7,6},{8,9},{9,8},{10,11... | collective-permute-start | bytes 30728 | tf_op jit(solution)/shard_map/ppermute | solution.py:466
  86.8 0.8 collective-permute-done.7.other_ref
  87.7 0.6 router_join.1
Async XLA Ops:
  0.6 0.9 %copy-start.2 = (bf16[1280,32]{0,1:T(8,128)(2,1)S(1)}, bf16[1280,32]{0,1:T(8,128)(2,1)}, u32[]{:S(2)}) copy-start(bf16[1280,32]{0,1:T(8,128)(2,1)} %param.6) | copy-start | bytes 245764
  1.5 36.2 %copy-start = (bf16[2,1280,640]{2,1,0:T(8,128)(2,1)S(1)}, bf16[2,1280,640]{2,1,0:T(8,128)(2,1)}, u32[]{:S(2)}) copy-start(bf16[2,1280,640]{2,1,0:T(8,128)(2,1)} %w_in_ref.1) | copy-start | bytes 9830404
  1.5 36.2 %copy-start.1 = (bf16[2,640,1280]{2,1,0:T(8,128)(2,1)S(1)}, bf16[2,640,1280]{2,1,0:T(8,128)(2,1)}, u32[]{:S(2)}) copy-start(bf16[2,640,1280]{2,1,0:T(8,128)(2,1)} %w_out_ref.1) | copy-start | bytes 9830404
  6.0 5.7 %collective-permute-start = (bf16[16,1408]{1,0:T(8,128)(2,1)S(1)}, bf16[16,1408]{1,0:T(8,128)(2,1)S(1)}, u32[]{:S(2)}, u32[]{:S(2)}) collective-permute-start(bf16[16,1408]{1,0:T(8,128)(2,1)S(1)} %get-tuple-element.39), channel_id=1, source_target_pairs={{0,16},{16,32},{32,48},{48,0},{1,17},{17,33},{33,49},{49,1},{2,18}... | collective-permute-start | bytes 135176 | tf_op jit(solution)/shard_map/ppermute | solution.py:326
  8.1 4.4 %collective-permute-start.1 = (bf16[16,1408]{1,0:T(8,128)(2,1)S(1)}, bf16[16,1408]{1,0:T(8,128)(2,1)S(1)}, u32[]{:S(2)}, u32[]{:S(2)}) collective-permute-start(bf16[16,1408]{1,0:T(8,128)(2,1)S(1)} %get-tuple-element.40), channel_id=1, source_target_pairs={{0,32},{16,48},{32,0},{48,16},{1,33},{17,49},{33,1},{49,17},{2,34}... | collective-permute-start | bytes 135176 | tf_op jit(solution)/shard_map/ppermute | solution.py:326
  10.5 3.2 %collective-permute-start.2 = (bf16[16,1408]{1,0:T(8,128)(2,1)S(1)}, bf16[16,1408]{1,0:T(8,128)(2,1)S(1)}, u32[]{:S(2)}, u32[]{:S(2)}) collective-permute-start(bf16[16,1408]{1,0:T(8,128)(2,1)S(1)} %get-tuple-element.41), channel_id=1, source_target_pairs={{0,48},{16,0},{32,16},{48,32},{1,49},{17,1},{33,17},{49,33},{2,50}... | collective-permute-start | bytes 135176 | tf_op jit(solution)/shard_map/ppermute | solution.py:326
  40.6 4.1 %collective-permute-start.3 = (bf16[16,1280]{1,0:T(8,128)(2,1)S(1)}, bf16[16,1280]{1,0:T(8,128)(2,1)S(1)}, u32[]{:S(2)}, u32[]{:S(2)}) collective-permute-start(bf16[16,1280]{1,0:T(8,128)(2,1)S(1)} %get-tuple-element.43), channel_id=1, source_target_pairs={{0,16},{16,32},{32,48},{48,0},{1,17},{17,33},{33,49},{49,1},{2,18}... | collective-permute-start | bytes 122888 | tf_op jit(solution)/shard_map/ppermute | solution.py:326
  40.7 4.5 %collective-permute-start.4 = (bf16[16,1280]{1,0:T(8,128)(2,1)S(1)}, bf16[16,1280]{1,0:T(8,128)(2,1)S(1)}, u32[]{:S(2)}, u32[]{:S(2)}) collective-permute-start(bf16[16,1280]{1,0:T(8,128)(2,1)S(1)} %get-tuple-element.44), channel_id=1, source_target_pairs={{0,32},{16,48},{32,0},{48,16},{1,33},{17,49},{33,1},{49,17},{2,34}... | collective-permute-start | bytes 122888 | tf_op jit(solution)/shard_map/ppermute | solution.py:326
  42.4 3.6 %collective-permute-start.5 = (bf16[16,1280]{1,0:T(8,128)(2,1)S(1)}, bf16[16,1280]{1,0:T(8,128)(2,1)S(1)}, u32[]{:S(2)}, u32[]{:S(2)}) collective-permute-start(bf16[16,1280]{1,0:T(8,128)(2,1)S(1)} %get-tuple-element.45), channel_id=1, source_target_pairs={{0,48},{16,0},{32,16},{48,32},{1,49},{17,1},{33,17},{49,33},{2,50}... | collective-permute-start | bytes 122888 | tf_op jit(solution)/shard_map/ppermute | solution.py:326
  67.5 1.7 %collective-permute-start.6 = (f32[16,1280]{1,0:T(8,128)S(1)}, f32[16,1280]{1,0:T(8,128)S(1)}, u32[]{:S(2)}, u32[]{:S(2)}) collective-permute-start(f32[16,1280]{1,0:T(8,128)S(1)} %get-tuple-element.52), channel_id=1, source_target_pairs={{0,1},{1,0},{2,3},{3,2},{4,5},{5,4},{6,7},{7,6},{8,9},{9,8},{10,11... | collective-permute-start | bytes 245768 | tf_op jit(solution)/shard_map/ppermute | solution.py:410
  70.0 14.3 %all-to-all-start.2 = ((bf16[64,4,640]{2,1,0:T(4,128)(2,1)}), bf16[64,4,640]{2,1,0:T(4,128)(2,1)S(1)}, u32[]{:S(2)}, u32[]{:S(2)}) async-start(bf16[64,4,640]{2,1,0:T(4,128)(2,1)} %router_split.1), calls=%async_computation.2 | async-start | bytes 655360 | tf_op jit(solution)/shard_map/all_to_all | solution.py:423
  75.0 3.5 %copy-start.3 = (bf16[1280,32]{0,1:T(8,128)(2,1)S(1)}, bf16[1280,32]{0,1:T(8,128)(2,1)}, u32[]{:S(2)}) copy-start(bf16[1280,32]{0,1:T(8,128)(2,1)} %param.6) | copy-start | bytes 245764
  84.5 3.2 %collective-permute-start.7 = (f32[16,160]{1,0:T(8,128)S(1)}, f32[16,160]{1,0:T(8,128)S(1)}, u32[]{:S(2)}, u32[]{:S(2)}) collective-permute-start(f32[16,160]{1,0:T(8,128)S(1)} %router_sum.1.half_ref), channel_id=1, source_target_pairs={{0,1},{1,0},{2,3},{3,2},{4,5},{5,4},{6,7},{7,6},{8,9},{9,8},{10,11... | collective-permute-start | bytes 30728 | tf_op jit(solution)/shard_map/ppermute | solution.py:466

commit v4 on v3

--- a/solution.py
+++ b/solution.py
@@ -14,7 +14,8 @@
 EXP = ("z", "yl", "core")
 CHIPS = ("yh", "x", "z", "yl")
 LANES = 128
-CHUNKS = 4
+CHUNKS = 2
+MIX_CHUNKS = 2
 MIB = 1024 * 1024
 
 VMEM = pl.BlockSpec(memory_space=pltpu.VMEM)
@@ -227,11 +228,6 @@
     own_lse_ref[...] = held_lse[x // 2]
 
 
-def weight_kernel(rows_ref, units_ref, w_in_ref, w_out_ref):
-    w_out_ref[0] = tn(units_ref[0], rows_ref[1]).astype(bf16)
-    w_in_ref[0] = tn(rows_ref[0], units_ref[1]).astype(bf16)
-
-
 def second_sum_kernel(in0, in1, in2, in3, slot_ref, lse_ref, out_ref):
     row = in0[...].astype(f32) + in1[...].astype(f32) + in2[...].astype(f32) + in3[...].astype(f32)
     row = row.astype(bf16).astype(f32)
@@ -311,12 +307,58 @@
     out_ref[half:] = jnp.where(first, other, own)
 
 
-def mix_kernel(mix_ref, rows_ref, router_ref, mixed_ref, grad_ref):
-    slots = rows_ref.shape[1]
-    mixed_ref[...] = tn(mix_ref[0], rows_ref[0]).astype(bf16)
-    table = jnp.concatenate([router_rows(router_ref, 16, slots // 16), rows_ref[1]], axis=0)
-    both = jnp.concatenate([mix_ref[1], mix_ref[2]], axis=0)
-    grad_ref[...] = tn(both, table).astype(bf16)
+def late_kernel(
+    rows_ref, units_ref, mix_ref, back_ref, router_ref, w_in_ref, w_out_ref, mixed_ref, grad_ref,
+    w_in, w_out, mixed, grad, sems, mix_sems,
+):
+    held, width, units = w_in.shape
+    chunk = mixed.shape[0] // MIX_CHUNKS
+    slots = back_ref.shape[1]
+
+    def weight_copies(place):
+        return [
+            pltpu.make_async_copy(kept.at[place], ref.at[place], sems.at[2 * place + number])
+            for number, (kept, ref) in enumerate(((w_out, w_out_ref), (w_in, w_in_ref)))
+        ]
+
+    def weight_step(place, carry):
+        first, second = weight_copies(place)
+        w_out[place] = tn(units_ref[place * 2], rows_ref[place * 2 + 1]).astype(bf16)
+        first.start()
+        w_in[place] = tn(rows_ref[place * 2], units_ref[place * 2 + 1]).astype(bf16)
+        second.start()
+        return carry
+
+    def mix_copies(part):
+        span = pl.ds(pl.multiple_of(part * chunk, chunk), chunk)
+        return [
+            pltpu.make_async_copy(kept.at[span, :], ref.at[span, :], mix_sems.at[2 * part + number])
+            for number, (kept, ref) in enumerate(((mixed, mixed_ref), (grad, grad_ref)))
+        ]
+
+    def mix_step(part, carry):
+        first, second = mix_copies(part)
+        span = pl.ds(pl.multiple_of(part * chunk, chunk), chunk)
+        mixed[span, :] = tn(mix_ref[0, :, span], back_ref[0]).astype(bf16)
+        first.start()
+        both = jnp.concatenate([mix_ref[1, :, span], mix_ref[2, :, span]], axis=0)
+        grad[span, :] = tn(both, table).astype(bf16)
+        second.start()
+        return carry
+
+    def wait(copies):
+        def step(part, carry):
+            for copy in copies(part):
+                copy.wait()
+            return carry
+
+        return step
+
+    table = jnp.concatenate([router_rows(router_ref, slots // held, held), back_ref[1]], axis=0)
+    lax.fori_loop(0, held, weight_step, 0)
+    lax.fori_loop(0, MIX_CHUNKS, mix_step, 0)
+    lax.fori_loop(0, held, wait(weight_copies), 0)
+    lax.fori_loop(0, MIX_CHUNKS, wait(mix_copies), 0)
 
 
 def around_x(arrays):
@@ -421,37 +463,21 @@
         (send, rows, units_held, mix, backs)
     )
     got = lax.all_to_all(send, CHIPS, 0, 0, tiled=True)
-    grad_w_in, grad_w_out = pl.pallas_call(
-        weight_kernel,
-        grid=(held,),
-        out_shape=[shape((held, width, units), bf16), shape((held, units, width), bf16)],
-        in_specs=[
-            pl.BlockSpec((2, owners, width), lambda k: (k, 0, 0)),
-            pl.BlockSpec((2, owners, units), lambda k: (k, 0, 0)),
+    late_shapes = [(held, width, units), (held, units, width), (length, width), (length, width)]
+    grad_w_in, grad_w_out, mixed, grad_tokens = pl.pallas_call(
+        late_kernel,
+        out_shape=[shape(dims, bf16) for dims in late_shapes],
+        in_specs=[VMEM] * 5,
+        out_specs=[HBM] * 4,
+        scratch_shapes=[pltpu.VMEM(dims, bf16) for dims in late_shapes]
+        + [
+            pltpu.SemaphoreType.DMA((2 * held,)),
+            pltpu.SemaphoreType.DMA((2 * MIX_CHUNKS,)),
         ],
-        out_specs=[
-            pl.BlockSpec((1, width, units), lambda k: (k, 0, 0)),
-            pl.BlockSpec((1, units, width), lambda k: (k, 0, 0)),
-        ],
-        compiler_params=params(8),
-        cost_estimate=cost(150 * expert_flops, 4 * held * width * units),
-        name="weights",
-    )(rows, units_held)
-    chunk = length // 4
-    mixed, grad_tokens = pl.pallas_call(
-        mix_kernel,
-        grid=(4,),
-        out_shape=[shape((length, width), bf16)] * 2,
-        in_specs=[
-            pl.BlockSpec((3, slots, chunk), lambda i: (0, 0, i)),
-            pl.BlockSpec((2, slots, width), lambda i: (0, 0, 0)),
-            pl.BlockSpec((slots, width), lambda i: (0, 0)),
-        ],
-        out_specs=[pl.BlockSpec((chunk, width), lambda i: (i, 0))] * 2,
-        compiler_params=params(8),
-        cost_estimate=cost(60 * token_flops, 4 * length * width),
-        name="mix",
-    )(mix, backs, router_t)
+        compiler_params=params(20),
+        cost_estimate=cost(200 * expert_flops, 4 * length * width),
+        name="late",
+    )(rows, units_held, mix, backs, router_t)
     got, mixed, grad_tokens, grad_w_in, grad_w_out = lax.optimization_barrier(
         (got, mixed, grad_tokens, grad_w_in, grad_w_out)
     )

time: 88.5 us -> 87.9 us (level)
  Pallas kernels: 18.8 us -> 16.2 us
  waiting for transfers between devices: 7.81 us -> 9.76 us
    pallas_call x2 -> x1, Pallas kernels: 7.22 us -> 5.27 us  [per_device(): pl.pallas_call(late_kernel, out_shape=[shape(dims, bf16) for dims in late...]
    all_to_all x1, waiting for transfers between devices: 2.03 us -> 3.98 us  [per_device(): got = lax.all_to_all(send, CHIPS, 0, 0, tiled=True)]
  transfers between devices with their start and end apart: 9 -> 9, of which waited for: 8 -> 8; matrix products, arithmetic and copies ran while one was open for 0% -> 0% of each run, Pallas kernels for 8% -> 6%
where the time goes in v4:
time: 87.9 us; the launch traced here: 87.6 us
  blocking collectives  42.7 us (49%)
  starting transfers between devices  17.3 us (20%)
  Pallas kernels  16.2 us (18%)
  waiting for transfers between devices  9.76 us (11%)
  local copies, waits for them, and re-layouts  0.89 us (1%)
    all_to_all x2, blocking collectives, per_device(): got = lax.all_to_all(send, ALL, 0, 0, tiled=True)  42.7 us
    ppermute x6, starting transfers between devices, around_x(): got.append(lax.ppermute(arrays[turn], 'x', pairs))  9.16 us
    pallas_call x1, Pallas kernels, per_device(): pl.pallas_call(late_kernel, out_shape=[shape(dims, bf16) for dims in late...  5.27 us
    all_to_all x1, starting transfers between devices, per_device(): got = lax.all_to_all(send, CHIPS, 0, 0, tiled=True)  5.01 us
    ppermute x6, waiting for transfers between devices, around_x(): got.append(lax.ppermute(arrays[turn], 'x', pairs))  4.02 us
    all_to_all x1, waiting for transfers between devices, per_device(): got = lax.all_to_all(send, CHIPS, 0, 0, tiled=True)  3.98 us
    pallas_call x1, Pallas kernels, per_device(): pl.pallas_call(first_kernel, out_shape=[shape((owners, wide), bf16)] * 4...  3.77 us
    pallas_call x1, Pallas kernels, per_device(): pl.pallas_call(expert_kernel, out_shape=[shape((owners, width), bf16)] *...  2.83 us
  transfers between devices with their start and end apart: 9, of which 8 were waited for; matrix products, arithmetic and copies ran while one was open for 0% of the time, Pallas kernels for 6%

profile of v4, /device:TPU:1, one launch (start us, length us, event | category | flops | bytes accessed | tf_op | source)
XLA Modules:
  0.0 87.6 jit_solution(1812494837100049856)
XLA Ops:
  0.6 0.0 copy-start.2
  0.7 0.9 %copy-done.2 = bf16[1280,32]{0,1:T(8,128)(2,1)S(1)} copy-done((bf16[1280,32]{0,1:T(8,128)(2,1)S(1)}, bf16[1280,32]{0,1:T(8,128)(2,1)}, u32[]{:S(2)}) %copy-start.2) | copy-done | bytes 81944
  1.5 0.0 copy-start
  1.5 0.0 copy-start.1
  1.5 3.8 %first.1 = (bf16[16,1408]{1,0:T(8,128)(2,1)S(1)}, bf16[16,1408]{1,0:T(8,128)(2,1)S(1)}, bf16[16,1408]{1,0:T(8,128)(2,1)S(1)}, bf16[16,1408]{1,0:T(8,128)(2,1)S(1...) custom-call(s32[1]{0:T(128)} %bitcast.place_ref, ...), custom_call_target="tpu_custom_call" | custom-call | flops 251658240 | bytes 5242880 | tf_op jit(solution)/shard_map/first/pallas_call | solution.py:390
  5.3 2.1 %collective-permute-start = (bf16[16,1408]{1,0:T(8,128)(2,1)S(1)}, bf16[16,1408]{1,0:T(8,128)(2,1)S(1)}, u32[]{:S(2)}, u32[]{:S(2)}) collective-permute-start(bf16[16,1408]{1,0:T(8,128)(2,1)S(1)} %get-tuple-element.39), channel_id=1, source_target_pairs={{0,16},{16,32},{32,48},{48,0},{1,17},{17,33},{33,49},{49,1},{2,18}... | collective-permute-start | bytes 135176 | tf_op jit(solution)/shard_map/ppermute | solution.py:368
  7.4 2.4 %collective-permute-start.1 = (bf16[16,1408]{1,0:T(8,128)(2,1)S(1)}, bf16[16,1408]{1,0:T(8,128)(2,1)S(1)}, u32[]{:S(2)}, u32[]{:S(2)}) collective-permute-start(bf16[16,1408]{1,0:T(8,128)(2,1)S(1)} %get-tuple-element.40), channel_id=1, source_target_pairs={{0,32},{16,48},{32,0},{48,16},{1,33},{17,49},{33,1},{49,17},{2,34}... | collective-permute-start | bytes 135176 | tf_op jit(solution)/shard_map/ppermute | solution.py:368
  9.9 1.2 %collective-permute-start.2 = (bf16[16,1408]{1,0:T(8,128)(2,1)S(1)}, bf16[16,1408]{1,0:T(8,128)(2,1)S(1)}, u32[]{:S(2)}, u32[]{:S(2)}) collective-permute-start(bf16[16,1408]{1,0:T(8,128)(2,1)S(1)} %get-tuple-element.41), channel_id=1, source_target_pairs={{0,48},{16,0},{32,16},{48,32},{1,49},{17,1},{33,17},{49,33},{2,50}... | collective-permute-start | bytes 135176 | tf_op jit(solution)/shard_map/ppermute | solution.py:368
  11.0 0.0 collective-permute-done.in1
  11.0 0.8 collective-permute-done.1.in2
  11.8 1.2 %collective-permute-done.2.in3 = bf16[16,1408]{1,0:T(8,128)(2,1)S(1)} collective-permute-done((bf16[16,1408]{1,0:T(8,128)(2,1)S(1)}, bf16[16,1408]{1,0:T(8,128)(2,1)S(1)}, u32[]{:S(2)}, u32[]{:S(2)}) %collective-permute-start.2) | collective-permute-done | bytes 45088 | tf_op jit(solution)/shard_map/ppermute | solution.py:368
  13.1 0.3 first_sum.1
  13.3 23.8 %all_to_all.15.got_ref = bf16[128,2,768]{2,1,0:T(2,128)(2,1)S(1)} all-to-all(bf16[128,2,768]{2,1,0:T(2,128)(2,1)S(1)} %first_sum.1), channel_id=1, replica_groups=mesh['yh'=2,'x'=4,'z'=4,'yl'=2,'core'=2] {'yh','x','z','yl','core'}, dimensions={0} | all-to-all | bytes 786432 | tf_op jit(solution)/shard_map/all_to_all | solution.py:414
  37.1 0.0 copy-done
  37.1 0.0 copy-done.1
  37.1 2.8 %experts.1 = (bf16[16,1280]{1,0:T(8,128)(2,1)S(1)}, bf16[16,1280]{1,0:T(8,128)(2,1)S(1)}, bf16[16,1280]{1,0:T(8,128)(2,1)S(1)}, bf16[16,1280]{1,0:T(8,128)(2,1)S...) custom-call(s32[1]{0:T(128)} %bitcast.place_ref, ...), custom_call_target="tpu_custom_call" | custom-call | flops 209715200 | bytes 6553600 | tf_op jit(solution)/shard_map/experts/pallas_call | solution.py:415
  39.9 0.1 collective-permute-start.3
  40.0 1.7 %collective-permute-start.4 = (bf16[16,1280]{1,0:T(8,128)(2,1)S(1)}, bf16[16,1280]{1,0:T(8,128)(2,1)S(1)}, u32[]{:S(2)}, u32[]{:S(2)}) collective-permute-start(bf16[16,1280]{1,0:T(8,128)(2,1)S(1)} %get-tuple-element.44), channel_id=1, source_target_pairs={{0,32},{16,48},{32,0},{48,16},{1,33},{17,49},{33,1},{49,17},{2,34}... | collective-permute-start | bytes 122888 | tf_op jit(solution)/shard_map/ppermute | solution.py:368
  41.7 1.7 %collective-permute-start.5 = (bf16[16,1280]{1,0:T(8,128)(2,1)S(1)}, bf16[16,1280]{1,0:T(8,128)(2,1)S(1)}, u32[]{:S(2)}, u32[]{:S(2)}) collective-permute-start(bf16[16,1280]{1,0:T(8,128)(2,1)S(1)} %get-tuple-element.45), channel_id=1, source_target_pairs={{0,48},{16,0},{32,16},{48,32},{1,49},{17,1},{33,17},{49,33},{2,50}... | collective-permute-start | bytes 122888 | tf_op jit(solution)/shard_map/ppermute | solution.py:368
  43.4 0.7 collective-permute-done.3.in1
  44.1 0.4 collective-permute-done.4.in2
  44.5 0.9 collective-permute-done.5.in3
  45.4 0.2 second_sum.1
  45.6 19.0 %all_to_all.16.got_ref = bf16[128,2,768]{2,1,0:T(2,128)(2,1)S(1)} all-to-all(bf16[128,2,768]{2,1,0:T(2,128)(2,1)S(1)} %second_sum.1), channel_id=1, replica_groups=mesh['yh'=2,'x'=4,'z'=4,'yl'=2,'core'=2] {'yh','x','z','yl','core'}, dimensions={0} | all-to-all | bytes 786432 | tf_op jit(solution)/shard_map/all_to_all | solution.py:439
  64.6 0.0 copy-start.3
  64.6 2.3 %tokens.1 = (bf16[3,32,1024]{2,1,0:T(8,128)(2,1)S(1)}, bf16[2,32,1280]{2,1,0:T(8,128)(2,1)S(1)}, f32[16,1280]{1,0:T(8,128)S(1)}, f32[16,1280]{1,0:T(8,128)S(1)}) custom-call(s32[1]{0:T(128)} %bitcast.place_ref, bf16[128,2,768]{2,1,0:T(2,128)(2,1)S(1)} %all_to_all.16.got_ref, f32[32,1024]{1,0:T(8,128)S(1)} %get-tuple-element.48.logits_ref, ...), custom_call_target="tpu_custom_call" | custom-call | flops 251658240 | bytes 5242880 | tf_op jit(solution)/shard_map/tokens/pallas_call | solution.py:440
  66.8 0.7 collective-permute-start.6
  67.6 0.9 %collective-permute-done.6.got_ref = f32[16,1280]{1,0:T(8,128)S(1)} collective-permute-done((f32[16,1280]{1,0:T(8,128)S(1)}, f32[16,1280]{1,0:T(8,128)S(1)}, u32[]{:S(2)}, u32[]{:S(2)}) %collective-permute-start.6) | collective-permute-done | bytes 81952 | tf_op jit(solution)/shard_map/ppermute | solution.py:452
  68.5 0.8 router_split.1
  69.4 5.0 %all-to-all-start.2 = ((bf16[64,4,640]{2,1,0:T(4,128)(2,1)}), bf16[64,4,640]{2,1,0:T(4,128)(2,1)S(1)}, u32[]{:S(2)}, u32[]{:S(2)}) async-start(bf16[64,4,640]{2,1,0:T(4,128)(2,1)} %router_split.1), calls=%async_computation.2 | async-start | bytes 655360 | tf_op jit(solution)/shard_map/all_to_all | solution.py:465
  74.4 0.0 copy-done.3
  74.4 5.3 %late.1 = (bf16[2,1280,640]{2,1,0:T(8,128)(2,1)}, bf16[2,640,1280]{2,1,0:T(8,128)(2,1)}, bf16[1024,1280]{1,0:T(8,128)(2,1)}, bf16[1024,1280]{1,0:T(8,128)(2,1)}) custom-call(bf16[4,16,1280]{2,1,0:T(8,128)(2,1)S(1)} %get-tuple-element.58.rows_ref, bf16[4,16,640]{2,1,0:T(8,128)(2,1)S(1)} %get-tuple-element.59.units_ref, ...), custom_call_target="tpu_custom_call" | custom-call | flops 10485760000 | bytes 5242880 | tf_op jit(solution)/shard_map/late/pallas_call | solution.py:467
  79.7 4.0 %all-to-all-done.2.got_ref = bf16[64,4,640]{2,1,0:T(4,128)(2,1)S(1)} async-done(((bf16[64,4,640]{2,1,0:T(4,128)(2,1)}), bf16[64,4,640]{2,1,0:T(4,128)(2,1)S(1)}, u32[]{:S(2)}, u32[]{:S(2)}) %all-to-all-start.2) | async-done | bytes 327712 | tf_op jit(solution)/shard_map/all_to_all | solution.py:465
  83.6 0.2 router_sum.1.half_ref
  83.8 2.4 %collective-permute-start.7 = (f32[16,160]{1,0:T(8,128)S(1)}, f32[16,160]{1,0:T(8,128)S(1)}, u32[]{:S(2)}, u32[]{:S(2)}) collective-permute-start(f32[16,160]{1,0:T(8,128)S(1)} %router_sum.1.half_ref), channel_id=1, source_target_pairs={{0,1},{1,0},{2,3},{3,2},{4,5},{5,4},{6,7},{7,6},{8,9},{9,8},{10,11... | collective-permute-start | bytes 30728 | tf_op jit(solution)/shard_map/ppermute | solution.py:492
  86.1 0.8 collective-permute-done.7.other_ref
  87.0 0.6 router_join.1
Async XLA Ops:
  0.6 0.9 %copy-start.2 = (bf16[1280,32]{0,1:T(8,128)(2,1)S(1)}, bf16[1280,32]{0,1:T(8,128)(2,1)}, u32[]{:S(2)}) copy-start(bf16[1280,32]{0,1:T(8,128)(2,1)} %param.6) | copy-start | bytes 245764
  1.5 35.5 %copy-start = (bf16[2,1280,640]{2,1,0:T(8,128)(2,1)S(1)}, bf16[2,1280,640]{2,1,0:T(8,128)(2,1)}, u32[]{:S(2)}) copy-start(bf16[2,1280,640]{2,1,0:T(8,128)(2,1)} %w_in_ref.1) | copy-start | bytes 9830404
  1.5 35.5 %copy-start.1 = (bf16[2,640,1280]{2,1,0:T(8,128)(2,1)S(1)}, bf16[2,640,1280]{2,1,0:T(8,128)(2,1)}, u32[]{:S(2)}) copy-start(bf16[2,640,1280]{2,1,0:T(8,128)(2,1)} %w_out_ref.1) | copy-start | bytes 9830404
  5.3 5.7 %collective-permute-start = (bf16[16,1408]{1,0:T(8,128)(2,1)S(1)}, bf16[16,1408]{1,0:T(8,128)(2,1)S(1)}, u32[]{:S(2)}, u32[]{:S(2)}) collective-permute-start(bf16[16,1408]{1,0:T(8,128)(2,1)S(1)} %get-tuple-element.39), channel_id=1, source_target_pairs={{0,16},{16,32},{32,48},{48,0},{1,17},{17,33},{33,49},{49,1},{2,18}... | collective-permute-start | bytes 135176 | tf_op jit(solution)/shard_map/ppermute | solution.py:368
  7.4 4.4 %collective-permute-start.1 = (bf16[16,1408]{1,0:T(8,128)(2,1)S(1)}, bf16[16,1408]{1,0:T(8,128)(2,1)S(1)}, u32[]{:S(2)}, u32[]{:S(2)}) collective-permute-start(bf16[16,1408]{1,0:T(8,128)(2,1)S(1)} %get-tuple-element.40), channel_id=1, source_target_pairs={{0,32},{16,48},{32,0},{48,16},{1,33},{17,49},{33,1},{49,17},{2,34}... | collective-permute-start | bytes 135176 | tf_op jit(solution)/shard_map/ppermute | solution.py:368
  9.9 3.2 %collective-permute-start.2 = (bf16[16,1408]{1,0:T(8,128)(2,1)S(1)}, bf16[16,1408]{1,0:T(8,128)(2,1)S(1)}, u32[]{:S(2)}, u32[]{:S(2)}) collective-permute-start(bf16[16,1408]{1,0:T(8,128)(2,1)S(1)} %get-tuple-element.41), channel_id=1, source_target_pairs={{0,48},{16,0},{32,16},{48,32},{1,49},{17,1},{33,17},{49,33},{2,50}... | collective-permute-start | bytes 135176 | tf_op jit(solution)/shard_map/ppermute | solution.py:368
  39.9 4.1 %collective-permute-start.3 = (bf16[16,1280]{1,0:T(8,128)(2,1)S(1)}, bf16[16,1280]{1,0:T(8,128)(2,1)S(1)}, u32[]{:S(2)}, u32[]{:S(2)}) collective-permute-start(bf16[16,1280]{1,0:T(8,128)(2,1)S(1)} %get-tuple-element.43), channel_id=1, source_target_pairs={{0,16},{16,32},{32,48},{48,0},{1,17},{17,33},{33,49},{49,1},{2,18}... | collective-permute-start | bytes 122888 | tf_op jit(solution)/shard_map/ppermute | solution.py:368
  40.0 4.5 %collective-permute-start.4 = (bf16[16,1280]{1,0:T(8,128)(2,1)S(1)}, bf16[16,1280]{1,0:T(8,128)(2,1)S(1)}, u32[]{:S(2)}, u32[]{:S(2)}) collective-permute-start(bf16[16,1280]{1,0:T(8,128)(2,1)S(1)} %get-tuple-element.44), channel_id=1, source_target_pairs={{0,32},{16,48},{32,0},{48,16},{1,33},{17,49},{33,1},{49,17},{2,34}... | collective-permute-start | bytes 122888 | tf_op jit(solution)/shard_map/ppermute | solution.py:368
  41.7 3.6 %collective-permute-start.5 = (bf16[16,1280]{1,0:T(8,128)(2,1)S(1)}, bf16[16,1280]{1,0:T(8,128)(2,1)S(1)}, u32[]{:S(2)}, u32[]{:S(2)}) collective-permute-start(bf16[16,1280]{1,0:T(8,128)(2,1)S(1)} %get-tuple-element.45), channel_id=1, source_target_pairs={{0,48},{16,0},{32,16},{48,32},{1,49},{17,1},{33,17},{49,33},{2,50}... | collective-permute-start | bytes 122888 | tf_op jit(solution)/shard_map/ppermute | solution.py:368
  64.6 9.8 %copy-start.3 = (bf16[1280,32]{0,1:T(8,128)(2,1)S(1)}, bf16[1280,32]{0,1:T(8,128)(2,1)}, u32[]{:S(2)}) copy-start(bf16[1280,32]{0,1:T(8,128)(2,1)} %param.6) | copy-start | bytes 245764
  66.8 1.7 %collective-permute-start.6 = (f32[16,1280]{1,0:T(8,128)S(1)}, f32[16,1280]{1,0:T(8,128)S(1)}, u32[]{:S(2)}, u32[]{:S(2)}) collective-permute-start(f32[16,1280]{1,0:T(8,128)S(1)} %get-tuple-element.52), channel_id=1, source_target_pairs={{0,1},{1,0},{2,3},{3,2},{4,5},{5,4},{6,7},{7,6},{8,9},{9,8},{10,11... | collective-permute-start | bytes 245768 | tf_op jit(solution)/shard_map/ppermute | solution.py:452
  69.4 14.3 %all-to-all-start.2 = ((bf16[64,4,640]{2,1,0:T(4,128)(2,1)}), bf16[64,4,640]{2,1,0:T(4,128)(2,1)S(1)}, u32[]{:S(2)}, u32[]{:S(2)}) async-start(bf16[64,4,640]{2,1,0:T(4,128)(2,1)} %router_split.1), calls=%async_computation.2 | async-start | bytes 655360 | tf_op jit(solution)/shard_map/all_to_all | solution.py:465
  83.8 3.2 %collective-permute-start.7 = (f32[16,160]{1,0:T(8,128)S(1)}, f32[16,160]{1,0:T(8,128)S(1)}, u32[]{:S(2)}, u32[]{:S(2)}) collective-permute-start(f32[16,160]{1,0:T(8,128)S(1)} %router_sum.1.half_ref), channel_id=1, source_target_pairs={{0,1},{1,0},{2,3},{3,2},{4,5},{5,4},{6,7},{7,6},{8,9},{9,8},{10,11... | collective-permute-start | bytes 30728 | tf_op jit(solution)/shard_map/ppermute | solution.py:492

commit v5 on v4

--- a/solution.py
+++ b/solution.py
@@ -140,12 +140,12 @@
     columns = []
     for place in range(held):
         columns += pieces(lse[place * owners : (place + 1) * owners])
-    extra = in_lanes(columns).astype(bf16)
+    extra = in_lanes(columns)
     for place in range(held):
         for array, value in enumerate((local_slot, local_grad)):
             quarter = place * 2 + array
             rows = value[place * owners : (place + 1) * owners]
-            held_rows[quarter, :, :width] = rows.astype(bf16)
+            held_rows[quarter, :, :width] = rows
             held_rows[quarter, :, width:] = extra
     x = place_ref[0] % 4
     for turn, out in enumerate((out0, out1, out2, out3)):
@@ -192,7 +192,7 @@
 def expert_kernel(
     place_ref, got_ref, w_in_ref, w_out_ref,
     out0, out1, out2, out3, own_slot_ref, own_lse_ref, rows_kept, units_kept,
-    held_rows, held_lse,
+    held_rows, held_lse, held_slots,
 ):
     held = w_in_ref.shape[0]
     owners = out0.shape[0]
@@ -203,9 +203,9 @@
             rows.append(data)
             lses.append(from_lanes(extra, 0))
         lse = log_sum_exp(lses)
-        slot = (
-            rows[0] * jnp.exp(lses[0] - lse) + rows[1] * jnp.exp(lses[1] - lse)
-        ).astype(bf16)
+        slot_full = rows[0] * jnp.exp(lses[0] - lse) + rows[1] * jnp.exp(lses[1] - lse)
+        held_slots[place] = slot_full
+        slot = slot_full.astype(bf16)
         grads = [read_rows(got_ref, y * 4 + place * 2 + 1, owners)[0] for y in range(2)]
         slot_grad = (grads[0] + grads[1]).astype(bf16)
         rows_kept[place * 2] = slot
@@ -224,7 +224,7 @@
     x = place_ref[0] % 4
     for turn, out in enumerate((out0, out1, out2, out3)):
         out[...] = held_rows[(x + turn) % 4]
-    own_slot_ref[...] = rows_kept[x // 2 * 2]
+    own_slot_ref[...] = held_slots[x // 2]
     own_lse_ref[...] = held_lse[x // 2]
 
 
@@ -238,7 +238,7 @@
 
 def token_kernel(
     place_ref, got_ref, logits_ref, tok_ref, grad_ref,
-    mix, rows, keep_ref, give_ref, sums,
+    mix, rows, keep_ref, give_ref, halves, sums,
 ):
     slots, length = logits_ref.shape
     owners = 16
@@ -252,6 +252,8 @@
         first, extra_a = read_rows(got_ref, place * 2 + 1, owners)
         second, extra_b = read_rows(got_ref, 4 + place * 2 + 1, owners)
         rows[1, place * owners : (place + 1) * owners] = (first + second).astype(bf16)
+        halves[place * owners : (place + 1) * owners] = first.astype(bf16)
+        halves[slots + place * owners : slots + (place + 1) * owners] = second.astype(bf16)
         shifts.append(from_lanes(extra_a, 3) + from_lanes(extra_b, 3))
     lse = jnp.concatenate(lses, axis=0)
     shift = jnp.concatenate(shifts, axis=0)
@@ -262,7 +264,8 @@
     mix[2] = share.astype(bf16)
     grad_probs = nt(rows[0], grad_ref[...])
     comb = probs * (grad_probs - jnp.sum(probs * grad_probs, axis=0, keepdims=True))
-    inner = nt(rows[1], tok_ref[...])
+    inner = nt(halves[...], tok_ref[...])
+    inner = inner[:slots] + inner[slots:]
     logit_grad = (comb + share * (inner - shift)).astype(bf16)
     mix[1] = logit_grad
     natural = tn(slot_order(owners, held), logit_grad).astype(bf16)
@@ -389,13 +392,13 @@
 
     *send, logits, tok_held, grad_held = pl.pallas_call(
         first_kernel,
-        out_shape=[shape((owners, wide), bf16)] * 4
+        out_shape=[shape((owners, wide), f32)] * 4
         + [shape((slots, length), f32)]
         + [shape((length, width), bf16)] * 2,
         in_specs=[SMEM, HBM, VMEM, HBM],
         out_specs=[VMEM] * 7,
         scratch_shapes=[
-            pltpu.VMEM((4, owners, wide), bf16),
+            pltpu.VMEM((4, owners, wide), f32),
             pltpu.SemaphoreType.DMA((2 * CHUNKS,)),
         ],
         compiler_params=params(48),
@@ -414,14 +417,15 @@
     got = lax.all_to_all(send, ALL, 0, 0, tiled=True)
     *send, own_slot, own_lse, rows, units_held = pl.pallas_call(
         expert_kernel,
-        out_shape=[shape((owners, width), bf16)] * 5
-        + [shape((owners, LANES), f32)]
+        out_shape=[shape((owners, width), bf16)] * 4
+        + [shape((owners, width), f32), shape((owners, LANES), f32)]
         + [shape((2 * held, owners, width), bf16), shape((2 * held, owners, units), bf16)],
         in_specs=[SMEM] + [VMEM] * 3,
         out_specs=[VMEM] * 8,
         scratch_shapes=[
             pltpu.VMEM((4, owners, width), bf16),
             pltpu.VMEM((held, owners, LANES), f32),
+            pltpu.VMEM((held, owners, width), f32),
         ],
         compiler_params=params(8),
         cost_estimate=cost(4 * expert_flops, 4 * held * width * units),
@@ -443,7 +447,10 @@
         + [shape((slots // 2, width), f32)] * 2,
         in_specs=[SMEM] + [VMEM] * 4,
         out_specs=[VMEM] * 4,
-        scratch_shapes=[pltpu.VMEM((2, slots // 2, width), f32)],
+        scratch_shapes=[
+            pltpu.VMEM((2 * slots, width), bf16),
+            pltpu.VMEM((2, slots // 2, width), f32),
+        ],
         compiler_params=params(8),
         cost_estimate=cost(3 * token_flops, 4 * length * width),
         name="tokens",

time: 87.9 us -> 88.4 us (level)
  waiting for transfers between devices: 9.76 us -> 10.7 us
    ppermute x6, waiting for transfers between devices: 4.02 us -> 4.93 us  [around_x(): got.append(lax.ppermute(arrays[turn], 'x', pairs))]
where the time goes in v5:
time: 88.4 us; the launch traced here: 88.2 us
  blocking collectives  42.3 us (48%)
  starting transfers between devices  17.3 us (20%)
  Pallas kernels  16.3 us (18%)
  waiting for transfers between devices  10.7 us (12%)
  local copies, waits for them, and re-layouts  0.89 us (1%)
    all_to_all x2, blocking collectives, per_device(): got = lax.all_to_all(send, ALL, 0, 0, tiled=True)  42.3 us
    ppermute x6, starting transfers between devices, around_x(): got.append(lax.ppermute(arrays[turn], 'x', pairs))  9.17 us
    pallas_call x1, Pallas kernels, per_device(): pl.pallas_call(late_kernel, out_shape=[shape(dims, bf16) for dims in late...  5.27 us
    all_to_all x1, starting transfers between devices, per_device(): got = lax.all_to_all(send, CHIPS, 0, 0, tiled=True)  5 us
    ppermute x6, waiting for transfers between devices, around_x(): got.append(lax.ppermute(arrays[turn], 'x', pairs))  4.93 us
    all_to_all x1, waiting for transfers between devices, per_device(): got = lax.all_to_all(send, CHIPS, 0, 0, tiled=True)  3.98 us
    pallas_call x1, Pallas kernels, per_device(): pl.pallas_call(first_kernel, out_shape=[shape((owners, wide), f32)] * 4 +...  3.76 us
    pallas_call x1, Pallas kernels, per_device(): pl.pallas_call(expert_kernel, out_shape=[shape((owners, width), bf16)] *...  2.86 us
  transfers between devices with their start and end apart: 9, of which 8 were waited for; matrix products, arithmetic and copies ran while one was open for 0% of the time, Pallas kernels for 6%

profile of v5, /device:TPU:1, one launch (start us, length us, event | category | flops | bytes accessed | tf_op | source)
XLA Modules:
  0.0 88.2 jit_solution(17146469154062010003)
XLA Ops:
  0.6 0.0 copy-start.2
  0.7 0.9 copy-done.2
  1.5 0.0 copy-start
  1.5 0.0 copy-start.1
  1.5 3.8 %first.1 = (f32[16,1408]{1,0:T(8,128)S(1)}, f32[16,1408]{1,0:T(8,128)S(1)}, f32[16,1408]{1,0:T(8,128)S(1)}, f32[16,1408]{1,0:T(8,128)S(1)}, f32[32,1024]{1,0:T(8...) custom-call(s32[1]{0:T(128)} %bitcast.place_ref, bf16[1024,1280]{1,0:T(8,128)(2,1)} %bitcast.9, ...), custom_call_target="tpu_custom_call" | custom-call | flops 251658240 | bytes 5242880 | tf_op jit(solution)/shard_map/first/pallas_call | solution.py:393
  5.3 2.1 %collective-permute-start = (f32[16,1408]{1,0:T(8,128)S(1)}, f32[16,1408]{1,0:T(8,128)S(1)}, u32[]{:S(2)}, u32[]{:S(2)}) collective-permute-start(f32[16,1408]{1,0:T(8,128)S(1)} %get-tuple-element.39), channel_id=1, source_target_pairs={{0,16},{16,32},{32,48},{48,0},{1,17},{17,33},{33,49},{49,1},{2,18}... | collective-permute-start | bytes 270344 | tf_op jit(solution)/shard_map/ppermute | solution.py:371
  7.4 2.5 %collective-permute-start.1 = (f32[16,1408]{1,0:T(8,128)S(1)}, f32[16,1408]{1,0:T(8,128)S(1)}, u32[]{:S(2)}, u32[]{:S(2)}) collective-permute-start(f32[16,1408]{1,0:T(8,128)S(1)} %get-tuple-element.40), channel_id=1, source_target_pairs={{0,32},{16,48},{32,0},{48,16},{1,33},{17,49},{33,1},{49,17},{2,34}... | collective-permute-start | bytes 270344 | tf_op jit(solution)/shard_map/ppermute | solution.py:371
  9.9 1.1 %collective-permute-start.2 = (f32[16,1408]{1,0:T(8,128)S(1)}, f32[16,1408]{1,0:T(8,128)S(1)}, u32[]{:S(2)}, u32[]{:S(2)}) collective-permute-start(f32[16,1408]{1,0:T(8,128)S(1)} %get-tuple-element.41), channel_id=1, source_target_pairs={{0,48},{16,0},{32,16},{48,32},{1,49},{17,1},{33,17},{49,33},{2,50}... | collective-permute-start | bytes 270344 | tf_op jit(solution)/shard_map/ppermute | solution.py:371
  11.0 0.0 collective-permute-done.in1
  11.0 2.5 %collective-permute-done.1.in2 = f32[16,1408]{1,0:T(8,128)S(1)} collective-permute-done((f32[16,1408]{1,0:T(8,128)S(1)}, f32[16,1408]{1,0:T(8,128)S(1)}, u32[]{:S(2)}, u32[]{:S(2)}) %collective-permute-start.1) | collective-permute-done | bytes 90144 | tf_op jit(solution)/shard_map/ppermute | solution.py:371
  13.5 0.4 collective-permute-done.2.in3
  14.0 0.2 first_sum.1
  14.2 23.3 %all_to_all.15.got_ref = bf16[128,2,768]{2,1,0:T(2,128)(2,1)S(1)} all-to-all(bf16[128,2,768]{2,1,0:T(2,128)(2,1)S(1)} %first_sum.1), channel_id=1, replica_groups=mesh['yh'=2,'x'=4,'z'=4,'yl'=2,'core'=2] {'yh','x','z','yl','core'}, dimensions={0} | all-to-all | bytes 786432 | tf_op jit(solution)/shard_map/all_to_all | solution.py:417
  37.5 0.0 copy-done
  37.6 0.0 copy-done.1
  37.6 2.9 %experts.1 = (bf16[16,1280]{1,0:T(8,128)(2,1)S(1)}, bf16[16,1280]{1,0:T(8,128)(2,1)S(1)}, bf16[16,1280]{1,0:T(8,128)(2,1)S(1)}, bf16[16,1280]{1,0:T(8,128)(2,1)S...) custom-call(s32[1]{0:T(128)} %bitcast.place_ref, ...), custom_call_target="tpu_custom_call" | custom-call | flops 209715200 | bytes 6553600 | tf_op jit(solution)/shard_map/experts/pallas_call | solution.py:418
  40.4 0.1 collective-permute-start.3
  40.5 1.7 %collective-permute-start.4 = (bf16[16,1280]{1,0:T(8,128)(2,1)S(1)}, bf16[16,1280]{1,0:T(8,128)(2,1)S(1)}, u32[]{:S(2)}, u32[]{:S(2)}) collective-permute-start(bf16[16,1280]{1,0:T(8,128)(2,1)S(1)} %get-tuple-element.44), channel_id=1, source_target_pairs={{0,32},{16,48},{32,0},{48,16},{1,33},{17,49},{33,1},{49,17},{2,34}... | collective-permute-start | bytes 122888 | tf_op jit(solution)/shard_map/ppermute | solution.py:371
  42.2 1.7 %collective-permute-start.5 = (bf16[16,1280]{1,0:T(8,128)(2,1)S(1)}, bf16[16,1280]{1,0:T(8,128)(2,1)S(1)}, u32[]{:S(2)}, u32[]{:S(2)}) collective-permute-start(bf16[16,1280]{1,0:T(8,128)(2,1)S(1)} %get-tuple-element.45), channel_id=1, source_target_pairs={{0,48},{16,0},{32,16},{48,32},{1,49},{17,1},{33,17},{49,33},{2,50}... | collective-permute-start | bytes 122888 | tf_op jit(solution)/shard_map/ppermute | solution.py:371
  43.9 0.7 collective-permute-done.3.in1
  44.6 0.4 collective-permute-done.4.in2
  45.0 0.9 collective-permute-done.5.in3
  45.9 0.2 second_sum.1
  46.1 19.0 %all_to_all.16.got_ref = bf16[128,2,768]{2,1,0:T(2,128)(2,1)S(1)} all-to-all(bf16[128,2,768]{2,1,0:T(2,128)(2,1)S(1)} %second_sum.1), channel_id=1, replica_groups=mesh['yh'=2,'x'=4,'z'=4,'yl'=2,'core'=2] {'yh','x','z','yl','core'}, dimensions={0} | all-to-all | bytes 786432 | tf_op jit(solution)/shard_map/all_to_all | solution.py:443
  65.1 0.0 copy-start.3
  65.1 2.3 %tokens.1 = (bf16[3,32,1024]{2,1,0:T(8,128)(2,1)S(1)}, bf16[2,32,1280]{2,1,0:T(8,128)(2,1)S(1)}, f32[16,1280]{1,0:T(8,128)S(1)}, f32[16,1280]{1,0:T(8,128)S(1)}) custom-call(s32[1]{0:T(128)} %bitcast.place_ref, bf16[128,2,768]{2,1,0:T(2,128)(2,1)S(1)} %all_to_all.16.got_ref, f32[32,1024]{1,0:T(8,128)S(1)} %get-tuple-element.48.logits_ref, ...), custom_call_target="tpu_custom_call" | custom-call | flops 251658240 | bytes 5242880 | tf_op jit(solution)/shard_map/tokens/pallas_call | solution.py:444
  67.4 0.7 collective-permute-start.6
  68.1 0.9 %collective-permute-done.6.got_ref = f32[16,1280]{1,0:T(8,128)S(1)} collective-permute-done((f32[16,1280]{1,0:T(8,128)S(1)}, f32[16,1280]{1,0:T(8,128)S(1)}, u32[]{:S(2)}, u32[]{:S(2)}) %collective-permute-start.6) | collective-permute-done | bytes 81952 | tf_op jit(solution)/shard_map/ppermute | solution.py:459
  69.1 0.8 router_split.1
  69.9 5.0 %all-to-all-start.2 = ((bf16[64,4,640]{2,1,0:T(4,128)(2,1)}), bf16[64,4,640]{2,1,0:T(4,128)(2,1)S(1)}, u32[]{:S(2)}, u32[]{:S(2)}) async-start(bf16[64,4,640]{2,1,0:T(4,128)(2,1)} %router_split.1), calls=%async_computation.2 | async-start | bytes 655360 | tf_op jit(solution)/shard_map/all_to_all | solution.py:472
  74.9 0.0 copy-done.3
  74.9 5.3 %late.1 = (bf16[2,1280,640]{2,1,0:T(8,128)(2,1)}, bf16[2,640,1280]{2,1,0:T(8,128)(2,1)}, bf16[1024,1280]{1,0:T(8,128)(2,1)}, bf16[1024,1280]{1,0:T(8,128)(2,1)}) custom-call(bf16[4,16,1280]{2,1,0:T(8,128)(2,1)S(1)} %get-tuple-element.58.rows_ref, bf16[4,16,640]{2,1,0:T(8,128)(2,1)S(1)} %get-tuple-element.59.units_ref, ...), custom_call_target="tpu_custom_call" | custom-call | flops 10485760000 | bytes 5242880 | tf_op jit(solution)/shard_map/late/pallas_call | solution.py:474
  80.2 4.0 %all-to-all-done.2.got_ref = bf16[64,4,640]{2,1,0:T(4,128)(2,1)S(1)} async-done(((bf16[64,4,640]{2,1,0:T(4,128)(2,1)}), bf16[64,4,640]{2,1,0:T(4,128)(2,1)S(1)}, u32[]{:S(2)}, u32[]{:S(2)}) %all-to-all-start.2) | async-done | bytes 327712 | tf_op jit(solution)/shard_map/all_to_all | solution.py:472
  84.2 0.2 router_sum.1.half_ref
  84.3 2.4 %collective-permute-start.7 = (f32[16,160]{1,0:T(8,128)S(1)}, f32[16,160]{1,0:T(8,128)S(1)}, u32[]{:S(2)}, u32[]{:S(2)}) collective-permute-start(f32[16,160]{1,0:T(8,128)S(1)} %router_sum.1.half_ref), channel_id=1, source_target_pairs={{0,1},{1,0},{2,3},{3,2},{4,5},{5,4},{6,7},{7,6},{8,9},{9,8},{10,11... | collective-permute-start | bytes 30728 | tf_op jit(solution)/shard_map/ppermute | solution.py:499
  86.7 0.8 collective-permute-done.7.other_ref
  87.5 0.6 router_join.1
Async XLA Ops:
  0.6 0.9 %copy-start.2 = (bf16[1280,32]{0,1:T(8,128)(2,1)S(1)}, bf16[1280,32]{0,1:T(8,128)(2,1)}, u32[]{:S(2)}) copy-start(bf16[1280,32]{0,1:T(8,128)(2,1)} %param.6) | copy-start | bytes 245764
  1.5 36.0 %copy-start = (bf16[2,1280,640]{2,1,0:T(8,128)(2,1)S(1)}, bf16[2,1280,640]{2,1,0:T(8,128)(2,1)}, u32[]{:S(2)}) copy-start(bf16[2,1280,640]{2,1,0:T(8,128)(2,1)} %w_in_ref.1) | copy-start | bytes 9830404
  1.5 36.0 %copy-start.1 = (bf16[2,640,1280]{2,1,0:T(8,128)(2,1)S(1)}, bf16[2,640,1280]{2,1,0:T(8,128)(2,1)}, u32[]{:S(2)}) copy-start(bf16[2,640,1280]{2,1,0:T(8,128)(2,1)} %w_out_ref.1) | copy-start | bytes 9830404
  5.3 5.7 %collective-permute-start = (f32[16,1408]{1,0:T(8,128)S(1)}, f32[16,1408]{1,0:T(8,128)S(1)}, u32[]{:S(2)}, u32[]{:S(2)}) collective-permute-start(f32[16,1408]{1,0:T(8,128)S(1)} %get-tuple-element.39), channel_id=1, source_target_pairs={{0,16},{16,32},{32,48},{48,0},{1,17},{17,33},{33,49},{49,1},{2,18}... | collective-permute-start | bytes 270344 | tf_op jit(solution)/shard_map/ppermute | solution.py:371
  7.4 6.1 %collective-permute-start.1 = (f32[16,1408]{1,0:T(8,128)S(1)}, f32[16,1408]{1,0:T(8,128)S(1)}, u32[]{:S(2)}, u32[]{:S(2)}) collective-permute-start(f32[16,1408]{1,0:T(8,128)S(1)} %get-tuple-element.40), channel_id=1, source_target_pairs={{0,32},{16,48},{32,0},{48,16},{1,33},{17,49},{33,1},{49,17},{2,34}... | collective-permute-start | bytes 270344 | tf_op jit(solution)/shard_map/ppermute | solution.py:371
  9.9 4.1 %collective-permute-start.2 = (f32[16,1408]{1,0:T(8,128)S(1)}, f32[16,1408]{1,0:T(8,128)S(1)}, u32[]{:S(2)}, u32[]{:S(2)}) collective-permute-start(f32[16,1408]{1,0:T(8,128)S(1)} %get-tuple-element.41), channel_id=1, source_target_pairs={{0,48},{16,0},{32,16},{48,32},{1,49},{17,1},{33,17},{49,33},{2,50}... | collective-permute-start | bytes 270344 | tf_op jit(solution)/shard_map/ppermute | solution.py:371
  40.4 4.1 %collective-permute-start.3 = (bf16[16,1280]{1,0:T(8,128)(2,1)S(1)}, bf16[16,1280]{1,0:T(8,128)(2,1)S(1)}, u32[]{:S(2)}, u32[]{:S(2)}) collective-permute-start(bf16[16,1280]{1,0:T(8,128)(2,1)S(1)} %get-tuple-element.43), channel_id=1, source_target_pairs={{0,16},{16,32},{32,48},{48,0},{1,17},{17,33},{33,49},{49,1},{2,18}... | collective-permute-start | bytes 122888 | tf_op jit(solution)/shard_map/ppermute | solution.py:371
  40.5 4.5 %collective-permute-start.4 = (bf16[16,1280]{1,0:T(8,128)(2,1)S(1)}, bf16[16,1280]{1,0:T(8,128)(2,1)S(1)}, u32[]{:S(2)}, u32[]{:S(2)}) collective-permute-start(bf16[16,1280]{1,0:T(8,128)(2,1)S(1)} %get-tuple-element.44), channel_id=1, source_target_pairs={{0,32},{16,48},{32,0},{48,16},{1,33},{17,49},{33,1},{49,17},{2,34}... | collective-permute-start | bytes 122888 | tf_op jit(solution)/shard_map/ppermute | solution.py:371
  42.2 3.6 %collective-permute-start.5 = (bf16[16,1280]{1,0:T(8,128)(2,1)S(1)}, bf16[16,1280]{1,0:T(8,128)(2,1)S(1)}, u32[]{:S(2)}, u32[]{:S(2)}) collective-permute-start(bf16[16,1280]{1,0:T(8,128)(2,1)S(1)} %get-tuple-element.45), channel_id=1, source_target_pairs={{0,48},{16,0},{32,16},{48,32},{1,49},{17,1},{33,17},{49,33},{2,50}... | collective-permute-start | bytes 122888 | tf_op jit(solution)/shard_map/ppermute | solution.py:371
  65.1 9.8 %copy-start.3 = (bf16[1280,32]{0,1:T(8,128)(2,1)S(1)}, bf16[1280,32]{0,1:T(8,128)(2,1)}, u32[]{:S(2)}) copy-start(bf16[1280,32]{0,1:T(8,128)(2,1)} %param.6) | copy-start | bytes 245764
  67.4 1.7 %collective-permute-start.6 = (f32[16,1280]{1,0:T(8,128)S(1)}, f32[16,1280]{1,0:T(8,128)S(1)}, u32[]{:S(2)}, u32[]{:S(2)}) collective-permute-start(f32[16,1280]{1,0:T(8,128)S(1)} %get-tuple-element.52), channel_id=1, source_target_pairs={{0,1},{1,0},{2,3},{3,2},{4,5},{5,4},{6,7},{7,6},{8,9},{9,8},{10,11... | collective-permute-start | bytes 245768 | tf_op jit(solution)/shard_map/ppermute | solution.py:459
  69.9 14.3 %all-to-all-start.2 = ((bf16[64,4,640]{2,1,0:T(4,128)(2,1)}), bf16[64,4,640]{2,1,0:T(4,128)(2,1)S(1)}, u32[]{:S(2)}, u32[]{:S(2)}) async-start(bf16[64,4,640]{2,1,0:T(4,128)(2,1)} %router_split.1), calls=%async_computation.2 | async-start | bytes 655360 | tf_op jit(solution)/shard_map/all_to_all | solution.py:472
  84.3 3.2 %collective-permute-start.7 = (f32[16,160]{1,0:T(8,128)S(1)}, f32[16,160]{1,0:T(8,128)S(1)}, u32[]{:S(2)}, u32[]{:S(2)}) collective-permute-start(f32[16,160]{1,0:T(8,128)S(1)} %router_sum.1.half_ref), channel_id=1, source_target_pairs={{0,1},{1,0},{2,3},{3,2},{4,5},{5,4},{6,7},{7,6},{8,9},{9,8},{10,11... | collective-permute-start | bytes 30728 | tf_op jit(solution)/shard_map/ppermute | solution.py:499

commit v6 on v5

--- a/solution.py
+++ b/solution.py
@@ -159,7 +159,7 @@
         jnp.concatenate([row[:, :half], extra], axis=1),
         jnp.concatenate([row[:, half:], extra], axis=1),
     ]
-    both = jnp.stack(halves, axis=1).astype(bf16)
+    both = jnp.stack(halves, axis=1).astype(out_ref.dtype)
     for member in range(out_ref.shape[0] // owners):
         out_ref[member * owners : (member + 1) * owners] = both
 
@@ -386,7 +386,7 @@
     held, _, units = w_in.shape
     owners = slots // held
     wide = width + LANES
-    sent = shape((8 * owners, 2, width // 2 + LANES), bf16)
+    sent = (8 * owners, 2, width // 2 + LANES)
     token_flops = 2 * length * width * slots
     expert_flops = 2 * held * owners * width * units
 
@@ -408,7 +408,7 @@
     got = around_x(send)
     send = pl.pallas_call(
         first_sum_kernel,
-        out_shape=sent,
+        out_shape=shape(sent, f32),
         in_specs=[SMEM] + [VMEM] * 4,
         out_specs=VMEM,
         compiler_params=params(8),
@@ -434,7 +434,7 @@
     got = around_x(send)
     send = pl.pallas_call(
         second_sum_kernel,
-        out_shape=sent,
+        out_shape=shape(sent, bf16),
         in_specs=[VMEM] * 6,
         out_specs=VMEM,
         compiler_params=params(8),

time: 88.4 us -> 92.4 us (1.045)
  blocking collectives: 42.3 us -> 46.3 us
    all_to_all x2, blocking collectives: 42.3 us -> 46.3 us  [per_device(): got = lax.all_to_all(send, ALL, 0, 0, tiled=True)]
where the time goes in v6:
time: 92.4 us; the launch traced here: 92.1 us
  blocking collectives  46.3 us (50%)
  starting transfers between devices  17.4 us (19%)
  Pallas kernels  16.2 us (18%)
  waiting for transfers between devices  10.5 us (11%)
    all_to_all x2, blocking collectives, per_device(): got = lax.all_to_all(send, ALL, 0, 0, tiled=True)  46.3 us
    ppermute x6, starting transfers between devices, around_x(): got.append(lax.ppermute(arrays[turn], 'x', pairs))  9.33 us
    pallas_call x1, Pallas kernels, per_device(): pl.pallas_call(late_kernel, out_shape=[shape(dims, bf16) for dims in late...  5.27 us
    all_to_all x1, starting transfers between devices, per_device(): got = lax.all_to_all(send, CHIPS, 0, 0, tiled=True)  5.01 us
    ppermute x6, waiting for transfers between devices, around_x(): got.append(lax.ppermute(arrays[turn], 'x', pairs))  4.77 us
    all_to_all x1, waiting for transfers between devices, per_device(): got = lax.all_to_all(send, CHIPS, 0, 0, tiled=True)  3.98 us
    pallas_call x1, Pallas kernels, per_device(): pl.pallas_call(first_kernel, out_shape=[shape((owners, wide), f32)] * 4 +...  3.76 us
    pallas_call x1, Pallas kernels, per_device(): pl.pallas_call(expert_kernel, out_shape=[shape((owners, width), bf16)] *...  2.79 us
  transfers between devices with their start and end apart: 9, of which 8 were waited for; matrix products, arithmetic and copies ran while one was open for 0% of the time, Pallas kernels for 6%

profile of v6, /device:TPU:1, one launch (start us, length us, event | category | flops | bytes accessed | tf_op | source)
XLA Modules:
  0.0 92.1 jit_solution(4645715306543493919)
XLA Ops:
  0.6 0.0 copy-start.2
  0.7 0.9 copy-done.2
  1.5 0.0 copy-start
  1.5 0.0 copy-start.1
  1.5 3.8 %first.1 = (f32[16,1408]{1,0:T(8,128)S(1)}, f32[16,1408]{1,0:T(8,128)S(1)}, f32[16,1408]{1,0:T(8,128)S(1)}, f32[16,1408]{1,0:T(8,128)S(1)}, f32[32,1024]{1,0:T(8...) custom-call(s32[1]{0:T(128)} %bitcast.place_ref, bf16[1024,1280]{1,0:T(8,128)(2,1)} %bitcast.9, ...), custom_call_target="tpu_custom_call" | custom-call | flops 251658240 | bytes 5242880 | tf_op jit(solution)/shard_map/first/pallas_call | solution.py:393
  5.3 2.1 %collective-permute-start = (f32[16,1408]{1,0:T(8,128)S(1)}, f32[16,1408]{1,0:T(8,128)S(1)}, u32[]{:S(2)}, u32[]{:S(2)}) collective-permute-start(f32[16,1408]{1,0:T(8,128)S(1)} %get-tuple-element.39), channel_id=1, source_target_pairs={{0,16},{16,32},{32,48},{48,0},{1,17},{17,33},{33,49},{49,1},{2,18}... | collective-permute-start | bytes 270344 | tf_op jit(solution)/shard_map/ppermute | solution.py:371
  7.4 2.5 %collective-permute-start.1 = (f32[16,1408]{1,0:T(8,128)S(1)}, f32[16,1408]{1,0:T(8,128)S(1)}, u32[]{:S(2)}, u32[]{:S(2)}) collective-permute-start(f32[16,1408]{1,0:T(8,128)S(1)} %get-tuple-element.40), channel_id=1, source_target_pairs={{0,32},{16,48},{32,0},{48,16},{1,33},{17,49},{33,1},{49,17},{2,34}... | collective-permute-start | bytes 270344 | tf_op jit(solution)/shard_map/ppermute | solution.py:371
  9.9 1.1 %collective-permute-start.2 = (f32[16,1408]{1,0:T(8,128)S(1)}, f32[16,1408]{1,0:T(8,128)S(1)}, u32[]{:S(2)}, u32[]{:S(2)}) collective-permute-start(f32[16,1408]{1,0:T(8,128)S(1)} %get-tuple-element.41), channel_id=1, source_target_pairs={{0,48},{16,0},{32,16},{48,32},{1,49},{17,1},{33,17},{49,33},{2,50}... | collective-permute-start | bytes 270344 | tf_op jit(solution)/shard_map/ppermute | solution.py:371
  11.0 0.0 collective-permute-done.in1
  11.0 2.5 %collective-permute-done.1.in2 = f32[16,1408]{1,0:T(8,128)S(1)} collective-permute-done((f32[16,1408]{1,0:T(8,128)S(1)}, f32[16,1408]{1,0:T(8,128)S(1)}, u32[]{:S(2)}, u32[]{:S(2)}) %collective-permute-start.1) | collective-permute-done | bytes 90144 | tf_op jit(solution)/shard_map/ppermute | solution.py:371
  13.5 0.4 collective-permute-done.2.in3
  14.0 0.3 first_sum.1
  14.2 27.1 %all_to_all.15.got_ref = f32[128,2,768]{2,1,0:T(2,128)S(1)} all-to-all(f32[128,2,768]{2,1,0:T(2,128)S(1)} %first_sum.1), channel_id=1, replica_groups=mesh['yh'=2,'x'=4,'z'=4,'yl'=2,'core'=2] {'yh','x','z','yl','core'}, dimensions={0} | all-to-all | bytes 1572864 | tf_op jit(solution)/shard_map/all_to_all | solution.py:417
  41.3 0.0 copy-done
  41.3 0.0 copy-done.1
  41.3 2.8 %experts.1 = (bf16[16,1280]{1,0:T(8,128)(2,1)S(1)}, bf16[16,1280]{1,0:T(8,128)(2,1)S(1)}, bf16[16,1280]{1,0:T(8,128)(2,1)S(1)}, bf16[16,1280]{1,0:T(8,128)(2,1)S...) custom-call(s32[1]{0:T(128)} %bitcast.place_ref, ...), custom_call_target="tpu_custom_call" | custom-call | flops 209715200 | bytes 6553600 | tf_op jit(solution)/shard_map/experts/pallas_call | solution.py:418
  44.1 0.1 collective-permute-start.3
  44.3 1.9 %collective-permute-start.4 = (bf16[16,1280]{1,0:T(8,128)(2,1)S(1)}, bf16[16,1280]{1,0:T(8,128)(2,1)S(1)}, u32[]{:S(2)}, u32[]{:S(2)}) collective-permute-start(bf16[16,1280]{1,0:T(8,128)(2,1)S(1)} %get-tuple-element.44), channel_id=1, source_target_pairs={{0,32},{16,48},{32,0},{48,16},{1,33},{17,49},{33,1},{49,17},{2,34}... | collective-permute-start | bytes 122888 | tf_op jit(solution)/shard_map/ppermute | solution.py:371
  46.2 1.6 %collective-permute-start.5 = (bf16[16,1280]{1,0:T(8,128)(2,1)S(1)}, bf16[16,1280]{1,0:T(8,128)(2,1)S(1)}, u32[]{:S(2)}, u32[]{:S(2)}) collective-permute-start(bf16[16,1280]{1,0:T(8,128)(2,1)S(1)} %get-tuple-element.45), channel_id=1, source_target_pairs={{0,48},{16,0},{32,16},{48,32},{1,49},{17,1},{33,17},{49,33},{2,50}... | collective-permute-start | bytes 122888 | tf_op jit(solution)/shard_map/ppermute | solution.py:371
  47.8 0.5 collective-permute-done.3.in1
  48.3 0.5 collective-permute-done.4.in2
  48.7 0.8 collective-permute-done.5.in3
  49.6 0.2 second_sum.1
  49.8 19.2 %all_to_all.16.got_ref = bf16[128,2,768]{2,1,0:T(2,128)(2,1)S(1)} all-to-all(bf16[128,2,768]{2,1,0:T(2,128)(2,1)S(1)} %second_sum.1), channel_id=1, replica_groups=mesh['yh'=2,'x'=4,'z'=4,'yl'=2,'core'=2] {'yh','x','z','yl','core'}, dimensions={0} | all-to-all | bytes 786432 | tf_op jit(solution)/shard_map/all_to_all | solution.py:443
  69.0 0.0 copy-start.3
  69.0 2.3 %tokens.1 = (bf16[3,32,1024]{2,1,0:T(8,128)(2,1)S(1)}, bf16[2,32,1280]{2,1,0:T(8,128)(2,1)S(1)}, f32[16,1280]{1,0:T(8,128)S(1)}, f32[16,1280]{1,0:T(8,128)S(1)}) custom-call(s32[1]{0:T(128)} %bitcast.place_ref, bf16[128,2,768]{2,1,0:T(2,128)(2,1)S(1)} %all_to_all.16.got_ref, f32[32,1024]{1,0:T(8,128)S(1)} %get-tuple-element.48.logits_ref, ...), custom_call_target="tpu_custom_call" | custom-call | flops 251658240 | bytes 5242880 | tf_op jit(solution)/shard_map/tokens/pallas_call | solution.py:444
  71.3 0.7 collective-permute-start.6
  72.1 0.9 %collective-permute-done.6.got_ref = f32[16,1280]{1,0:T(8,128)S(1)} collective-permute-done((f32[16,1280]{1,0:T(8,128)S(1)}, f32[16,1280]{1,0:T(8,128)S(1)}, u32[]{:S(2)}, u32[]{:S(2)}) %collective-permute-start.6) | collective-permute-done | bytes 81952 | tf_op jit(solution)/shard_map/ppermute | solution.py:459
  73.0 0.8 router_split.1
  73.8 5.0 %all-to-all-start.2 = ((bf16[64,4,640]{2,1,0:T(4,128)(2,1)}), bf16[64,4,640]{2,1,0:T(4,128)(2,1)S(1)}, u32[]{:S(2)}, u32[]{:S(2)}) async-start(bf16[64,4,640]{2,1,0:T(4,128)(2,1)} %router_split.1), calls=%async_computation.2 | async-start | bytes 655360 | tf_op jit(solution)/shard_map/all_to_all | solution.py:472
  78.9 0.0 copy-done.3
  78.9 5.3 %late.1 = (bf16[2,1280,640]{2,1,0:T(8,128)(2,1)}, bf16[2,640,1280]{2,1,0:T(8,128)(2,1)}, bf16[1024,1280]{1,0:T(8,128)(2,1)}, bf16[1024,1280]{1,0:T(8,128)(2,1)}) custom-call(bf16[4,16,1280]{2,1,0:T(8,128)(2,1)S(1)} %get-tuple-element.58.rows_ref, bf16[4,16,640]{2,1,0:T(8,128)(2,1)S(1)} %get-tuple-element.59.units_ref, ...), custom_call_target="tpu_custom_call" | custom-call | flops 10485760000 | bytes 5242880 | tf_op jit(solution)/shard_map/late/pallas_call | solution.py:474
  84.1 4.0 %all-to-all-done.2.got_ref = bf16[64,4,640]{2,1,0:T(4,128)(2,1)S(1)} async-done(((bf16[64,4,640]{2,1,0:T(4,128)(2,1)}), bf16[64,4,640]{2,1,0:T(4,128)(2,1)S(1)}, u32[]{:S(2)}, u32[]{:S(2)}) %all-to-all-start.2) | async-done | bytes 327712 | tf_op jit(solution)/shard_map/all_to_all | solution.py:472
  88.1 0.2 router_sum.1.half_ref
  88.3 2.4 %collective-permute-start.7 = (f32[16,160]{1,0:T(8,128)S(1)}, f32[16,160]{1,0:T(8,128)S(1)}, u32[]{:S(2)}, u32[]{:S(2)}) collective-permute-start(f32[16,160]{1,0:T(8,128)S(1)} %router_sum.1.half_ref), channel_id=1, source_target_pairs={{0,1},{1,0},{2,3},{3,2},{4,5},{5,4},{6,7},{7,6},{8,9},{9,8},{10,11... | collective-permute-start | bytes 30728 | tf_op jit(solution)/shard_map/ppermute | solution.py:499
  90.6 0.8 collective-permute-done.7.other_ref
  91.5 0.6 router_join.1
Async XLA Ops:
  0.6 0.9 copy-start.2
  1.5 39.8 %copy-start = (bf16[2,1280,640]{2,1,0:T(8,128)(2,1)S(1)}, bf16[2,1280,640]{2,1,0:T(8,128)(2,1)}, u32[]{:S(2)}) copy-start(bf16[2,1280,640]{2,1,0:T(8,128)(2,1)} %w_in_ref.1) | copy-start | bytes 9830404
  1.5 39.8 %copy-start.1 = (bf16[2,640,1280]{2,1,0:T(8,128)(2,1)S(1)}, bf16[2,640,1280]{2,1,0:T(8,128)(2,1)}, u32[]{:S(2)}) copy-start(bf16[2,640,1280]{2,1,0:T(8,128)(2,1)} %w_out_ref.1) | copy-start | bytes 9830404
  5.3 5.7 %collective-permute-start = (f32[16,1408]{1,0:T(8,128)S(1)}, f32[16,1408]{1,0:T(8,128)S(1)}, u32[]{:S(2)}, u32[]{:S(2)}) collective-permute-start(f32[16,1408]{1,0:T(8,128)S(1)} %get-tuple-element.39), channel_id=1, source_target_pairs={{0,16},{16,32},{32,48},{48,0},{1,17},{17,33},{33,49},{49,1},{2,18}... | collective-permute-start | bytes 270344 | tf_op jit(solution)/shard_map/ppermute | solution.py:371
  7.4 6.1 %collective-permute-start.1 = (f32[16,1408]{1,0:T(8,128)S(1)}, f32[16,1408]{1,0:T(8,128)S(1)}, u32[]{:S(2)}, u32[]{:S(2)}) collective-permute-start(f32[16,1408]{1,0:T(8,128)S(1)} %get-tuple-element.40), channel_id=1, source_target_pairs={{0,32},{16,48},{32,0},{48,16},{1,33},{17,49},{33,1},{49,17},{2,34}... | collective-permute-start | bytes 270344 | tf_op jit(solution)/shard_map/ppermute | solution.py:371
  9.9 4.1 %collective-permute-start.2 = (f32[16,1408]{1,0:T(8,128)S(1)}, f32[16,1408]{1,0:T(8,128)S(1)}, u32[]{:S(2)}, u32[]{:S(2)}) collective-permute-start(f32[16,1408]{1,0:T(8,128)S(1)} %get-tuple-element.41), channel_id=1, source_target_pairs={{0,48},{16,0},{32,16},{48,32},{1,49},{17,1},{33,17},{49,33},{2,50}... | collective-permute-start | bytes 270344 | tf_op jit(solution)/shard_map/ppermute | solution.py:371
  44.1 4.1 %collective-permute-start.3 = (bf16[16,1280]{1,0:T(8,128)(2,1)S(1)}, bf16[16,1280]{1,0:T(8,128)(2,1)S(1)}, u32[]{:S(2)}, u32[]{:S(2)}) collective-permute-start(bf16[16,1280]{1,0:T(8,128)(2,1)S(1)} %get-tuple-element.43), channel_id=1, source_target_pairs={{0,16},{16,32},{32,48},{48,0},{1,17},{17,33},{33,49},{49,1},{2,18}... | collective-permute-start | bytes 122888 | tf_op jit(solution)/shard_map/ppermute | solution.py:371
  44.3 4.5 %collective-permute-start.4 = (bf16[16,1280]{1,0:T(8,128)(2,1)S(1)}, bf16[16,1280]{1,0:T(8,128)(2,1)S(1)}, u32[]{:S(2)}, u32[]{:S(2)}) collective-permute-start(bf16[16,1280]{1,0:T(8,128)(2,1)S(1)} %get-tuple-element.44), channel_id=1, source_target_pairs={{0,32},{16,48},{32,0},{48,16},{1,33},{17,49},{33,1},{49,17},{2,34}... | collective-permute-start | bytes 122888 | tf_op jit(solution)/shard_map/ppermute | solution.py:371
  46.2 3.4 %collective-permute-start.5 = (bf16[16,1280]{1,0:T(8,128)(2,1)S(1)}, bf16[16,1280]{1,0:T(8,128)(2,1)S(1)}, u32[]{:S(2)}, u32[]{:S(2)}) collective-permute-start(bf16[16,1280]{1,0:T(8,128)(2,1)S(1)} %get-tuple-element.45), channel_id=1, source_target_pairs={{0,48},{16,0},{32,16},{48,32},{1,49},{17,1},{33,17},{49,33},{2,50}... | collective-permute-start | bytes 122888 | tf_op jit(solution)/shard_map/ppermute | solution.py:371
  69.0 9.8 %copy-start.3 = (bf16[1280,32]{0,1:T(8,128)(2,1)S(1)}, bf16[1280,32]{0,1:T(8,128)(2,1)}, u32[]{:S(2)}) copy-start(bf16[1280,32]{0,1:T(8,128)(2,1)} %param.6) | copy-start | bytes 245764
  71.3 1.7 %collective-permute-start.6 = (f32[16,1280]{1,0:T(8,128)S(1)}, f32[16,1280]{1,0:T(8,128)S(1)}, u32[]{:S(2)}, u32[]{:S(2)}) collective-permute-start(f32[16,1280]{1,0:T(8,128)S(1)} %get-tuple-element.52), channel_id=1, source_target_pairs={{0,1},{1,0},{2,3},{3,2},{4,5},{5,4},{6,7},{7,6},{8,9},{9,8},{10,11... | collective-permute-start | bytes 245768 | tf_op jit(solution)/shard_map/ppermute | solution.py:459
  73.8 14.3 %all-to-all-start.2 = ((bf16[64,4,640]{2,1,0:T(4,128)(2,1)}), bf16[64,4,640]{2,1,0:T(4,128)(2,1)S(1)}, u32[]{:S(2)}, u32[]{:S(2)}) async-start(bf16[64,4,640]{2,1,0:T(4,128)(2,1)} %router_split.1), calls=%async_computation.2 | async-start | bytes 655360 | tf_op jit(solution)/shard_map/all_to_all | solution.py:472
  88.3 3.2 %collective-permute-start.7 = (f32[16,160]{1,0:T(8,128)S(1)}, f32[16,160]{1,0:T(8,128)S(1)}, u32[]{:S(2)}, u32[]{:S(2)}) collective-permute-start(f32[16,160]{1,0:T(8,128)S(1)} %router_sum.1.half_ref), channel_id=1, source_target_pairs={{0,1},{1,0},{2,3},{3,2},{4,5},{5,4},{6,7},{7,6},{8,9},{9,8},{10,11... | collective-permute-start | bytes 30728 | tf_op jit(solution)/shard_map/ppermute | solution.py:499

commit v7 on v6

--- a/solution.py
+++ b/solution.py
@@ -142,10 +142,13 @@
         columns += pieces(lse[place * owners : (place + 1) * owners])
     extra = in_lanes(columns)
     for place in range(held):
-        for array, value in enumerate((local_slot, local_grad)):
-            quarter = place * 2 + array
-            rows = value[place * owners : (place + 1) * owners]
-            held_rows[quarter, :, :width] = rows
+        span = slice(place * owners, (place + 1) * owners)
+        half = width // 2
+        for side in range(2):
+            quarter = place * 2 + side
+            columns = slice(side * half, (side + 1) * half)
+            held_rows[quarter, :, :half] = local_slot[span, columns]
+            held_rows[quarter, :, half:width] = local_grad[span, columns]
             held_rows[quarter, :, width:] = extra
     x = place_ref[0] % 4
     for turn, out in enumerate((out0, out1, out2, out3)):
@@ -181,12 +184,23 @@
         extra = block[:, width:]
         lses.append(jnp.where(x // 2 == 0, from_lanes(extra, 0), from_lanes(extra, 3)))
     lse = log_sum_exp(lses)
-    row = None
+    half = width // 2
+    slot, grad = 0.0, 0.0
     for block, part in zip(blocks, lses):
-        scale = jnp.where(x % 2 == 0, jnp.exp(part - lse), 1.0)
-        term = block[:, :width] * scale
-        row = term if row is None else row + term
-    write_rows(out_ref, row, in_lanes(pieces(lse)))
+        slot = slot + block[:, :half] * jnp.exp(part - lse)
+        grad = grad + block[:, half:width]
+    high = slot.astype(bf16).astype(f32)
+    cut = out_ref.shape[2] - half
+    both = jnp.stack(
+        [
+            jnp.concatenate([high, grad[:, :cut]], axis=1),
+            jnp.concatenate([slot - high, grad[:, cut:], in_lanes(pieces(lse))], axis=1),
+        ],
+        axis=1,
+    ).astype(bf16)
+    owners = high.shape[0]
+    for member in range(out_ref.shape[0] // owners):
+        out_ref[member * owners : (member + 1) * owners] = both
 
 
 def expert_kernel(
@@ -197,16 +211,23 @@
     held = w_in_ref.shape[0]
     owners = out0.shape[0]
     for place in range(held):
-        rows, lses = [], []
+        rows, grads, lses = [], [], []
+        half = w_in_ref.shape[1] // 2
         for y in range(2):
-            data, extra = read_rows(got_ref, y * 4 + place * 2, owners)
-            rows.append(data)
-            lses.append(from_lanes(extra, 0))
+            slots, slot_grads = [], []
+            for side in range(2):
+                first = (y * 4 + place * 2 + side) * owners
+                upper = got_ref[first : first + owners, 0, :].astype(f32)
+                lower = got_ref[first : first + owners, 1, :].astype(f32)
+                slots.append(upper[:, :half] + lower[:, :half])
+                slot_grads += [upper[:, half:], lower[:, half:-LANES]]
+            rows.append(jnp.concatenate(slots, axis=1))
+            grads.append(jnp.concatenate(slot_grads, axis=1))
+            lses.append(from_lanes(lower[:, -LANES:], 0))
         lse = log_sum_exp(lses)
         slot_full = rows[0] * jnp.exp(lses[0] - lse) + rows[1] * jnp.exp(lses[1] - lse)
         held_slots[place] = slot_full
         slot = slot_full.astype(bf16)
-        grads = [read_rows(got_ref, y * 4 + place * 2 + 1, owners)[0] for y in range(2)]
         slot_grad = (grads[0] + grads[1]).astype(bf16)
         rows_kept[place * 2] = slot
         rows_kept[place * 2 + 1] = slot_grad
@@ -408,7 +429,7 @@
     got = around_x(send)
     send = pl.pallas_call(
         first_sum_kernel,
-        out_shape=shape(sent, f32),
+        out_shape=shape((8 * owners, 2, 8 * LANES), bf16),
         in_specs=[SMEM] + [VMEM] * 4,
         out_specs=VMEM,
         compiler_params=params(8),

time: 92.4 us -> 89.9 us (0.973)
  blocking collectives: 46.3 us -> 43.7 us
    all_to_all x2, blocking collectives: 46.3 us -> 43.7 us  [per_device(): got = lax.all_to_all(send, ALL, 0, 0, tiled=True)]
where the time goes in v7:
time: 89.9 us; the launch traced here: 89.6 us
  blocking collectives  43.7 us (49%)
  starting transfers between devices  17.2 us (19%)
  Pallas kernels  16.4 us (18%)
  waiting for transfers between devices  10.8 us (12%)
    all_to_all x2, blocking collectives, per_device(): got = lax.all_to_all(send, ALL, 0, 0, tiled=True)  43.7 us
    ppermute x6, starting transfers between devices, around_x(): got.append(lax.ppermute(arrays[turn], 'x', pairs))  9.08 us
    pallas_call x1, Pallas kernels, per_device(): pl.pallas_call(late_kernel, out_shape=[shape(dims, bf16) for dims in late...  5.27 us
    ppermute x6, waiting for transfers between devices, around_x(): got.append(lax.ppermute(arrays[turn], 'x', pairs))  5.01 us
    all_to_all x1, starting transfers between devices, per_device(): got = lax.all_to_all(send, CHIPS, 0, 0, tiled=True)  5 us
    all_to_all x1, waiting for transfers between devices, per_device(): got = lax.all_to_all(send, CHIPS, 0, 0, tiled=True)  3.98 us
    pallas_call x1, Pallas kernels, per_device(): pl.pallas_call(first_kernel, out_shape=[shape((owners, wide), f32)] * 4 +...  3.75 us
    pallas_call x1, Pallas kernels, per_device(): pl.pallas_call(expert_kernel, out_shape=[shape((owners, width), bf16)] *...  2.99 us
  transfers between devices with their start and end apart: 9, of which 8 were waited for; matrix products, arithmetic and copies ran while one was open for 0% of the time, Pallas kernels for 6%

profile of v7, /device:TPU:1, one launch (start us, length us, event | category | flops | bytes accessed | tf_op | source)
XLA Modules:
  0.0 89.6 jit_solution(6609517826209089471)
XLA Ops:
  0.6 0.0 copy-start.2
  0.7 0.9 copy-done.2
  1.5 0.0 copy-start
  1.5 0.0 copy-start.1
  1.5 3.7 %first.1 = (f32[16,1408]{1,0:T(8,128)S(1)}, f32[16,1408]{1,0:T(8,128)S(1)}, f32[16,1408]{1,0:T(8,128)S(1)}, f32[16,1408]{1,0:T(8,128)S(1)}, f32[32,1024]{1,0:T(8...) custom-call(s32[1]{0:T(128)} %bitcast.place_ref, bf16[1024,1280]{1,0:T(8,128)(2,1)} %bitcast.9, ...), custom_call_target="tpu_custom_call" | custom-call | flops 251658240 | bytes 5242880 | tf_op jit(solution)/shard_map/first/pallas_call | solution.py:414
  5.3 2.1 %collective-permute-start = (f32[16,1408]{1,0:T(8,128)S(1)}, f32[16,1408]{1,0:T(8,128)S(1)}, u32[]{:S(2)}, u32[]{:S(2)}) collective-permute-start(f32[16,1408]{1,0:T(8,128)S(1)} %get-tuple-element.39), channel_id=1, source_target_pairs={{0,16},{16,32},{32,48},{48,0},{1,17},{17,33},{33,49},{49,1},{2,18}... | collective-permute-start | bytes 270344 | tf_op jit(solution)/shard_map/ppermute | solution.py:392
  7.4 2.5 %collective-permute-start.1 = (f32[16,1408]{1,0:T(8,128)S(1)}, f32[16,1408]{1,0:T(8,128)S(1)}, u32[]{:S(2)}, u32[]{:S(2)}) collective-permute-start(f32[16,1408]{1,0:T(8,128)S(1)} %get-tuple-element.40), channel_id=1, source_target_pairs={{0,32},{16,48},{32,0},{48,16},{1,33},{17,49},{33,1},{49,17},{2,34}... | collective-permute-start | bytes 270344 | tf_op jit(solution)/shard_map/ppermute | solution.py:392
  9.9 1.2 %collective-permute-start.2 = (f32[16,1408]{1,0:T(8,128)S(1)}, f32[16,1408]{1,0:T(8,128)S(1)}, u32[]{:S(2)}, u32[]{:S(2)}) collective-permute-start(f32[16,1408]{1,0:T(8,128)S(1)} %get-tuple-element.41), channel_id=1, source_target_pairs={{0,48},{16,0},{32,16},{48,32},{1,49},{17,1},{33,17},{49,33},{2,50}... | collective-permute-start | bytes 270344 | tf_op jit(solution)/shard_map/ppermute | solution.py:392
  11.0 0.0 collective-permute-done.in1
  11.0 2.5 %collective-permute-done.1.in2 = f32[16,1408]{1,0:T(8,128)S(1)} collective-permute-done((f32[16,1408]{1,0:T(8,128)S(1)}, f32[16,1408]{1,0:T(8,128)S(1)}, u32[]{:S(2)}, u32[]{:S(2)}) %collective-permute-start.1) | collective-permute-done | bytes 90144 | tf_op jit(solution)/shard_map/ppermute | solution.py:392
  13.5 0.4 collective-permute-done.2.in3
  13.9 0.3 first_sum.1
  14.2 24.7 %all_to_all.15.got_ref = bf16[128,2,1024]{2,1,0:T(2,128)(2,1)S(1)} all-to-all(bf16[128,2,1024]{2,1,0:T(2,128)(2,1)S(1)} %first_sum.1), channel_id=1, replica_groups=mesh['yh'=2,'x'=4,'z'=4,'yl'=2,'core'=2] {'yh','x','z','yl','core'}, dimensions={0} | all-to-all | bytes 1048576 | tf_op jit(solution)/shard_map/all_to_all | solution.py:438
  38.9 0.0 copy-done
  38.9 0.0 copy-done.1
  38.9 3.0 %experts.1 = (bf16[16,1280]{1,0:T(8,128)(2,1)S(1)}, bf16[16,1280]{1,0:T(8,128)(2,1)S(1)}, bf16[16,1280]{1,0:T(8,128)(2,1)S(1)}, bf16[16,1280]{1,0:T(8,128)(2,1)S...) custom-call(s32[1]{0:T(128)} %bitcast.place_ref, ...), custom_call_target="tpu_custom_call" | custom-call | flops 209715200 | bytes 6553600 | tf_op jit(solution)/shard_map/experts/pallas_call | solution.py:439
  41.9 0.1 collective-permute-start.3
  42.0 1.7 %collective-permute-start.4 = (bf16[16,1280]{1,0:T(8,128)(2,1)S(1)}, bf16[16,1280]{1,0:T(8,128)(2,1)S(1)}, u32[]{:S(2)}, u32[]{:S(2)}) collective-permute-start(bf16[16,1280]{1,0:T(8,128)(2,1)S(1)} %get-tuple-element.44), channel_id=1, source_target_pairs={{0,32},{16,48},{32,0},{48,16},{1,33},{17,49},{33,1},{49,17},{2,34}... | collective-permute-start | bytes 122888 | tf_op jit(solution)/shard_map/ppermute | solution.py:392
  43.7 1.6 %collective-permute-start.5 = (bf16[16,1280]{1,0:T(8,128)(2,1)S(1)}, bf16[16,1280]{1,0:T(8,128)(2,1)S(1)}, u32[]{:S(2)}, u32[]{:S(2)}) collective-permute-start(bf16[16,1280]{1,0:T(8,128)(2,1)S(1)} %get-tuple-element.45), channel_id=1, source_target_pairs={{0,48},{16,0},{32,16},{48,32},{1,49},{17,1},{33,17},{49,33},{2,50}... | collective-permute-start | bytes 122888 | tf_op jit(solution)/shard_map/ppermute | solution.py:392
  45.3 0.8 collective-permute-done.3.in1
  46.0 0.4 collective-permute-done.4.in2
  46.5 0.9 collective-permute-done.5.in3
  47.3 0.2 second_sum.1
  47.6 19.0 %all_to_all.16.got_ref = bf16[128,2,768]{2,1,0:T(2,128)(2,1)S(1)} all-to-all(bf16[128,2,768]{2,1,0:T(2,128)(2,1)S(1)} %second_sum.1), channel_id=1, replica_groups=mesh['yh'=2,'x'=4,'z'=4,'yl'=2,'core'=2] {'yh','x','z','yl','core'}, dimensions={0} | all-to-all | bytes 786432 | tf_op jit(solution)/shard_map/all_to_all | solution.py:464
  66.6 0.0 copy-start.3
  66.6 2.3 %tokens.1 = (bf16[3,32,1024]{2,1,0:T(8,128)(2,1)S(1)}, bf16[2,32,1280]{2,1,0:T(8,128)(2,1)S(1)}, f32[16,1280]{1,0:T(8,128)S(1)}, f32[16,1280]{1,0:T(8,128)S(1)}) custom-call(s32[1]{0:T(128)} %bitcast.place_ref, bf16[128,2,768]{2,1,0:T(2,128)(2,1)S(1)} %all_to_all.16.got_ref, f32[32,1024]{1,0:T(8,128)S(1)} %get-tuple-element.48.logits_ref, ...), custom_call_target="tpu_custom_call" | custom-call | flops 251658240 | bytes 5242880 | tf_op jit(solution)/shard_map/tokens/pallas_call | solution.py:465
  68.9 0.7 collective-permute-start.6
  69.6 0.9 %collective-permute-done.6.got_ref = f32[16,1280]{1,0:T(8,128)S(1)} collective-permute-done((f32[16,1280]{1,0:T(8,128)S(1)}, f32[16,1280]{1,0:T(8,128)S(1)}, u32[]{:S(2)}, u32[]{:S(2)}) %collective-permute-start.6) | collective-permute-done | bytes 81952 | tf_op jit(solution)/shard_map/ppermute | solution.py:480
  70.6 0.8 router_split.1
  71.4 5.0 %all-to-all-start.2 = ((bf16[64,4,640]{2,1,0:T(4,128)(2,1)}), bf16[64,4,640]{2,1,0:T(4,128)(2,1)S(1)}, u32[]{:S(2)}, u32[]{:S(2)}) async-start(bf16[64,4,640]{2,1,0:T(4,128)(2,1)} %router_split.1), calls=%async_computation.2 | async-start | bytes 655360 | tf_op jit(solution)/shard_map/all_to_all | solution.py:493
  76.4 0.0 copy-done.3
  76.4 5.3 %late.1 = (bf16[2,1280,640]{2,1,0:T(8,128)(2,1)}, bf16[2,640,1280]{2,1,0:T(8,128)(2,1)}, bf16[1024,1280]{1,0:T(8,128)(2,1)}, bf16[1024,1280]{1,0:T(8,128)(2,1)}) custom-call(bf16[4,16,1280]{2,1,0:T(8,128)(2,1)S(1)} %get-tuple-element.58.rows_ref, bf16[4,16,640]{2,1,0:T(8,128)(2,1)S(1)} %get-tuple-element.59.units_ref, ...), custom_call_target="tpu_custom_call" | custom-call | flops 10485760000 | bytes 5242880 | tf_op jit(solution)/shard_map/late/pallas_call | solution.py:495
  81.7 4.0 %all-to-all-done.2.got_ref = bf16[64,4,640]{2,1,0:T(4,128)(2,1)S(1)} async-done(((bf16[64,4,640]{2,1,0:T(4,128)(2,1)}), bf16[64,4,640]{2,1,0:T(4,128)(2,1)S(1)}, u32[]{:S(2)}, u32[]{:S(2)}) %all-to-all-start.2) | async-done | bytes 327712 | tf_op jit(solution)/shard_map/all_to_all | solution.py:493
  85.7 0.2 router_sum.1.half_ref
  85.8 2.4 %collective-permute-start.7 = (f32[16,160]{1,0:T(8,128)S(1)}, f32[16,160]{1,0:T(8,128)S(1)}, u32[]{:S(2)}, u32[]{:S(2)}) collective-permute-start(f32[16,160]{1,0:T(8,128)S(1)} %router_sum.1.half_ref), channel_id=1, source_target_pairs={{0,1},{1,0},{2,3},{3,2},{4,5},{5,4},{6,7},{7,6},{8,9},{9,8},{10,11... | collective-permute-start | bytes 30728 | tf_op jit(solution)/shard_map/ppermute | solution.py:520
  88.2 0.8 collective-permute-done.7.other_ref
  89.0 0.6 router_join.1
Async XLA Ops:
  0.6 0.9 copy-start.2
  1.5 37.4 %copy-start = (bf16[2,1280,640]{2,1,0:T(8,128)(2,1)S(1)}, bf16[2,1280,640]{2,1,0:T(8,128)(2,1)}, u32[]{:S(2)}) copy-start(bf16[2,1280,640]{2,1,0:T(8,128)(2,1)} %w_in_ref.1) | copy-start | bytes 9830404
  1.5 37.4 %copy-start.1 = (bf16[2,640,1280]{2,1,0:T(8,128)(2,1)S(1)}, bf16[2,640,1280]{2,1,0:T(8,128)(2,1)}, u32[]{:S(2)}) copy-start(bf16[2,640,1280]{2,1,0:T(8,128)(2,1)} %w_out_ref.1) | copy-start | bytes 9830404
  5.3 5.7 %collective-permute-start = (f32[16,1408]{1,0:T(8,128)S(1)}, f32[16,1408]{1,0:T(8,128)S(1)}, u32[]{:S(2)}, u32[]{:S(2)}) collective-permute-start(f32[16,1408]{1,0:T(8,128)S(1)} %get-tuple-element.39), channel_id=1, source_target_pairs={{0,16},{16,32},{32,48},{48,0},{1,17},{17,33},{33,49},{49,1},{2,18}... | collective-permute-start | bytes 270344 | tf_op jit(solution)/shard_map/ppermute | solution.py:392
  7.4 6.1 %collective-permute-start.1 = (f32[16,1408]{1,0:T(8,128)S(1)}, f32[16,1408]{1,0:T(8,128)S(1)}, u32[]{:S(2)}, u32[]{:S(2)}) collective-permute-start(f32[16,1408]{1,0:T(8,128)S(1)} %get-tuple-element.40), channel_id=1, source_target_pairs={{0,32},{16,48},{32,0},{48,16},{1,33},{17,49},{33,1},{49,17},{2,34}... | collective-permute-start | bytes 270344 | tf_op jit(solution)/shard_map/ppermute | solution.py:392
  9.9 4.1 %collective-permute-start.2 = (f32[16,1408]{1,0:T(8,128)S(1)}, f32[16,1408]{1,0:T(8,128)S(1)}, u32[]{:S(2)}, u32[]{:S(2)}) collective-permute-start(f32[16,1408]{1,0:T(8,128)S(1)} %get-tuple-element.41), channel_id=1, source_target_pairs={{0,48},{16,0},{32,16},{48,32},{1,49},{17,1},{33,17},{49,33},{2,50}... | collective-permute-start | bytes 270344 | tf_op jit(solution)/shard_map/ppermute | solution.py:392
  41.9 4.1 %collective-permute-start.3 = (bf16[16,1280]{1,0:T(8,128)(2,1)S(1)}, bf16[16,1280]{1,0:T(8,128)(2,1)S(1)}, u32[]{:S(2)}, u32[]{:S(2)}) collective-permute-start(bf16[16,1280]{1,0:T(8,128)(2,1)S(1)} %get-tuple-element.43), channel_id=1, source_target_pairs={{0,16},{16,32},{32,48},{48,0},{1,17},{17,33},{33,49},{49,1},{2,18}... | collective-permute-start | bytes 122888 | tf_op jit(solution)/shard_map/ppermute | solution.py:392
  42.0 4.5 %collective-permute-start.4 = (bf16[16,1280]{1,0:T(8,128)(2,1)S(1)}, bf16[16,1280]{1,0:T(8,128)(2,1)S(1)}, u32[]{:S(2)}, u32[]{:S(2)}) collective-permute-start(bf16[16,1280]{1,0:T(8,128)(2,1)S(1)} %get-tuple-element.44), channel_id=1, source_target_pairs={{0,32},{16,48},{32,0},{48,16},{1,33},{17,49},{33,1},{49,17},{2,34}... | collective-permute-start | bytes 122888 | tf_op jit(solution)/shard_map/ppermute | solution.py:392
  43.7 3.7 %collective-permute-start.5 = (bf16[16,1280]{1,0:T(8,128)(2,1)S(1)}, bf16[16,1280]{1,0:T(8,128)(2,1)S(1)}, u32[]{:S(2)}, u32[]{:S(2)}) collective-permute-start(bf16[16,1280]{1,0:T(8,128)(2,1)S(1)} %get-tuple-element.45), channel_id=1, source_target_pairs={{0,48},{16,0},{32,16},{48,32},{1,49},{17,1},{33,17},{49,33},{2,50}... | collective-permute-start | bytes 122888 | tf_op jit(solution)/shard_map/ppermute | solution.py:392
  66.6 9.8 %copy-start.3 = (bf16[1280,32]{0,1:T(8,128)(2,1)S(1)}, bf16[1280,32]{0,1:T(8,128)(2,1)}, u32[]{:S(2)}) copy-start(bf16[1280,32]{0,1:T(8,128)(2,1)} %param.6) | copy-start | bytes 245764
  68.9 1.7 %collective-permute-start.6 = (f32[16,1280]{1,0:T(8,128)S(1)}, f32[16,1280]{1,0:T(8,128)S(1)}, u32[]{:S(2)}, u32[]{:S(2)}) collective-permute-start(f32[16,1280]{1,0:T(8,128)S(1)} %get-tuple-element.52), channel_id=1, source_target_pairs={{0,1},{1,0},{2,3},{3,2},{4,5},{5,4},{6,7},{7,6},{8,9},{9,8},{10,11... | collective-permute-start | bytes 245768 | tf_op jit(solution)/shard_map/ppermute | solution.py:480
  71.4 14.3 %all-to-all-start.2 = ((bf16[64,4,640]{2,1,0:T(4,128)(2,1)}), bf16[64,4,640]{2,1,0:T(4,128)(2,1)S(1)}, u32[]{:S(2)}, u32[]{:S(2)}) async-start(bf16[64,4,640]{2,1,0:T(4,128)(2,1)} %router_split.1), calls=%async_computation.2 | async-start | bytes 655360 | tf_op jit(solution)/shard_map/all_to_all | solution.py:493
  85.8 3.2 %collective-permute-start.7 = (f32[16,160]{1,0:T(8,128)S(1)}, f32[16,160]{1,0:T(8,128)S(1)}, u32[]{:S(2)}, u32[]{:S(2)}) collective-permute-start(f32[16,160]{1,0:T(8,128)S(1)} %router_sum.1.half_ref), channel_id=1, source_target_pairs={{0,1},{1,0},{2,3},{3,2},{4,5},{5,4},{6,7},{7,6},{8,9},{9,8},{10,11... | collective-permute-start | bytes 30728 | tf_op jit(solution)/shard_map/ppermute | solution.py:520
